TPU v7x, 32 devices: a whole 2x2x4 slice. The times are simulated.
32 devices in a mesh: ctx: 8 (over z, y), tp: 4 (over x, core).
Axes of the slice: x: 2, y: 2, z: 4, core: 2. Of those that a mesh axis runs over, the one named last changes fastest.
Arguments:
- hidden_in: bfloat16 [4096, 1536], P('ctx'), may hold values from -6 to 6
- norm_one: bfloat16 [1536], P('ctx'), may hold values from 0.5 to 1.5
- w_query: bfloat16 [1536, 1536], P('ctx', 'tp'), may hold values from -0.15625 to 0.15625
- w_key: bfloat16 [1536, 1536], P('ctx', 'tp'), may hold values from -0.15625 to 0.15625
- w_value: bfloat16 [1536, 1536], P('ctx', 'tp'), may hold values from -0.15625 to 0.15625
- w_gate_out: bfloat16 [1536, 1536], P('ctx', 'tp'), may hold values from -0.15625 to 0.15625
- w_forget: bfloat16 [1536, 24], P('ctx', 'tp'), may hold values from -0.15625 to 0.15625
- forget_bias: float32 [24], P('tp'), may hold values from 3.5 to 11.5
- head_gains: bfloat16 [128, 24], P('ctx', 'tp'), may hold values from 0.5 to 1.5
- w_output: bfloat16 [1536, 1536], P('ctx', 'tp'), may hold values from -0.625 to 0.625
- norm_two: bfloat16 [1536], P('ctx'), may hold values from 0.5 to 1.5
- w_gate: bfloat16 [1536, 4096], P('ctx', 'tp'), may hold values from -0.15625 to 0.15625
- w_up: bfloat16 [1536, 4096], P('ctx', 'tp'), may hold values from -0.15625 to 0.15625
- w_down: bfloat16 [1536, 4096], P('ctx', 'tp'), may hold values from -0.1875 to 0.1875
- out_grad: bfloat16 [4096, 1536], P('ctx'), may hold values from -6 to 6
- doc_lengths: int32 [2], replicated, may hold values from 1024 to 2304, as said below
- group_map: int32 [16], replicated, may hold values from 0 to 15, as said below
- skip_list: int32 [16, 16], replicated, may hold values 0 or 1
Outputs:
- layer_out: float32 [4096, 1536], P('ctx', 'tp')
- input_grad: float32 [4096, 1536], P('ctx')
- norm_one_grad: float32 [1536], P('ctx')
- w_query_grad: float32 [1536, 1536], P('ctx', 'tp')
- w_key_grad: float32 [1536, 1536], P('ctx', 'tp')
- w_value_grad: float32 [1536, 1536], P('ctx', 'tp')
- w_gate_out_grad: float32 [1536, 1536], P('ctx', 'tp')
- w_forget_grad: float32 [1536, 24], P('ctx', 'tp')
- forget_bias_grad: float32 [24], P('tp')
- head_gains_grad: float32 [128, 24], P('ctx', 'tp')
- w_output_grad: float32 [1536, 1536], P('ctx', 'tp')
- norm_two_grad: float32 [1536], P('ctx')
- w_gate_grad: float32 [1536, 4096], P('ctx', 'tp')
- w_up_grad: float32 [1536, 4096], P('ctx', 'tp')
- w_down_grad: float32 [1536, 4096], P('ctx', 'tp')
Inputs may be any that keep to these rules, and one draw needn't show every extreme that they name: `doc_lengths`: documents lie end to end in this order and fill the pack of 4096 tokens; one of them is 2304 tokens long and stands first or last, each other one has 1024 tokens or more. `group_map`: each group stands in one slot; slots 2i and 2i + 1 hold one group of the first half of the pack and one of the second half. `skip_list`: only entries below the diagonal are read.
All inputs are finite; a program needn't handle non-finite values.
Results may differ from a plain program's by a relative error of at most 0.02.
Values may be sent and summed in bfloat16 or wider, within the bound.
A program may use at most 192 MiB of HBM per device.

v0:
```python
import jax
import jax.numpy as jnp
from jax import lax
from jax.sharding import PartitionSpec as P

EPS = 1e-06
HIGHEST = lax.Precision.HIGHEST


def rms_scale(value):
    return value * lax.rsqrt(jnp.mean(value * value, axis=-1, keepdims=True) + EPS)


def rms_back(grad_in, value):
    inverse = lax.rsqrt(jnp.mean(value * value, axis=-1, keepdims=True) + EPS)
    normal = value * inverse
    return inverse * (grad_in - normal * jnp.mean(grad_in * normal, axis=-1, keepdims=True))


def contract_rows(left, right):
    return lax.dot_general(
        left, right, (((0,), (0,)), ((), ())), preferred_element_type=jnp.float32
    )


def contract_cols(left, right):
    return lax.dot_general(
        left, right, (((1,), (1,)), ((), ())), preferred_element_type=jnp.float32
    )


def locate(row_ids, group_map, doc_ends, group_rows):
    slot_ids = jnp.arange(group_map.shape[0], dtype=jnp.int32)
    slot_hits = (row_ids // group_rows)[:, None] == slot_ids[None, :]
    group_of = jnp.sum(jnp.where(slot_hits, group_map[None, :], 0), axis=1)
    position = group_of * group_rows + row_ids % group_rows
    doc_of = jnp.sum((position[:, None] >= doc_ends[None, :]).astype(jnp.int32), axis=1)
    return (position, doc_of, group_of)


def pair_mask(query_info, key_info, skip_list, group_rows):
    query_pos, query_doc, query_group = query_info
    key_pos, key_doc, key_group = key_info
    query_count = query_pos.shape[0] // group_rows
    key_count = key_pos.shape[0] // group_rows
    query_heads = query_group.reshape(query_count, group_rows)[:, 0]
    key_heads = key_group.reshape(key_count, group_rows)[:, 0]
    table = skip_list[query_heads][:, key_heads]
    small_skip = (table == 1) & (key_heads[None, :] < query_heads[:, None])
    skipped = jnp.broadcast_to(
        small_skip[:, None, :, None], (query_count, group_rows, key_count, group_rows)
    ).reshape(query_pos.shape[0], key_pos.shape[0])
    same_doc = query_doc[:, None] == key_doc[None, :]
    causal = key_pos[None, :] <= query_pos[:, None]
    return same_doc & causal & jnp.logical_not(skipped)


def group_prefix(per_row, group_map, group_rows, reverse):
    slot_total = group_map.shape[0]
    blocks = per_row.reshape(slot_total, group_rows, per_row.shape[1])
    if reverse:
        inside = jnp.flip(jnp.cumsum(jnp.flip(blocks, 1), axis=1), 1)
        totals = inside[:, 0]
        earlier = group_map[None, :] > group_map[:, None]
    else:
        inside = jnp.cumsum(blocks, axis=1)
        totals = inside[:, -1]
        earlier = group_map[None, :] < group_map[:, None]
    before = jnp.dot(earlier.astype(jnp.float32), totals, precision=HIGHEST)
    return (before[:, None, :] + inside).reshape(per_row.shape)


def score_block(queries, query_offsets, key_block, key_offsets, allowed):
    scores = jnp.einsum("qhe,khe->qhk", queries, key_block, preferred_element_type=jnp.float32)
    scores = scores + query_offsets[:, :, None] - key_offsets.T[None, :, :]
    return jnp.where(allowed[:, None, :], scores, -1e30)


def pair_grads(query_part, key_part, allowed):
    queries, query_offsets, log_total, row_delta, grad_attn = query_part
    key_block, value_block, key_offsets = key_part
    scores = score_block(queries, query_offsets, key_block, key_offsets, allowed)
    recomputed = jnp.where(allowed[:, None, :], jnp.exp(scores - log_total[:, :, None]), 0.0)
    grad_probs = jnp.einsum(
        "qhe,khe->qhk", grad_attn, value_block, preferred_element_type=jnp.float32
    )
    grad_wide = recomputed * (grad_probs - row_delta[:, :, None])
    return (recomputed, grad_wide.astype(jnp.bfloat16), grad_wide)


def keep_state(state):
    return state


def over_blocks(running, pieces, step, group_rows):
    block_limit = group_rows * max(1, 1024 // group_rows)
    piece_rows = pieces[0].shape[0]

    def one_block(block_index, inner_state):
        offset_row = block_index * block_limit
        sliced = tuple(
            (lax.dynamic_slice_in_dim(member, offset_row, block_limit, 0) for member in pieces)
        )
        return step(inner_state, sliced, offset_row)

    return lax.fori_loop(0, piece_rows // block_limit, one_block, running)


def on_device(
    hidden_in,
    norm_one,
    w_query,
    w_key,
    w_value,
    w_gate_out,
    w_forget,
    forget_bias,
    head_gains,
    w_output,
    norm_two,
    w_gate,
    w_up,
    w_down,
    out_grad,
    doc_lengths,
    group_map,
    skip_list,
):
    device_ctx = lax.axis_index("ctx")
    device_tp = lax.axis_index("tp")
    ctx_count = lax.axis_size("ctx")
    row_count = hidden_in.shape[0]
    group_rows = row_count // 2
    model_width = hidden_in.shape[1]
    heads_local = forget_bias.shape[0]
    (
        gain_one,
        gain_two,
        gains_head,
        query_weight,
        key_weight,
        value_weight,
        gate_out_weight,
        forget_weight,
        output_weight,
        gate_weight,
        up_weight,
        down_weight,
    ) = (
        lax.all_gather(norm_one, "ctx", axis=0, tiled=True),
        lax.all_gather(norm_two, "ctx", axis=0, tiled=True),
        lax.all_gather(head_gains, "ctx", axis=0, tiled=True),
        lax.all_gather(w_query, "ctx", axis=0, tiled=True),
        lax.all_gather(w_key, "ctx", axis=0, tiled=True),
        lax.all_gather(w_value, "ctx", axis=0, tiled=True),
        lax.all_gather(w_gate_out, "ctx", axis=0, tiled=True),
        lax.all_gather(w_forget, "ctx", axis=0, tiled=True),
        lax.all_gather(w_output, "ctx", axis=0, tiled=True),
        lax.all_gather(w_gate, "ctx", axis=0, tiled=True),
        lax.all_gather(w_up, "ctx", axis=0, tiled=True),
        lax.all_gather(w_down, "ctx", axis=0, tiled=True),
    )
    head_dim = gains_head.shape[0] // 2
    head_width = heads_local * head_dim
    query_gain = gains_head[:head_dim].T.astype(jnp.float32)
    key_gain = gains_head[head_dim:].T.astype(jnp.float32)
    doc_ends = jnp.cumsum(doc_lengths)
    query_info = locate(
        device_ctx * row_count + jnp.arange(row_count, dtype=jnp.int32),
        group_map,
        doc_ends,
        group_rows,
    )
    inputs = hidden_in.astype(jnp.float32)
    normal_one = rms_scale(inputs)
    normed_one = (normal_one * gain_one.astype(jnp.float32)).astype(jnp.bfloat16)
    query_raw = jnp.dot(normed_one, query_weight, preferred_element_type=jnp.float32).reshape(
        row_count, heads_local, head_dim
    )
    key_raw = jnp.dot(normed_one, key_weight, preferred_element_type=jnp.float32).reshape(
        row_count, heads_local, head_dim
    )
    value_flat = jnp.dot(normed_one, value_weight, preferred_element_type=jnp.float32).astype(
        jnp.bfloat16
    )
    gate_logit = jnp.dot(normed_one, gate_out_weight, preferred_element_type=jnp.float32)
    forget_logit = (
        jnp.dot(normed_one, forget_weight, preferred_element_type=jnp.float32) + forget_bias
    )
    query_norm = rms_scale(query_raw)
    key_norm = rms_scale(key_raw)
    query_rows = (query_norm * query_gain * 0.125).astype(jnp.bfloat16)
    key_flat = (key_norm * key_gain).astype(jnp.bfloat16).reshape(row_count, head_width)
    log_forget = jax.nn.log_sigmoid(forget_logit)
    logs_all = lax.all_gather(log_forget, "ctx", axis=0, tiled=True)
    offsets_all = group_prefix(logs_all, group_map, group_rows, False)
    offsets_mine = lax.dynamic_slice_in_dim(offsets_all, device_ctx * row_count, row_count, 0)

    def absorb_step(running, pieces, first_row):
        key_piece, value_piece = pieces
        block_rows = key_piece.shape[0]
        key_info = locate(
            first_row + jnp.arange(block_rows, dtype=jnp.int32), group_map, doc_ends, group_rows
        )
        allowed = pair_mask(query_info, key_info, skip_list, group_rows)
        key_offsets = lax.dynamic_slice_in_dim(offsets_all, first_row, block_rows, 0)

        def absorb_compute(state):
            peak_old, total_old, accum_old = state
            scores = score_block(
                query_rows,
                offsets_mine,
                key_piece.reshape(block_rows, heads_local, head_dim),
                key_offsets,
                allowed,
            )
            peak_new = jnp.maximum(peak_old, jnp.max(scores, axis=-1))
            weights = jnp.where(allowed[:, None, :], jnp.exp(scores - peak_new[:, :, None]), 0.0)
            rescale = jnp.exp(peak_old - peak_new)
            total_new = total_old * rescale + jnp.sum(weights, axis=-1)
            accum_new = accum_old * rescale[:, :, None] + jnp.einsum(
                "qhk,khe->qhe",
                weights,
                value_piece.reshape(block_rows, heads_local, head_dim).astype(jnp.float32),
                precision=HIGHEST,
                preferred_element_type=jnp.float32,
            )
            return (peak_new, total_new, accum_new)

        return lax.cond(jnp.any(allowed), absorb_compute, keep_state, running)

    start_state = (
        jnp.full((row_count, heads_local), -1e30, jnp.float32),
        jnp.zeros((row_count, heads_local), jnp.float32),
        jnp.zeros((row_count, heads_local, head_dim), jnp.float32),
    )
    row_peak, row_total, accum = over_blocks(
        start_state,
        (
            lax.all_gather(key_flat, "ctx", axis=0, tiled=True),
            lax.all_gather(value_flat, "ctx", axis=0, tiled=True),
        ),
        absorb_step,
        group_rows,
    )
    attended = accum / row_total[:, :, None]
    log_total = row_peak + jnp.log(row_total)
    attended_flat = attended.reshape(row_count, head_width)
    gate_open = jax.nn.sigmoid(gate_logit)
    gated = (attended_flat * gate_open).astype(jnp.bfloat16)
    branch = lax.psum(contract_cols(gated, output_weight), "tp")
    middle = inputs + branch
    normal_two = rms_scale(middle)
    normed_two = (normal_two * gain_two.astype(jnp.float32)).astype(jnp.bfloat16)
    gate_value = jnp.dot(normed_two, gate_weight, preferred_element_type=jnp.float32)
    up_value = jnp.dot(normed_two, up_weight, preferred_element_type=jnp.float32)
    sig_gate = jax.nn.sigmoid(gate_value)
    silu_gate = gate_value * sig_gate
    hidden = (silu_gate * up_value).astype(jnp.bfloat16)
    ffn_out = lax.psum_scatter(
        contract_cols(hidden, down_weight).astype(jnp.bfloat16),
        "tp",
        scatter_dimension=1,
        tiled=True,
    ).astype(jnp.float32)
    width_tp = model_width // lax.axis_size("tp")
    layer_out = lax.dynamic_slice_in_dim(middle, device_tp * width_tp, width_tp, 1) + ffn_out
    grad_out = out_grad.astype(jnp.float32)
    grad_hidden = jnp.dot(out_grad, down_weight, preferred_element_type=jnp.float32)
    down_grad = contract_rows(out_grad, hidden)
    grad_gate = (grad_hidden * up_value * sig_gate * (1.0 + gate_value * (1.0 - sig_gate))).astype(
        jnp.bfloat16
    )
    grad_up = (grad_hidden * silu_gate).astype(jnp.bfloat16)
    gate_grad = contract_rows(normed_two, grad_gate)
    up_grad = contract_rows(normed_two, grad_up)
    normed_two_grad = lax.psum(
        contract_cols(grad_gate, gate_weight) + contract_cols(grad_up, up_weight), "tp"
    )
    gain_two_grad = jnp.sum(normed_two_grad * normal_two, axis=0)
    grad_middle = grad_out + rms_back(normed_two_grad * gain_two.astype(jnp.float32), middle)
    grad_branch = grad_middle.astype(jnp.bfloat16)
    output_grad = contract_rows(grad_branch, gated)
    grad_gated = jnp.dot(grad_branch, output_weight, preferred_element_type=jnp.float32)
    grad_attended = (grad_gated * gate_open).astype(jnp.bfloat16)
    grad_gate_logit = (grad_gated * attended_flat * gate_open * (1.0 - gate_open)).astype(
        jnp.bfloat16
    )
    grad_attn = grad_attended.reshape(row_count, heads_local, head_dim)
    row_delta = jnp.sum(grad_attn.astype(jnp.float32) * attended, axis=-1)
    query_part = (query_rows, offsets_mine, log_total, row_delta, grad_attn)
    total_rows = row_count * ctx_count

    def revisit_step(running, pieces, first_row):
        key_piece, value_piece = pieces
        block_rows = key_piece.shape[0]
        key_info = locate(
            first_row + jnp.arange(block_rows, dtype=jnp.int32), group_map, doc_ends, group_rows
        )
        allowed = pair_mask(query_info, key_info, skip_list, group_rows)
        key_offsets = lax.dynamic_slice_in_dim(offsets_all, first_row, block_rows, 0)
        key_block = key_piece.reshape(block_rows, heads_local, head_dim)
        value_block = value_piece.reshape(block_rows, heads_local, head_dim)

        def revisit_compute(state):
            query_acc, query_off_acc, key_all, value_all, key_off_all = state
            prob_rows, grad_scores, scores_wide = pair_grads(
                query_part, (key_block, value_block, key_offsets), allowed
            )
            query_acc = query_acc + jnp.einsum(
                "qhk,khe->qhe", grad_scores, key_block, preferred_element_type=jnp.float32
            )
            query_off_acc = query_off_acc + jnp.sum(scores_wide, axis=2)
            key_term = jnp.einsum(
                "qhk,qhe->khe", grad_scores, query_rows, preferred_element_type=jnp.float32
            ).reshape(block_rows, head_width)
            value_term = jnp.einsum(
                "qhk,qhe->khe",
                prob_rows,
                grad_attn.astype(jnp.float32),
                precision=HIGHEST,
                preferred_element_type=jnp.float32,
            ).reshape(block_rows, head_width)
            key_off_term = -jnp.sum(scores_wide, axis=0).T
            key_all = lax.dynamic_update_slice_in_dim(key_all, key_term, first_row, 0)
            value_all = lax.dynamic_update_slice_in_dim(value_all, value_term, first_row, 0)
            key_off_all = lax.dynamic_update_slice_in_dim(key_off_all, key_off_term, first_row, 0)
            return (query_acc, query_off_acc, key_all, value_all, key_off_all)

        return lax.cond(jnp.any(allowed), revisit_compute, keep_state, running)

    begin_state = (
        jnp.zeros((row_count, heads_local, head_dim), jnp.float32),
        jnp.zeros((row_count, heads_local), jnp.float32),
        jnp.zeros((total_rows, head_width), jnp.float32),
        jnp.zeros((total_rows, head_width), jnp.float32),
        jnp.zeros((total_rows, heads_local), jnp.float32),
    )
    grad_query, grad_off_query, key_all, value_all, key_off_all = over_blocks(
        begin_state,
        (
            lax.all_gather(key_flat, "ctx", axis=0, tiled=True),
            lax.all_gather(value_flat, "ctx", axis=0, tiled=True),
        ),
        revisit_step,
        group_rows,
    )
    grad_key, grad_value, grad_off_key = (
        lax.psum_scatter(key_all, "ctx", scatter_dimension=0, tiled=True),
        lax.psum_scatter(value_all, "ctx", scatter_dimension=0, tiled=True),
        lax.psum_scatter(key_off_all, "ctx", scatter_dimension=0, tiled=True),
    )
    grad_key3 = grad_key.reshape(row_count, heads_local, head_dim)
    key_raw_grad = (
        rms_back(grad_key3 * key_gain, key_raw).astype(jnp.bfloat16).reshape(row_count, head_width)
    )
    query_raw_grad = (
        rms_back(grad_query * query_gain * 0.125, query_raw)
        .astype(jnp.bfloat16)
        .reshape(row_count, head_width)
    )
    value_low = grad_value.astype(jnp.bfloat16)
    query_gain_grad = jnp.sum(grad_query * query_norm * 0.125, axis=0).T
    key_gain_grad = jnp.sum(grad_key3 * key_norm, axis=0).T
    head_gain_grad = jnp.concatenate([query_gain_grad, key_gain_grad], axis=0)
    grad_offsets = grad_off_query + grad_off_key
    offsets_grads_all = lax.all_gather(grad_offsets, "ctx", axis=0, tiled=True)
    suffix_all = group_prefix(offsets_grads_all, group_map, group_rows, True)
    grad_log_forget = lax.dynamic_slice_in_dim(suffix_all, device_ctx * row_count, row_count, 0)
    grad_forget_logit = (grad_log_forget * jax.nn.sigmoid(-forget_logit)).astype(jnp.bfloat16)
    bias_part = jnp.sum(grad_forget_logit.astype(jnp.float32), axis=0)
    normed_one_part = (
        contract_cols(query_raw_grad, query_weight)
        + contract_cols(key_raw_grad, key_weight)
        + contract_cols(value_low, value_weight)
        + contract_cols(grad_gate_logit, gate_out_weight)
        + contract_cols(grad_forget_logit, forget_weight)
    )
    normed_one_grad = lax.psum(normed_one_part.astype(jnp.bfloat16), "tp").astype(jnp.float32)
    gain_one_grad = jnp.sum(normed_one_grad * normal_one, axis=0)
    input_grad = grad_middle + rms_back(normed_one_grad * gain_one.astype(jnp.float32), inputs)
    query_grad = contract_rows(normed_one, query_raw_grad)
    key_weight_grad = contract_rows(normed_one, key_raw_grad)
    value_weight_grad = contract_rows(normed_one, value_low)
    gate_out_grad = contract_rows(normed_one, grad_gate_logit)
    forget_grad = contract_rows(normed_one, grad_forget_logit)
    bias_rows = jnp.broadcast_to(bias_part[None, :], (ctx_count, heads_local))
    (
        gain_one_share,
        query_share,
        key_share,
        value_share,
        gate_out_share,
        forget_share,
        head_gain_share,
        output_share,
        gain_two_share,
        gate_share,
        up_share,
        down_share,
        bias_share,
    ) = (
        lax.psum_scatter(
            gain_one_grad.astype(jnp.bfloat16), "ctx", scatter_dimension=0, tiled=True
        ).astype(jnp.float32),
        lax.psum_scatter(
            query_grad.astype(jnp.bfloat16), "ctx", scatter_dimension=0, tiled=True
        ).astype(jnp.float32),
        lax.psum_scatter(
            key_weight_grad.astype(jnp.bfloat16), "ctx", scatter_dimension=0, tiled=True
        ).astype(jnp.float32),
        lax.psum_scatter(
            value_weight_grad.astype(jnp.bfloat16), "ctx", scatter_dimension=0, tiled=True
        ).astype(jnp.float32),
        lax.psum_scatter(
            gate_out_grad.astype(jnp.bfloat16), "ctx", scatter_dimension=0, tiled=True
        ).astype(jnp.float32),
        lax.psum_scatter(
            forget_grad.astype(jnp.bfloat16), "ctx", scatter_dimension=0, tiled=True
        ).astype(jnp.float32),
        lax.psum_scatter(
            head_gain_grad.astype(jnp.bfloat16), "ctx", scatter_dimension=0, tiled=True
        ).astype(jnp.float32),
        lax.psum_scatter(
            output_grad.astype(jnp.bfloat16), "ctx", scatter_dimension=0, tiled=True
        ).astype(jnp.float32),
        lax.psum_scatter(
            gain_two_grad.astype(jnp.bfloat16), "ctx", scatter_dimension=0, tiled=True
        ).astype(jnp.float32),
        lax.psum_scatter(
            gate_grad.astype(jnp.bfloat16), "ctx", scatter_dimension=0, tiled=True
        ).astype(jnp.float32),
        lax.psum_scatter(
            up_grad.astype(jnp.bfloat16), "ctx", scatter_dimension=0, tiled=True
        ).astype(jnp.float32),
        lax.psum_scatter(
            down_grad.astype(jnp.bfloat16), "ctx", scatter_dimension=0, tiled=True
        ).astype(jnp.float32),
        lax.psum_scatter(
            bias_rows.astype(jnp.bfloat16), "ctx", scatter_dimension=0, tiled=True
        ).astype(jnp.float32),
    )
    bias_grad = bias_share.reshape(heads_local)
    return (
        layer_out,
        input_grad,
        gain_one_share,
        query_share,
        key_share,
        value_share,
        gate_out_share,
        forget_share,
        bias_grad,
        head_gain_share,
        output_share,
        gain_two_share,
        gate_share,
        up_share,
        down_share,
    )


def solution(mesh):
    in_specs = (
        P("ctx", None),
        P("ctx"),
        P("ctx", "tp"),
        P("ctx", "tp"),
        P("ctx", "tp"),
        P("ctx", "tp"),
        P("ctx", "tp"),
        P("tp"),
        P("ctx", "tp"),
        P("ctx", "tp"),
        P("ctx"),
        P("ctx", "tp"),
        P("ctx", "tp"),
        P("ctx", "tp"),
        P("ctx", None),
        P(),
        P(),
        P(),
    )
    out_specs = (
        P("ctx", "tp"),
        P("ctx", None),
        P("ctx"),
        P("ctx", "tp"),
        P("ctx", "tp"),
        P("ctx", "tp"),
        P("ctx", "tp"),
        P("ctx", "tp"),
        P("tp"),
        P("ctx", "tp"),
        P("ctx", "tp"),
        P("ctx"),
        P("ctx", "tp"),
        P("ctx", "tp"),
        P("ctx", "tp"),
    )
    return jax.shard_map(
        on_device, mesh=mesh, in_specs=in_specs, out_specs=out_specs, check_vma=False
    )
```

profile of v0, /device:TPU:0, one launch (start us, length us, event | category | flops | bytes accessed | tf_op | source)
XLA Modules:
  0.0 1989.4 jit_solution(16959622387015706038)
XLA Ops:
  205.2 59.5 %all-gather.15.cloned.1.call-done = bf16[4096,384]{0,1:T(8,128)(2,1)} async-done(((bf16[512,384]{0,1:T(8,128)(2,1)}), bf16[4096,384]{0,1:T(8,128)(2,1)}) %all-gather.15.cloned.1.call-update) | async-done | bytes 3145744 | tf_op jit(solution)/shard_map/all_gather | solution.py:240
  265.7 122.6 %while.46 = (s32[]{:T(128)}, f32[512,6]{0,1:T(8,128)S(1)}, f32[512,6]{0,1:T(8,128)S(1)}, f32[512,6,64]{0,2,1:T(8,128)}, s32[512]{0:T(512)}, /*index=5*/s32[16]{0...) while((s32[]{:T(128)}, f32[512,6]{0,1:T(8,128)S(1)}, ...), condition=%wide.wide.region_16.17_spmd, body=%wide.wide.region_8.16_spmd.sunk | while | flops 2870991872 | bytes 53285720 | solution.py:106
  399.4 64.5 %all-reduce.11.cloned.1.call-done = f32[512,1536]{1,0:T(8,128)} async-done(((f32[512,1536]{1,0:T(8,128)}), f32[512,1536]{1,0:T(8,128)}) %all-reduce.11.cloned.1.call-update) | async-done | bytes 3145744 | tf_op jit(solution)/shard_map/psum | solution.py:251
  469.0 57.7 %all-gather.29.cloned.1.call-done = bf16[1536,1024]{1,0:T(8,128)(2,1)} async-done(((bf16[192,1024]{1,0:T(8,128)(2,1)}), bf16[1536,1024]{1,0:T(8,128)(2,1)}) %all-gather.29.cloned.1.call-update) | async-done | bytes 3145744 | tf_op jit(solution)/shard_map/all_gather | solution.py:160
  532.2 55.6 %all-gather.27.cloned.1.call-done = bf16[1536,1024]{1,0:T(8,128)(2,1)} async-done(((bf16[192,1024]{1,0:T(8,128)(2,1)}), bf16[1536,1024]{1,0:T(8,128)(2,1)}) %all-gather.27.cloned.1.call-update) | async-done | bytes 3145744 | tf_op jit(solution)/shard_map/all_gather | solution.py:159
  593.4 55.8 %all-gather.31.cloned.1.call-done = bf16[1536,1024]{1,0:T(8,128)(2,1)} async-done(((bf16[192,1024]{1,0:T(8,128)(2,1)}), bf16[1536,1024]{1,0:T(8,128)(2,1)}) %all-gather.31.cloned.1.call-update) | async-done | bytes 3145744 | tf_op jit(solution)/shard_map/all_gather | solution.py:161
  667.8 62.0 %all-reduce.13.cloned.1.call-done = f32[512,1536]{1,0:T(8,128)} async-done(((f32[512,1536]{1,0:T(8,128)}), f32[512,1536]{1,0:T(8,128)}) %all-reduce.13.cloned.1.call-update) | async-done | bytes 3145744 | tf_op jit(solution)/shard_map/psum | solution.py:277
  746.9 167.6 %while.47 = (s32[]{:T(128)}, f32[512,6,64]{0,2,1:T(8,128)S(1)}, f32[512,6]{0,1:T(8,128)}, f32[4096,384]{0,1:T(8,128)}, f32[4096,384]{0,1:T(8,128)}, /*index=5*/f...) while((s32[]{:T(128)}, f32[512,6,64]{0,2,1:T(8,128)S(1)}, ...), condition=%wide.wide.region_31.32_spmd, body=%wide.wide.region_23.31_spmd.sunk | while | flops 4078748672 | bytes 83842176 | solution.py:106
  753.0 35.9 %conditional.7 = ((f32[512,6,64]{0,2,1:T(8,128)S(1)}, f32[512,6]{0,1:T(8,128)}, f32[4096,384]{0,1:T(8,128)}, f32[4096,384]{0,1:T(8,128)}, f32[4096,6]{0,1:T(8,128)})) conditional(s32[]{:T(128)} %convert_element_type.421, (f32[512,6,64]{0,2,1:T(8,128)S(1)}, f32[512,6]{0,1:T(8,128)}, f32[4096,384]{0,1:T(8,128)}, f32[4096,384]{0,1:T(8,128)}, ...), branch_computations={%region_27.27_spmd, %region_28.30_spmd} | conditional | flops 4076025856 | bytes 83767648 | solution.py:330
  794.7 35.9 %conditional.7 = ((f32[512,6,64]{0,2,1:T(8,128)S(1)}, f32[512,6]{0,1:T(8,128)}, f32[4096,384]{0,1:T(8,128)}, f32[4096,384]{0,1:T(8,128)}, f32[4096,6]{0,1:T(8,128)})) conditional(s32[]{:T(128)} %convert_element_type.421, (f32[512,6,64]{0,2,1:T(8,128)S(1)}, f32[512,6]{0,1:T(8,128)}, f32[4096,384]{0,1:T(8,128)}, f32[4096,384]{0,1:T(8,128)}, ...), branch_computations={%region_27.27_spmd, %region_28.30_spmd} | conditional | flops 4076025856 | bytes 83767648 | solution.py:330
  915.7 59.0 %reduce-scatter.27.cloned.1.call-done = f32[512,6]{0,1:T(8,128)} async-done(((f32[4096,6]{0,1:T(8,128)}), f32[512,6]{0,1:T(8,128)}) %reduce-scatter.27.cloned.1.call-update) | async-done | bytes 12304 | tf_op jit(solution)/shard_map/reduce_scatter | solution.py:351
  1059.2 36.8 %reduce-scatter.23.cloned.1.call-done = f32[512,384]{0,1:T(8,128)} async-done(((f32[4096,384]{0,1:T(8,128)}), f32[512,384]{0,1:T(8,128)}) %reduce-scatter.23.cloned.1.call-update) | async-done | bytes 786448 | tf_op jit(solution)/shard_map/reduce_scatter | solution.py:349
  1104.8 112.2 %reduce-scatter.25.cloned.1.call-done = f32[512,384]{0,1:T(8,128)} async-done(((f32[4096,384]{0,1:T(8,128)}), f32[512,384]{0,1:T(8,128)}) %reduce-scatter.25.cloned.1.call-update) | async-done | bytes 786448 | tf_op jit(solution)/shard_map/reduce_scatter | solution.py:350
  1228.8 52.4 %reduce-scatter.45.cloned.1.call-done = bf16[192,6]{1,0:T(8,128)(2,1)} async-done(((bf16[1536,6]{1,0:T(8,128)(2,1)}), bf16[192,6]{1,0:T(8,128)(2,1)}) %reduce-scatter.45.cloned.1.call-update) | async-done | bytes 2320
  1314.2 64.4 %reduce-scatter.37.cloned.1.call-done = bf16[192,384]{1,0:T(8,128)(2,1)} async-done(((bf16[1536,384]{1,0:T(8,128)(2,1)}), bf16[192,384]{1,0:T(8,128)(2,1)}) %reduce-scatter.37.cloned.1.call-update) | async-done | bytes 147472 | tf_op jit(solution)/shard_map/reduce_scatter | solution.py:424
  1380.2 65.2 %reduce-scatter.35.cloned.1.call-done = bf16[192,384]{1,0:T(8,128)(2,1)} async-done(((bf16[1536,384]{1,0:T(8,128)(2,1)}), bf16[192,384]{1,0:T(8,128)(2,1)}) %reduce-scatter.35.cloned.1.call-update) | async-done | bytes 147472 | tf_op jit(solution)/shard_map/reduce_scatter | solution.py:415
  1447.0 65.0 %reduce-scatter.29.cloned.1.call-done = bf16[192,384]{1,0:T(8,128)(2,1)} async-done(((bf16[1536,384]{1,0:T(8,128)(2,1)}), bf16[192,384]{1,0:T(8,128)(2,1)}) %reduce-scatter.29.cloned.1.call-update) | async-done | bytes 147472 | tf_op jit(solution)/shard_map/reduce_scatter | solution.py:406
  1513.7 75.8 %reduce-scatter.49.cloned.1.call-done = bf16[192,1024]{1,0:T(8,128)(2,1)} async-done(((bf16[1536,1024]{1,0:T(8,128)(2,1)}), bf16[192,1024]{1,0:T(8,128)(2,1)}) %reduce-scatter.49.cloned.1.call-update) | async-done | bytes 393232
  1593.7 73.4 %reduce-scatter.41.cloned.1.call-done = bf16[192,1024]{1,0:T(8,128)(2,1)} async-done(((bf16[1536,1024]{1,0:T(8,128)(2,1)}), bf16[192,1024]{1,0:T(8,128)(2,1)}) %reduce-scatter.41.cloned.1.call-update) | async-done | bytes 393232 | tf_op jit(solution)/shard_map/reduce_scatter | solution.py:433
  1669.1 75.6 %reduce-scatter.39.cloned.1.call-done = bf16[192,1024]{1,0:T(8,128)(2,1)} async-done(((bf16[1536,1024]{1,0:T(8,128)(2,1)}), bf16[192,1024]{1,0:T(8,128)(2,1)}) %reduce-scatter.39.cloned.1.call-update) | async-done | bytes 393232 | tf_op jit(solution)/shard_map/reduce_scatter | solution.py:430
  1746.6 54.5 %reduce-scatter.47.cloned.1.call-done = bf16[16,6]{1,0:T(8,128)(2,1)} async-done(((bf16[128,6]{1,0:T(8,128)(2,1)}), bf16[16,6]{1,0:T(8,128)(2,1)}) %reduce-scatter.47.cloned.1.call-update) | async-done | bytes 208
  1802.5 43.6 %all-reduce.15.cloned.1.call-done = bf16[512,1536]{1,0:T(8,128)(2,1)} async-done(((bf16[512,1536]{1,0:T(8,128)(2,1)}), bf16[512,1536]{1,0:T(8,128)(2,1)}) %all-reduce.15.cloned.1.call-update) | async-done | bytes 1572880 | tf_op jit(solution)/shard_map/psum | solution.py:379
  1849.1 37.2 %all-reduce.5 = (bf16[1536]{0:T(1024)(128)(2,1)S(1)}, bf16[8,6]{1,0:T(8,128)(2,1)S(1)}, bf16[1536]{0:T(1024)(128)(2,1)S(1)}) all-reduce(bf16[1536]{0:T(1024)(128)(2,1)S(1)} %get-tuple-element.2100, bf16[8,6]{1,0:T(8,128)(2,1)S(1)} %broadcast_in_dim.313, bf16[1536]{0:T(1024)(128)(2,1)S(1)} %copy-done.57), channel_id=6, replica_groups=mesh['ctx'=8,'tp'=4] {'ctx'}, use_global_device_ids=true, to_apply=%region_42.43.clone | all-reduce | flops 3120 | bytes 12480
  1915.6 65.1 %reduce-scatter.33.cloned.1.call-done = bf16[192,384]{1,0:T(8,128)(2,1)} async-done(((bf16[1536,384]{1,0:T(8,128)(2,1)}), bf16[192,384]{1,0:T(8,128)(2,1)}) %reduce-scatter.33.cloned.1.call-update) | async-done | bytes 147472 | tf_op jit(solution)/shard_map/reduce_scatter | solution.py:412
  (668 shorter events, 904.8 us)
Async XLA Ops:
  8.7 168.4 %all-gather.17.cloned.1.call-start = ((), (), s32[]{:S(2)}) async-start(), calls=%async_computation.16 | async-start | bytes 1327104 | tf_op jit(solution)/shard_map/all_gather | solution.py:153
  9.4 191.1 %all-gather.21.cloned.1.call-start = ((), (), s32[]{:S(2)}) async-start(), calls=%async_computation.18 | async-start | bytes 3538944 | tf_op jit(solution)/shard_map/all_gather | solution.py:241
  57.7 207.0 %all-gather.15.cloned.1.call-start = ((), (), s32[]{:S(2)}) async-start(), calls=%async_computation.15 | async-start | bytes 3538944 | tf_op jit(solution)/shard_map/all_gather | solution.py:240
  100.8 288.7 %all-gather.23.cloned.1.call-start = ((), (), s32[]{:S(2)}) async-start(), calls=%async_computation.19 | async-start | bytes 1327104 | tf_op jit(solution)/shard_map/all_gather | solution.py:156
  101.4 291.7 %all-gather.25.cloned.1.call-start = ((), (), s32[]{:S(2)}) async-start(), calls=%async_computation.20 | async-start | bytes 1327104 | tf_op jit(solution)/shard_map/all_gather | solution.py:158
  102.2 361.8 %all-reduce.11.cloned.1.call-start = ((), (), s32[]{:S(2)}) async-start(), calls=%async_computation.21 | async-start | bytes 6291456 | tf_op jit(solution)/shard_map/psum | solution.py:251
  398.0 189.9 %all-gather.27.cloned.1.call-start = ((), (), s32[]{:S(2)}) async-start(), calls=%async_computation.22 | async-start | bytes 3538944 | tf_op jit(solution)/shard_map/all_gather | solution.py:159
  398.6 250.6 %all-gather.31.cloned.1.call-start = ((), (), s32[]{:S(2)}) async-start(), calls=%async_computation.24 | async-start | bytes 3538944 | tf_op jit(solution)/shard_map/all_gather | solution.py:161
  399.3 330.5 %all-reduce.13.cloned.1.call-start = ((), (), s32[]{:S(2)}) async-start(), calls=%async_computation.25 | async-start | bytes 6291456 | tf_op jit(solution)/shard_map/psum | solution.py:277
  662.6 312.1 %reduce-scatter.27.cloned.1.call-start = ((), (), s32[]{:S(2)}) async-start(), calls=%async_computation.28 | async-start | bytes 147456 | tf_op jit(solution)/shard_map/reduce_scatter | solution.py:351
  914.5 181.5 %reduce-scatter.23.cloned.1.call-start = ((), (), s32[]{:S(2)}) async-start(), calls=%async_computation.26 | async-start | bytes 7077888 | tf_op jit(solution)/shard_map/reduce_scatter | solution.py:349
  915.1 301.9 %reduce-scatter.25.cloned.1.call-start = ((), (), s32[]{:S(2)}) async-start(), calls=%async_computation.27 | async-start | bytes 7077888 | tf_op jit(solution)/shard_map/reduce_scatter | solution.py:350
  915.7 365.6 %reduce-scatter.45.cloned.1.call-start = ((), (), s32[]{:S(2)}) async-start(), calls=%async_computation.38 | async-start | bytes 442368
  1014.9 296.0 %reduce-scatter.43.cloned.1.call-start = ((), (), s32[]{:S(2)}) async-start(), calls=%async_computation.37 | async-start | bytes 1966080
  1022.8 355.7 %reduce-scatter.37.cloned.1.call-start = ((), (), s32[]{:S(2)}) async-start(), calls=%async_computation.34 | async-start | bytes 1327104 | tf_op jit(solution)/shard_map/reduce_scatter | solution.py:424
  1026.9 418.4 %reduce-scatter.35.cloned.1.call-start = ((), (), s32[]{:S(2)}) async-start(), calls=%async_computation.33 | async-start | bytes 1327104 | tf_op jit(solution)/shard_map/reduce_scatter | solution.py:415
  1029.3 482.7 %reduce-scatter.29.cloned.1.call-start = ((), (), s32[]{:S(2)}) async-start(), calls=%async_computation.30 | async-start | bytes 1327104 | tf_op jit(solution)/shard_map/reduce_scatter | solution.py:406
  1034.2 555.3 %reduce-scatter.49.cloned.1.call-start = ((), (), s32[]{:S(2)}) async-start(), calls=%async_computation.40 | async-start | bytes 3538944
  1044.3 622.9 %reduce-scatter.41.cloned.1.call-start = ((), (), s32[]{:S(2)}) async-start(), calls=%async_computation.36 | async-start | bytes 3538944 | tf_op jit(solution)/shard_map/reduce_scatter | solution.py:433
  1049.6 695.1 %reduce-scatter.39.cloned.1.call-start = ((), (), s32[]{:S(2)}) async-start(), calls=%async_computation.35 | async-start | bytes 3538944 | tf_op jit(solution)/shard_map/reduce_scatter | solution.py:430
  1055.1 746.0 %reduce-scatter.47.cloned.1.call-start = ((), (), s32[]{:S(2)}) async-start(), calls=%async_computation.39 | async-start | bytes 36864
  1099.8 746.4 %all-reduce.15.cloned.1.call-start = ((), (), s32[]{:S(2)}) async-start(), calls=%async_computation.29 | async-start | bytes 3145728 | tf_op jit(solution)/shard_map/psum | solution.py:379
  1223.5 690.4 %reduce-scatter.31.cloned.1.call-start = ((), (), s32[]{:S(2)}) async-start(), calls=%async_computation.31 | async-start | bytes 1327104 | tf_op jit(solution)/shard_map/reduce_scatter | solution.py:409
  1225.9 754.8 %reduce-scatter.33.cloned.1.call-start = ((), (), s32[]{:S(2)}) async-start(), calls=%async_computation.32 | async-start | bytes 1327104 | tf_op jit(solution)/shard_map/reduce_scatter | solution.py:412
  (97 other events, 3500.2 us)
Sparse Core Ops, SparseCore 0:
  10.2 43.8 all-gather.18
  56.3 39.8 all-gather.12
  98.4 40.0 all-gather.16
  141.1 59.3 all-gather.20
  203.0 61.6 all-gather.14
  397.4 66.5 all-reduce.10
  466.1 60.5 all-gather.28
  528.8 59.0 all-gather.26
  590.0 59.0 all-gather.30
  662.7 67.0 all-reduce.12
  914.6 60.0 reduce-scatter.26
  978.2 117.8 reduce-scatter.22
  1099.5 117.4 reduce-scatter.24
  1220.7 60.5 reduce-scatter.44
  1314.5 64.0 reduce-scatter.36
  1382.3 62.9 reduce-scatter.34
  1449.0 62.9 reduce-scatter.28
  1516.0 73.3 reduce-scatter.48
  1593.5 73.6 reduce-scatter.40
  1671.2 73.4 reduce-scatter.38
  1748.6 52.5 reduce-scatter.46
  1804.2 41.8 all-reduce.14
  1849.8 64.1 reduce-scatter.30
  1917.6 63.0 reduce-scatter.32
  (3 shorter events, 106.0 us)
where the time goes:
time: 2000 us; the launch traced here: 1990 us
  waiting for transfers between devices  1300 us (65%)
  matrix products  252 us (13%)
  blocking collectives  180 us (9%)
  other arithmetic  121 us (6%)
  local copies, waits for them, and re-layouts  108 us (5%)
    unnamed x31, waiting for transfers between devices  217 us
    reduce_scatter x1, waiting for transfers between devices, on_device(): lax.psum_scatter(value_all, 'ctx', scatter_dimension=0, tiled=True)  112 us
    reduce_scatter x1, waiting for transfers between devices, on_device(): lax.psum_scatter(gate_grad.astype(jnp.bfloat16), 'ctx', scatter_dimension...  75.6 us
    reduce_scatter x1, waiting for transfers between devices, on_device(): lax.psum_scatter(up_grad.astype(jnp.bfloat16), 'ctx', scatter_dimension=0...  73.4 us
    reduce_scatter x1, waiting for transfers between devices, on_device(): lax.psum_scatter(gate_out_grad.astype(jnp.bfloat16), 'ctx', scatter_dimen...  65.2 us
    reduce_scatter x1, waiting for transfers between devices, on_device(): lax.psum_scatter(value_weight_grad.astype(jnp.bfloat16), 'ctx', scatter_d...  65.1 us
    reduce_scatter x1, waiting for transfers between devices, on_device(): lax.psum_scatter(query_grad.astype(jnp.bfloat16), 'ctx', scatter_dimensio...  65 us
    psum x1, waiting for transfers between devices, on_device(): branch = lax.psum(contract_cols(gated, output_weight), 'tp')  64.5 us
  transfers between devices with their start and end apart: 27, of which 24 were waited for; matrix products, arithmetic and copies ran while one was open for 14% of the time, Pallas kernels for 0%

commit v1 on v0

v1 whole, which is shorter than its diff:
```python
import functools

import jax
import jax.numpy as jnp
from jax import lax
from jax.experimental import pallas as pl
from jax.experimental.pallas import tpu as pltpu
from jax.sharding import PartitionSpec as P

EPS = 1e-06
HIGHEST = lax.Precision.HIGHEST
MESH = pl.DeviceIdType.MESH
VMEM = pltpu.VMEM
VMEM_LIMIT = 60 * 1024 * 1024
F32 = jnp.float32
BF16 = jnp.bfloat16


def rms_scale(value):
    return value * lax.rsqrt(jnp.mean(value * value, axis=-1, keepdims=True) + EPS)


def rms_back(grad_in, value):
    inverse = lax.rsqrt(jnp.mean(value * value, axis=-1, keepdims=True) + EPS)
    normal = value * inverse
    return inverse * (grad_in - normal * jnp.mean(grad_in * normal, axis=-1, keepdims=True))


def dot(left, right):
    return jnp.dot(left, right, preferred_element_type=F32)


def contract_cols(left, right):
    return lax.dot_general(left, right, (((1,), (1,)), ((), ())), preferred_element_type=F32)


def contract_cols_exact(left, right):
    return lax.dot_general(left, right, (((1,), (1,)), ((), ())), precision=HIGHEST)


def contract_rows(left, right):
    return lax.dot_general(left, right, (((0,), (0,)), ((), ())), preferred_element_type=F32)


def ring_place(ctx, n):
    odd = lax.rem(ctx, 2)
    half = lax.div(ctx, 2)
    return (1 - odd) * half + odd * (n - 1 - half)


def ring_owner(place, n):
    late = lax.div(place, n // 2)
    return (1 - late) * (2 * place) + late * (2 * (n - 1 - place) + 1)


def wrap(place, n):
    return lax.rem(place + 2 * n, n)


def ring_setup(n):
    me = lax.axis_index("ctx")
    tp = lax.axis_index("tp")
    place = ring_place(me, n)
    right = ring_owner(wrap(place + 1, n), n)
    left = ring_owner(wrap(place - 1, n), n)
    return me, tp, place, (right, left)


def greet(peers):
    barrier = pltpu.get_barrier_semaphore()
    for peer in peers:
        pl.semaphore_signal(barrier, inc=1, device_id=peer, device_id_type=MESH)
    pl.semaphore_wait(barrier, len(peers))


def ctx_peers(me, tp, n):
    return [(lax.rem(me + i, n), tp) for i in range(1, n)]


def remote(src, dst, send, recv, device):
    return pltpu.make_async_remote_copy(
        src_ref=src, dst_ref=dst, send_sem=send, recv_sem=recv, device_id=device, device_id_type=MESH
    )


class Gather:
    def __init__(self, n, place, sides, tp, chunks, send, recv):
        self.n, self.place, self.sides, self.tp = n, place, sides, tp
        self.chunks, self.send, self.recv = chunks, send, recv
        self.arrived = None

    def owner(self, side, back):
        return ring_owner(wrap(self.place - back if side == 0 else self.place + back, self.n), self.n)

    def copy(self, index, step, first):
        side, source, target = self.chunks[index]
        target = target(self.owner(side, step))
        return remote(
            source if first else target, target, self.send.at[index, step], self.recv.at[index, step],
            (self.sides[side], self.tp),
        )

    def arrive(self, index, step):
        side, _, target = self.chunks[index]
        target = target(self.owner(side, step + 1))
        remote(
            target, target, self.send.at[index, step], self.recv.at[index, step], (self.sides[side], self.tp)
        ).wait_recv()
        if self.arrived is not None:
            self.arrived(index, step)

    def begin(self, indices=None):
        for index in indices if indices is not None else range(len(self.chunks)):
            self.copy(index, 0, True).start()

    def forward(self, step):
        for index in range(len(self.chunks)):
            self.arrive(index, step - 1)
            self.copy(index, step, False).start()

    def last(self):
        for index in range(len(self.chunks)):
            self.arrive(index, self.n - 2)

    def sent(self):
        def finish(step, carry):
            for index in range(len(self.chunks)):
                self.copy(index, step, False).wait_send()
            return carry

        lax.fori_loop(0, self.n - 1, finish, 0)


class Moves:
    def __init__(self, semaphores):
        self.semaphores, self.count, self.open = semaphores, 0, {}

    def start(self, name, source, target):
        copy = pltpu.make_async_copy(source, target, self.semaphores.at[self.count])
        self.count += 1
        copy.start()
        self.open[name] = copy

    def wait(self, *names):
        for name in names or list(self.open):
            self.open.pop(name).wait()


def start_kernel(
    n, heads, group_map, doc_lengths, skip, earlier_ref, x_ref, small_in, bias_ref, wq_in, wk_in, wv_in, wg_in, wo_in,
    wq_out, wk_out, wv_out, wg_out, wo_ref, u_out, q_out, qr_out, kr_out, gl_out, fz_ref, k_out, v_out, aug_out,
    att_out, term_ref, gain_one, gain_two, qgain_ref, kgain_ref, wf_ref,
    x_vmem, wq_ref, wk_ref, wv_ref, wg_ref, u_ref, q_ref, k_all, v_all, aug_ref, att_ref, acc_ref, cat_ref,
    diff_ref, span_ref, tot_ref, before_ref, inside_all,
    small_all, acc_r, acc_l, inside_src,
    wsend, wrecv, osend, orecv, ksend, krecv, ssend, srecv, isend, irecv, spill, local,
):
    me, tp, place, sides = ring_setup(n)
    moves = Moves(local)
    moves.start("x", x_ref, x_vmem)
    greet(ctx_peers(me, tp, n))
    rows, cols = x_ref.shape
    shard, width = wq_in.shape
    half = rows // 2
    head_dim = width // heads

    def shard_rows(owner):
        return pl.ds(pl.multiple_of(owner * shard, 16), shard)

    def window(ref, c0, cw):
        return lambda owner: ref.at[shard_rows(owner), pl.ds(c0, cw)]

    def token_rows(owner):
        return pl.ds(pl.multiple_of(owner * rows, rows), rows)

    def block(ref, pair):
        return lambda owner: ref.at[pair, token_rows(owner), :]

    ring = (n, place, sides, tp)
    projections = Gather(
        *ring,
        [
            (side, source, window(target, 0, width))
            for side, source, target in ((0, wq_in, wq_ref), (1, wv_in, wv_ref), (0, wk_in, wk_ref), (1, wg_in, wg_ref))
        ],
        wsend, wrecv,
    )
    middle = width // 256 * 128
    outputs = Gather(
        *ring,
        [
            (side, wo_in.at[:, pl.ds(c0, cw)], window(wo_ref, c0, cw))
            for side, c0, cw in ((0, 0, middle), (1, middle, width - middle))
        ],
        osend, orecv,
    )
    members = [(0, k_all, k_out, 0), (1, k_all, k_out, 2), (0, v_all, v_out, 0), (1, v_all, v_out, 2)]
    members += [(0, k_all, k_out, 1), (1, v_all, v_out, 1)]
    pairs = Gather(
        *ring, [(side, block(ref, pair)(me), block(ref, pair)) for side, ref, _, pair in members], ksend, krecv
    )

    def spill_copy(index, step):
        side, ref, out, pair = members[index]
        owner = pairs.owner(side, step + 1)
        return pltpu.make_async_copy(
            block(ref, pair)(owner), block(out, pair)(owner), spill.at[index, step]
        )

    pairs.arrived = lambda index, step: spill_copy(index, step).start()

    projections.begin()
    exchange_start(n, me, tp, lambda peer: small_in, small_all, ssend, srecv)
    gathered = ((wq_in, wq_ref), (wk_in, wk_ref), (wv_in, wv_ref), (wg_in, wg_ref), (wo_in, wo_ref))
    for i, (source, target) in enumerate(gathered):
        moves.start(i, source, target.at[shard_rows(me)])
    moves.start("small", small_in, small_all.at[me])
    moves.wait("small")
    exchange_wait(n, me, tp, lambda peer: small_in, small_all, ssend, srecv)
    projections.forward(1)

    count = 2 * head_dim // n
    for i in range(n):
        block_small = small_all[i].astype(F32)
        gain_one[:, i * shard : (i + 1) * shard] = block_small[0:1, :shard]
        gain_two[:, i * shard : (i + 1) * shard] = block_small[1:2, :shard]
        wf_ref[:, i * shard : (i + 1) * shard] = block_small[8:16, :shard]
        target, at = (qgain_ref, i) if i < n // 2 else (kgain_ref, i - n // 2)
        for h in range(heads):
            lane = h * head_dim + at * count
            target[:, lane : lane + count] = block_small[2 + h : 3 + h, :count]

    size = 64

    def norm_rows(i, carry):
        here = pl.ds(pl.multiple_of(i * size, size), size)
        normed = (rms_scale(x_vmem[here, :].astype(F32)) * gain_one[...]).astype(BF16)
        for j in range(n):
            u_ref[j, here, :] = normed[:, j * shard : (j + 1) * shard]
        return carry

    moves.wait("x")
    lax.fori_loop(0, rows // size, norm_rows, 0)
    moves.start("u", u_ref, u_out)

    def grow(back):
        for side, acc, sources in ((0, acc_r, (wq_ref, wk_ref)), (1, acc_l, (wv_ref, wg_ref))):
            owner = projections.owner(side, back)
            for i, source in enumerate(sources):
                acc[:, i * width : (i + 1) * width] += dot(u_ref[owner], source[shard_rows(owner), :])

    acc_r[...] = jnp.zeros_like(acc_r)
    acc_l[...] = jnp.zeros_like(acc_l)
    moves.wait(0, 1, 2, 3, 4)
    grow(0)
    projections.forward(2)
    grow(1)
    grow(2)
    forget = jnp.zeros((16, rows), F32)
    for j in range(n):
        forget += contract_cols(small_all[j, :, :shard], u_ref[j])
    fz = forget[8:16] + bias_ref[:, 0:1]
    fz_ref[...] = fz
    logs = jnp.minimum(fz, 0.0) - jnp.log1p(jnp.exp(-jnp.abs(fz)))
    head = lax.broadcasted_iota(jnp.int32, logs.shape, 0)
    logs = jnp.where(head < heads, logs, 0.0)
    upto = (
        lax.broadcasted_iota(jnp.int32, (half, half), 0) <= lax.broadcasted_iota(jnp.int32, (half, half), 1)
    ).astype(F32)
    for g in range(2):
        inside_src[:, g * half : (g + 1) * half] = jnp.dot(
            logs[:, g * half : (g + 1) * half], upto, precision=HIGHEST, preferred_element_type=F32
        )
    exchange_start(n, me, tp, lambda peer: inside_src, inside_all, isend, irecv)
    moves.start("inside", inside_src, inside_all.at[me])

    def step_on(step, carry):
        projections.forward(step)
        grow(step)
        return carry

    lax.fori_loop(3, n - 2, step_on, 0)
    outputs.begin()
    projections.forward(n - 2)
    grow(n - 2)
    outputs.forward(1)
    projections.last()
    grow(n - 1)

    def head_norm(value):
        return value * lax.rsqrt(head_means(value * value, heads) + EPS)

    my_rows = token_rows(me)
    for pair in range(heads // 2):
        v_all[pair, my_rows, :] = acc_l[:, pair * LANES : (pair + 1) * LANES].astype(BF16)
    pairs.begin([2, 3, 5])
    keys = (head_norm(acc_r[:, width:]) * kgain_ref[...]).astype(BF16)
    for pair in range(heads // 2):
        k_all[pair, my_rows, :] = keys[:, pair * LANES : (pair + 1) * LANES]
    pairs.begin([0, 1, 4])
    for i, (source, target) in enumerate(
        ((wq_ref, wq_out), (wk_ref, wk_out), (wv_ref, wv_out), (wg_ref, wg_out))
    ):
        moves.start(i, source, target)
    moves.start("qr", acc_r.at[:, pl.ds(0, width)], qr_out)
    moves.start("kr", acc_r.at[:, pl.ds(width, width)], kr_out)
    moves.start("gl", acc_l.at[:, pl.ds(width, width)], gl_out)
    for i, (ref, out) in enumerate(((k_all, k_out), (v_all, v_out))):
        for pair in range(heads // 2):
            moves.start((i, pair), block(ref, pair)(me), block(out, pair)(me))
    q_ref[...] = (head_norm(acc_r[:, :width]) * qgain_ref[...] * 0.125).astype(BF16)
    moves.start("q", q_ref, q_out)

    moves.wait("inside")
    exchange_wait(n, me, tp, lambda peer: inside_src, inside_all, isend, irecv)
    tot_ref[...] = jnp.zeros_like(tot_ref)
    for i in range(n):
        for g in range(2):
            tot_ref[:, 2 * i + g : 2 * i + g + 1] = inside_all[i, :, (g + 1) * half - 1 : (g + 1) * half]
    before_ref[...] = jnp.dot(tot_ref[...], earlier_ref[...], precision=HIGHEST, preferred_element_type=F32)
    lane8 = lax.broadcasted_iota(jnp.int32, (8, LANES), 1)

    def offsets_of(shard_index):
        parts = []
        for g in range(2):
            before = jnp.sum(jnp.where(lane8 == 2 * shard_index + g, before_ref[...], 0.0), axis=1, keepdims=True)
            parts.append(inside_all[shard_index, :, g * half : (g + 1) * half] + before)
        return jnp.concatenate(parts, axis=1)

    def aug_rows(i, carry):
        aug_ref[token_rows(i), :] = key_pieces(offsets_of(i))
        return carry

    pairs.forward(1)
    lax.fori_loop(0, n, aug_rows, 0)
    moves.start("aug", aug_ref, aug_out)

    first, second = group_map[2 * me], group_map[2 * me + 1]
    in_order = first < second
    query_groups = (jnp.minimum(first, second), jnp.maximum(first, second))
    mine = turn(offsets_of(me))
    term_ref[...] = mine
    spread_heads(q_ref, row_pieces(mine, True), put_rows(cat_ref), heads, in_order)
    acc_ref[...] = jnp.zeros_like(acc_ref)
    query_at = lax.broadcasted_iota(jnp.int32, (half, half), 0)
    key_at = lax.broadcasted_iota(jnp.int32, (half, half), 1)
    diff_ref[...] = key_at - query_at
    for i, group in enumerate(query_groups):
        span_ref[i] = document_start(group * half + query_at, doc_lengths) - key_at
    ones = jnp.ones((half, LANES), BF16)

    def attend(i, back):
        late = lax.div(i, 2)
        pair = (1 - late) * 2 * i + late
        side = lax.rem(i, 2)
        owner = ring_owner(wrap(place + (2 * side - 1) * back, n), n)
        one, two = group_map[2 * owner], group_map[2 * owner + 1]
        forward = one < two
        key_groups = (jnp.minimum(one, two), jnp.maximum(one, two))
        top = pl.ds(pl.multiple_of(owner * rows, rows), half)
        bottom = pl.ds(pl.multiple_of(owner * rows + half, half), half)
        blocks = []
        for ref in (k_all.at[pair], v_all.at[pair], aug_ref):
            blocks.append(in_pack_order(forward, ref[top, :], ref[bottom, :]))
        for qi, ki in ((0, 0), (1, 0), (1, 1)):
            query_group, key_group = query_groups[qi], key_groups[ki]
            skipped = jnp.where(key_group < query_group, skip[query_group, key_group], 0)
            mask = (diff_ref[...] <= (query_group - key_group) * half) & (
                span_ref[qi] <= key_group * half - (skipped == 1).astype(jnp.int32) * (1 << 30)
            )
            here = pl.ds(qi * half, half)
            keys = jnp.concatenate([blocks[0][ki], blocks[2][ki]], axis=1)
            values = jnp.concatenate([blocks[1][ki], ones], axis=1)
            for e in range(2):
                h = 2 * pair + e
                weights = jnp.where(mask, jnp.exp(contract_cols(cat_ref[h, here, :], keys)), 0.0)
                acc_ref[h, here, :] += dot(weights.astype(BF16), values)

    def attend_all(count, back):
        def body(i, carry):
            attend(i, back)
            return carry

        lax.fori_loop(0, count, body, 0)

    attend_all(3, 0)
    attend_all(2, 1)

    def pair_step(step, count):
        outputs.forward(step)
        pairs.forward(step)
        attend_all(count, step)

    def early_step(step, carry):
        pair_step(step, 2)
        return carry

    def late_step(step, carry):
        pair_step(step, 4)
        return carry

    lax.fori_loop(2, n // 2, early_step, 0)
    pair_step(n // 2, 3)
    lax.fori_loop(n // 2 + 1, n - 1, late_step, 0)
    outputs.last()
    pairs.last()
    attend_all(4, n - 1)

    lane = lax.broadcasted_iota(jnp.int32, (rows, LANES), 1)
    low = low_lanes(rows)
    totals = jnp.ones((rows, LANES), F32)
    for pair in range(heads // 2):
        parts = []
        for h in (2 * pair, 2 * pair + 1):
            value = jnp.concatenate(in_pack_order(in_order, acc_ref[h, :half, :], acc_ref[h, half:, :]), axis=0)
            parts.append(value)
            totals = jnp.where(lane == h, value[:, LANES:], totals)
        att_ref[:, pair * LANES : (pair + 1) * LANES] = jnp.where(
            low, parts[0][:, :LANES], parts[1][:, :LANES]
        ) / jnp.where(low, parts[0][:, LANES:], parts[1][:, LANES:])
    moves.start("att", att_ref, att_out)
    term_ref[...] -= jnp.log(totals)

    def spilled(step, carry):
        for index in range(len(members)):
            spill_copy(index, step).wait()
        return carry

    lax.fori_loop(0, n - 1, spilled, 0)
    moves.wait()
    projections.sent()
    outputs.sent()
    pairs.sent()


def start_forward(n, collective_id, group_map, doc_lengths, skip, earlier, x, small, bias, weights, out_weight):
    rows, cols = x.shape
    shard, width = out_weight.shape
    heads = bias.shape[0]
    half = rows // 2
    dma = pltpu.SemaphoreType.DMA
    vmem = pl.BlockSpec(memory_space=VMEM)
    anywhere = pl.BlockSpec(memory_space=pl.ANY)
    bias = jnp.broadcast_to(jnp.pad(bias, (0, 8 - heads))[:, None], (8, LANES))
    by_pair = (heads // 2, n * rows, LANES)
    weight, wide, narrow = (n * shard, width), (rows, cols), (rows, width)
    shapes = (
        [(weight, BF16)] * 5
        + [((n, rows, shard), BF16), (narrow, BF16)]
        + [(narrow, F32)] * 3
        + [((8, rows), F32)]
        + [(by_pair, BF16)] * 2
        + [((n * rows, LANES), BF16), (narrow, F32), ((rows, LANES), F32)]
        + [((1, cols), F32)] * 2
        + [((1, width), F32)] * 2
        + [((8, cols), F32)]
    )
    return pl.pallas_call(
        functools.partial(start_kernel, n, heads),
        out_shape=[jax.ShapeDtypeStruct(*shape) for shape in shapes],
        in_specs=[smem(), smem(), smem(), vmem, anywhere, vmem, vmem] + [anywhere] * 5,
        out_specs=[anywhere if i < 10 or 11 <= i <= 14 else vmem for i in range(len(shapes))],
        scratch_shapes=[
            VMEM(wide, BF16),
            *[VMEM(weight, BF16)] * 4,
            VMEM((n, rows, shard), BF16),
            VMEM(narrow, BF16),
            *[VMEM(by_pair, BF16)] * 2,
            VMEM((n * rows, LANES), BF16),
            VMEM(narrow, F32),
            VMEM((heads, rows, 2 * LANES), F32),
            VMEM((heads, rows, 2 * LANES), BF16),
            VMEM((half, half), jnp.int32),
            VMEM((2, half, half), jnp.int32),
            VMEM((8, LANES), F32),
            VMEM((8, LANES), F32),
            VMEM((n, 8, rows), F32),
            VMEM((n, 16, 256), BF16),
            VMEM((rows, 2 * width), F32),
            VMEM((rows, 2 * width), F32),
            VMEM((8, rows), F32),
            *[dma((4, n - 1))] * 2,
            *[dma((2, n - 1))] * 2,
            *[dma((6, n - 1))] * 2,
            *[dma((n - 1,))] * 4,
            dma((6, n - 1)),
            dma((26,)),
        ],
        compiler_params=pltpu.CompilerParams(
            collective_id=collective_id, has_side_effects=True, vmem_limit_bytes=VMEM_LIMIT
        ),
    )(group_map, doc_lengths, skip, earlier, x, small, bias, *weights, out_weight)


class ScatterRing:
    def __init__(self, n, plan, local_term, slots, firsts, write, send, recv, place, sides, tp, source=None):
        self.n, self.place, self.sides, self.tp = n, place, sides, tp
        self.source, self.next = source, 1
        self.local_term, self.write = local_term, write
        self.slots, self.firsts, self.send, self.recv = slots, firsts, send, recv
        self.order = []
        starts = [0, 0]
        for index in range(max(len(plan[0]), len(plan[1]))):
            for side in (0, 1):
                if index < len(plan[side]):
                    width, tag = plan[side][index]
                    self.order.append((side, index, starts[side], width, tag))
                    starts[side] += width

    def target(self, side, step):
        step = -1 - step if side == 0 else 1 + step
        return ring_owner(wrap(self.place + step, self.n), self.n)

    def hop(self, side, index, start, width, step, first):
        cols = pl.ds(start, width)
        slots = self.slots[side]
        if not first:
            source = slots.at[step - 1, :, cols]
        elif self.source is None:
            source = self.firsts[side].at[:, cols]
        else:
            source = self.source(self.target(side, 0), side, cols)
        return remote(
            source,
            slots.at[step, :, cols],
            self.send.at[side, index, step],
            self.recv.at[side, index, step],
            (self.sides[side], self.tp),
        )

    def begin(self):
        for side, index, start, width, tag in self.order:
            if self.source is None:
                term = self.local_term(self.target(side, 0), tag)
                self.firsts[side][:, start : start + width] = term.astype(BF16)
            self.hop(side, index, start, width, 0, True).start()

    def forward(self, step):
        for side, index, start, width, tag in self.order:
            term = self.local_term(self.target(side, step), tag)
            slot = self.slots[side].at[step - 1, :, pl.ds(start, width)]
            self.hop(side, index, start, width, step - 1, True).wait_recv()
            slot[...] = (slot[...].astype(F32) + term).astype(BF16)
            self.hop(side, index, start, width, step, False).start()

    def span(self, first, last):
        def body(step, carry):
            self.forward(step)
            return carry

        if last > first:
            lax.fori_loop(first, last, body, 0)

    def advance(self, count):
        last = min(self.next + count, self.n - 1)
        self.span(self.next, last)
        self.next = last

    def end(self):
        n = self.n
        self.advance(n)
        for side, index, start, width, tag in self.order:
            term = self.local_term(self.target(side, n - 1), tag)
            self.hop(side, index, start, width, n - 2, True).wait_recv()
            self.write(tag, self.slots[side][n - 2, :, start : start + width].astype(F32) + term)
        if self.source is None:
            self.sent()

    def sent(self):
        for side, index, start, width, tag in self.order:
            self.hop(side, index, start, width, 0, True).wait_send()

        def finish(step, carry):
            for side, index, start, width, tag in self.order:
                self.hop(side, index, start, width, step, False).wait_send()
            return carry

        lax.fori_loop(1, self.n - 1, finish, 0)


def exchange_start(n, me, tp, source_of, landing, send, recv):
    for i in range(1, n):
        peer = lax.rem(me + i, n)
        remote(source_of(peer), landing.at[me], send.at[i - 1], recv.at[i - 1], (peer, tp)).start()


def exchange_wait(n, me, tp, source_of, landing, send, recv):
    for i in range(1, n):
        peer = lax.rem(me - i + n, n)
        remote(source_of(peer), landing.at[peer], send.at[i - 1], recv.at[i - 1], (peer, tp)).wait()


def ordered_sum(n, landing):
    total = landing[0]
    for i in range(1, n):
        total = total + landing[i]
    return total


def pair_scatter_kernel(
    n, key_ref, value_ref, col_ref, row_ref, key_out, value_out, off_out, tot_out,
    slot_r, slot_l, first_r, first_l, off_ref, tot_ref, off_land, tot_land,
    send, recv, osend, orecv, tsend, trecv, local,
):
    me, tp, place, sides = ring_setup(n)
    off_ref[...] = col_ref[...]
    off_ref[me] += row_ref[...]
    group_rows = row_ref.shape[1] // 2
    tot_ref[...] = jnp.zeros_like(tot_ref)
    for i in range(n):
        for g in range(2):
            tot_ref[:, 2 * i + g : 2 * i + g + 1] = jnp.sum(
                off_ref[i, :, g * group_rows : (g + 1) * group_rows], axis=1, keepdims=True
            )
    greet(ctx_peers(me, tp, n))
    exchange_start(n, me, tp, lambda peer: off_ref.at[peer], off_land, osend, orecv)
    exchange_start(n, me, tp, lambda peer: tot_ref, tot_land, tsend, trecv)
    mine = pltpu.make_async_copy(off_ref.at[me], off_land.at[me], local.at[0])
    mine_tot = pltpu.make_async_copy(tot_ref, tot_land.at[me], local.at[1])
    mine.start()
    mine_tot.start()
    width = key_ref.shape[2]
    plan = [
        [(w, (0, c)) for c, w in pieces(width, 128)],
        [(w, (1, c)) for c, w in pieces(width, 128)],
    ]

    def local_term(owner, tag):
        which, c0 = tag
        return (key_ref, value_ref)[which][owner, :, c0 : c0 + 128].astype(F32)

    def write(tag, value):
        which, c0 = tag
        (key_out, value_out)[which][:, c0 : c0 + 128] = value

    ring = ScatterRing(
        n, plan, local_term, (slot_r, slot_l), (first_r, first_l), write, send, recv, place, sides, tp
    )
    ring.begin()
    ring.end()
    mine.wait()
    mine_tot.wait()
    exchange_wait(n, me, tp, lambda peer: off_ref.at[peer], off_land, osend, orecv)
    exchange_wait(n, me, tp, lambda peer: tot_ref, tot_land, tsend, trecv)
    off_out[...] = ordered_sum(n, off_land)
    tot_out[...] = ordered_sum(n, tot_land)


def pieces(width, step):
    return [(c, min(step, width - c)) for c in range(0, width, step)]


def pair_scatter(n, collective_id, keys, values, columns, own_rows):
    _, rows, width = keys.shape
    offs, tots = columns, jax.ShapeDtypeStruct((8, LANES), F32)
    chunks = len(pieces(width, 128))
    return pl.pallas_call(
        functools.partial(pair_scatter_kernel, n),
        out_shape=[
            jax.ShapeDtypeStruct((rows, width), F32),
            jax.ShapeDtypeStruct((rows, width), F32),
            jax.ShapeDtypeStruct(offs.shape[1:], F32),
            jax.ShapeDtypeStruct(tots.shape, F32),
        ],
        in_specs=[pl.BlockSpec(memory_space=VMEM)] * 4,
        out_specs=[pl.BlockSpec(memory_space=VMEM)] * 4,
        scratch_shapes=[
            VMEM((n - 1, rows, width), BF16),
            VMEM((n - 1, rows, width), BF16),
            VMEM((rows, width), BF16),
            VMEM((rows, width), BF16),
            VMEM(offs.shape, F32),
            VMEM(tots.shape, F32),
            VMEM(offs.shape, F32),
            VMEM((n,) + tots.shape, F32),
            pltpu.SemaphoreType.DMA((2, chunks, n - 1)),
            pltpu.SemaphoreType.DMA((2, chunks, n - 1)),
            pltpu.SemaphoreType.DMA((n - 1,)),
            pltpu.SemaphoreType.DMA((n - 1,)),
            pltpu.SemaphoreType.DMA((n - 1,)),
            pltpu.SemaphoreType.DMA((n - 1,)),
            pltpu.SemaphoreType.DMA((2,)),
        ],
        compiler_params=pltpu.CompilerParams(
            collective_id=collective_id, has_side_effects=True, vmem_limit_bytes=VMEM_LIMIT
        ),
    )(keys, values, columns, own_rows)


def weight_scatter_kernel(n, plan, left_count, grads, *refs):
    lefts, refs = refs[:left_count], refs[left_count:]
    rights, refs = refs[:grads], refs[grads:]
    small_ref, part_ref, x_ref, gain_ref, dmid_ref, refs = *refs[:5], refs[5:]
    outs, refs = refs[:grads], refs[grads:]
    small_out, input_out, slot_r, slot_l, first_r, first_l, own_small, land, sum_out, refs = *refs[:9], refs[9:]
    tp_bufs, refs = refs[:4], refs[4:]
    send, recv, xsend, xrecv, tsend, trecv, local = refs
    me, tp, place, sides = ring_setup(n)
    chip, core, sibling, across = tp_setup()
    greet(ctx_peers(me, tp, n) + [sibling, across])
    shard = lefts[0].shape[2]
    half = part_ref.shape[0] // 2

    def local_term(owner, tag):
        left, right, c0, cw = tag
        return contract_rows(lefts[left][owner], rights[right][:, c0 : c0 + cw])

    def write(tag, value):
        _, right, c0, cw = tag
        outs[right][:, c0 : c0 + cw] = value

    ring = ScatterRing(
        n, plan, local_term, (slot_r, slot_l), (first_r, first_l), write, send, recv, place, sides, tp
    )

    def part(which, c):
        cols = part_ref.shape[1] // TP_CHUNKS
        return part_ref[pl.ds(pl.multiple_of(which * half, half), half), c * cols : (c + 1) * cols].astype(F32)

    total = TpSum(part, sum_out, tp_bufs, tsend, trecv, core, sibling, across)
    total.first()
    total.second()
    ring.begin()
    total.third()
    ring.advance(1)
    total.fourth()

    own_small[...] = small_ref[...]
    cols = part_ref.shape[1]
    size = 64

    def gain_rows(i, acc):
        rows = pl.ds(pl.multiple_of(i * size, size), size)
        value = x_ref[rows, :].astype(F32)
        inverse = lax.rsqrt(jnp.mean(value * value, axis=-1, keepdims=True) + EPS)
        normal = value * inverse
        grad = sum_out[rows, :].astype(F32)
        back = grad * gain_ref[...]
        back = inverse * (back - normal * jnp.mean(back * normal, axis=-1, keepdims=True))
        input_out[rows, :] = dmid_ref[rows, :] + back
        return acc + jnp.sum((grad * normal).reshape(size // 8, 8, cols), axis=0)

    gains = lax.fori_loop(0, 2 * half // size, gain_rows, jnp.zeros((8, cols), F32))
    gains = jnp.sum(gains, axis=0, keepdims=True)
    for i in range(n):
        own_small[i, 0:1, :shard] = gains[:, i * shard : (i + 1) * shard]
    exchange_start(n, me, tp, lambda peer: own_small.at[peer], land, xsend, xrecv)
    mine = pltpu.make_async_copy(own_small.at[me], land.at[me], local.at[0])
    mine.start()
    ring.end()
    mine.wait()
    exchange_wait(n, me, tp, lambda peer: own_small.at[peer], land, xsend, xrecv)
    small_out[...] = ordered_sum(n, land)


def weight_scatter(n, collective_id, plan, lefts, rights, small, part, x, gain, dmid):
    rows = lefts[0].shape[2]
    chunks = max(len(plan[0]), len(plan[1]))
    totals = [sum(width for width, _ in side) for side in plan]
    return pl.pallas_call(
        functools.partial(weight_scatter_kernel, n, plan, len(lefts), len(rights)),
        out_shape=[jax.ShapeDtypeStruct((rows, right.shape[1]), F32) for right in rights]
        + [jax.ShapeDtypeStruct(small.shape[1:], F32), jax.ShapeDtypeStruct(part.shape, F32)],
        in_specs=[pl.BlockSpec(memory_space=VMEM)] * (len(lefts) + len(rights) + 5),
        out_specs=[pl.BlockSpec(memory_space=VMEM)] * (len(rights) + 2),
        scratch_shapes=[
            VMEM((n - 1, rows, totals[0]), BF16),
            VMEM((n - 1, rows, totals[1]), BF16),
            VMEM((rows, totals[0]), BF16),
            VMEM((rows, totals[1]), BF16),
            VMEM(small.shape, F32),
            VMEM(small.shape, F32),
            VMEM(part.shape, BF16),
            *tp_buffers(*part.shape),
            pltpu.SemaphoreType.DMA((2, chunks, n - 1)),
            pltpu.SemaphoreType.DMA((2, chunks, n - 1)),
            pltpu.SemaphoreType.DMA((n - 1,)),
            pltpu.SemaphoreType.DMA((n - 1,)),
            pltpu.SemaphoreType.DMA((3, TP_CHUNKS)),
            pltpu.SemaphoreType.DMA((3, TP_CHUNKS)),
            pltpu.SemaphoreType.DMA((1,)),
        ],
        compiler_params=pltpu.CompilerParams(
            collective_id=collective_id, has_side_effects=True, vmem_limit_bytes=VMEM_LIMIT
        ),
    )(*lefts, *rights, small, part, x, gain, dmid)


def tp_setup():
    ctx = lax.axis_index("ctx")
    tp = lax.axis_index("tp")
    chip = lax.div(tp, 2)
    core = lax.rem(tp, 2)
    sibling = (ctx, 2 * chip + 1 - core)
    across = (ctx, 2 * (1 - chip) + core)
    return chip, core, sibling, across


TP_CHUNKS = 4


def tp_buffers(rows, width):
    return [VMEM((rows // 2, width), BF16) for _ in range(4)]


class TpSum:
    def __init__(self, part, out, bufs, send, recv, core, sibling, across):
        self.part, self.out, self.send, self.recv = part, out, send, recv
        self.away, self.land_a, self.half_b, self.land_b = bufs
        self.core, self.sibling, self.across = core, sibling, across
        self.half = self.away.shape[0]
        self.size = self.away.shape[1] // TP_CHUNKS

    def cols(self, c):
        return pl.ds(c * self.size, self.size)

    def copy(self, stage, c, which=None):
        cols = self.cols(c)
        if stage == 0:
            source, target, device = self.away.at[:, cols], self.land_a.at[:, cols], self.sibling
        elif stage == 1:
            source, target, device = self.half_b.at[:, cols], self.land_b.at[:, cols], self.across
        else:
            source = target = self.out.at[self.rows(which), cols]
            device = self.sibling
        return remote(source, target, self.send.at[stage, c], self.recv.at[stage, c], device)

    def rows(self, which):
        return pl.ds(pl.multiple_of(which * self.half, self.half), self.half)

    def first(self):
        for c in range(TP_CHUNKS):
            self.away[:, self.cols(c)] = self.part(1 - self.core, c).astype(BF16)
            self.copy(0, c).start()

    def second(self):
        for c in range(TP_CHUNKS):
            cols = self.cols(c)
            mine = self.part(self.core, c)
            self.copy(0, c).wait_recv()
            self.half_b[:, cols] = (mine + self.land_a[:, cols].astype(F32)).astype(BF16)
            self.copy(1, c).start()

    def third(self):
        for c in range(TP_CHUNKS):
            cols = self.cols(c)
            self.copy(1, c).wait_recv()
            both = self.half_b[:, cols].astype(F32) + self.land_b[:, cols].astype(F32)
            self.out[self.rows(self.core), cols] = both.astype(BF16)
            self.copy(2, c, self.core).start()

    def fourth(self):
        for c in range(TP_CHUNKS):
            self.copy(2, c, 1 - self.core).wait_recv()
            self.copy(0, c).wait_send()
            self.copy(1, c).wait_send()
            self.copy(2, c, self.core).wait_send()


class TpSplit:
    def __init__(self, part, bufs, send, recv, chip, core, sibling, across):
        self.part, self.send, self.recv = part, send, recv
        self.away, self.land_a, self.half_b, self.land_b = bufs
        self.chip, self.core, self.sibling, self.across = chip, core, sibling, across

    def copy(self, stage):
        if stage < 2:
            return remote(
                self.away.at[stage], self.land_a.at[stage], self.send.at[stage], self.recv.at[stage], self.sibling
            )
        return remote(self.half_b, self.land_b, self.send.at[2], self.recv.at[2], self.across)

    def first(self):
        for i, chip in enumerate((1 - self.chip, self.chip)):
            self.away[i] = self.part(chip, 1 - self.core).astype(BF16)
            self.copy(i).start()

    def second(self):
        mine = self.part(1 - self.chip, self.core)
        self.copy(0).wait_recv()
        self.half_b[...] = (mine + self.land_a[0].astype(F32)).astype(BF16)
        self.copy(2).start()

    def third(self):
        mine = self.part(self.chip, self.core)
        self.copy(1).wait_recv()
        self.copy(2).wait_recv()
        total = mine + self.land_a[1].astype(F32) + self.land_b[...].astype(F32)
        for stage in range(3):
            self.copy(stage).wait_send()
        return total


def feed_kernel(n, heads, attention, *refs):
    if attention:
        (group_map, doc_lengths, skip, q_in, term_in, k_in, v_in, aug_in), refs = refs[:8], refs[8:]
    (att_in, gl_in, outw_in, x_in, gain_ref, grad_in, wg_in, wu_in, wd_in), refs = refs[:9], refs[9:]
    (gated_out, layer_ref, down_out, gate_out, up_out, dmid_out, do_out, dgl_out, gain_out), refs = refs[:9], refs[9:]
    if attention:
        (dm_out, dq_out, drow_ref, dk_out, dv_out, dcol_ref), refs = refs[:6], refs[6:]
    (
        att_ref, gl_ref, outw_ref, x_ref, grad_ref, gated_ref, normed_ref, dgt_ref, dup_ref, do_ref, dgl_ref,
        gate_all, up_all, down_all, accs, dhid_acc, hid_ref, branch_ref, mid_ref, dw_ref, dy_ref,
        a0, a1, a2, a3, b3, s0, s1, s2, s3, dslot_r, dslot_l, dfirst_r, dfirst_l, eslot_r, eslot_l, efirst_r, efirst_l,
        gsend, grecv, hsend, hrecv, asend, arecv, bsend, brecv, ssend, srecv, dsend, drecv, esend, erecv, local,
    ), refs = refs[:53], refs[53:]
    if attention:
        term_ref, dm_ref, diff_ref, span_ref, stage, kv_sem, stage_sem = refs
    gate_acc, up_acc = accs.at[0], accs.at[1]
    me, tp, place, sides = ring_setup(n)
    chip, core, sibling, across = tp_setup()
    moves = Moves(local)
    for name, source, target in (
        ("att", att_in, att_ref), ("gl", gl_in, gl_ref), ("outw", outw_in, outw_ref), ("grad", grad_in, grad_ref),
        ("x", x_in, x_ref),
    ):
        moves.start(name, source, target)
    if attention:
        moves.start("term", term_in, term_ref)
    greet([(side, tp) for side in sides] + [sibling, across])
    shard, hidden = wg_in.shape
    rows, width = x_in.shape
    half = rows // 2
    hw = hidden // 2
    size = 64
    ring = (n, place, sides, tp)

    def rows_of(owner):
        return pl.ds(pl.multiple_of(owner * shard, 16), shard)

    def window(ref, c0, cw):
        return lambda owner: ref.at[rows_of(owner), pl.ds(c0, cw)]

    def chunks(members):
        return [(side, source.at[:, pl.ds(c0, cw)], window(target, c0, cw)) for side, source, target, c0, cw in members]

    gates = Gather(
        *ring,
        chunks(
            [
                (side, source, target, c0, hw)
                for c0 in (0, hw)
                for side, source, target in ((0, wg_in, gate_all), (1, wu_in, up_all))
            ]
        ),
        gsend, grecv,
    )
    downs = Gather(
        *ring,
        chunks([(side, wd_in, down_all, side * hw + c0, hw // 2) for c0 in (0, hw // 2) for side in (0, 1)]),
        hsend, hrecv,
    )
    gates.begin()
    for i, (source, target) in enumerate(((wg_in, gate_all), (wu_in, up_all), (wd_in, down_all))):
        moves.start(i, source, target.at[rows_of(me)])

    moves.wait("att", "gl")
    gated_ref[...] = (att_ref[...] * jax.nn.sigmoid(gl_ref[...])).astype(BF16)
    moves.start("gated", gated_ref, gated_out)
    moves.wait("outw")
    span = width // TP_CHUNKS

    def branch_part(which, c):
        mine = gated_ref[pl.ds(pl.multiple_of(which * half, half), half), :]
        return contract_cols(mine, outw_ref[c * span : (c + 1) * span, :])

    branch = TpSum(branch_part, branch_ref, (a0, a1, a2, a3), asend, arecv, core, sibling, across)
    branch.first()
    branch.second()
    gates.forward(1)
    moves.wait("grad")
    for j in range(n):
        dy_ref[j] = grad_ref[:, j * shard : (j + 1) * shard]
    dhid_acc[...] = jnp.zeros_like(dhid_acc)
    gate_acc[...] = jnp.zeros_like(gate_acc)
    up_acc[...] = jnp.zeros_like(up_acc)

    def grow_back(back):
        for side in (0, 1):
            owner = downs.owner(side, back)
            cols = pl.ds(side * hw, hw)
            dhid_acc[:, cols] += dot(dy_ref[owner], down_all[rows_of(owner), cols])

    def grow(back):
        for side, acc, source in ((0, gate_acc, gate_all), (1, up_acc, up_all)):
            owner = gates.owner(side, back)
            acc[...] += dot(normed_ref[owner], source[rows_of(owner), :])

    moves.wait(0, 1, 2)
    grow_back(0)
    gates.forward(2)
    branch.third()
    branch.fourth()
    moves.wait("x")

    def norm_rows(i, carry):
        here = pl.ds(pl.multiple_of(i * size, size), size)
        middle = x_ref[here, :].astype(F32) + branch_ref[here, :].astype(F32)
        mid_ref[here, :] = middle
        normed = (rms_scale(middle) * gain_ref[...]).astype(BF16)
        for j in range(n):
            normed_ref[j, here, :] = normed[:, j * shard : (j + 1) * shard]
        return carry

    lax.fori_loop(0, rows // size, norm_rows, 0)
    own = pl.ds(pl.multiple_of(tp * span, span), span)
    layer_ref[...] = mid_ref[:, own]
    if attention:
        narrow = q_in.shape[1]
        q_ref = x_ref.at[:, pl.ds(0, narrow)]
        moves.start("q", q_in, q_ref)
        for i in range(n):
            moves.start(
                ("aug", i),
                aug_in.at[pl.ds(i * rows, rows), :],
                x_ref.at[:, pl.ds(narrow + i * LANES, LANES)],
            )
    gates.forward(3)

    def grow_step(step, carry):
        grow(step)
        return carry

    lax.fori_loop(0, 4, grow_step, 0)

    def gate_step(step, carry):
        gates.forward(step)
        grow(step)
        return carry

    lax.fori_loop(4, n - 1, gate_step, 0)
    downs.begin()
    gates.last()
    grow(n - 1)

    def hid_rows(i, carry):
        here = pl.ds(pl.multiple_of(i * size, size), size)
        gate, up = gate_acc[here, :], up_acc[here, :]
        open_gate = jax.nn.sigmoid(gate)
        silu = gate * open_gate
        hid_ref[here, :] = (silu * up).astype(BF16)
        gate_acc[here, :] = up * open_gate * (1.0 + gate * (1.0 - open_gate))
        up_acc[here, :] = silu
        return carry

    lax.fori_loop(0, rows // size, hid_rows, 0)

    def down_step(step, carry):
        downs.forward(step)
        grow_back(step)
        return carry

    lax.fori_loop(1, n - 2, down_step, 0)
    downs.forward(n - 2)

    def down_term(owner, tag):
        return contract_rows(dy_ref[owner], hid_ref[:, tag * hw : (tag + 1) * hw])

    down_ref = accs.at[0, pl.ds(0, shard), :]
    gate_ref = accs.at[0, pl.ds(shard, shard), :]
    up_ref = accs.at[1, pl.ds(0, shard), :]

    def down_write(tag, value):
        down_ref[:, tag * hw : (tag + 1) * hw] = value

    def early_term(owner, tag):
        which, c0 = tag
        return contract_rows(normed_ref[owner], (dgt_ref, dup_ref)[which][:, c0 : c0 + hw])

    def early_write(tag, value):
        which, c0 = tag
        (gate_ref, up_ref)[which][:, c0 : c0 + hw] = value

    backs = ScatterRing(
        n, [[(hw, 0)], [(hw, 1)]], down_term, (dslot_r, dslot_l), (dfirst_r, dfirst_l), down_write,
        dsend, drecv, place, sides, tp,
    )
    earlies = ScatterRing(
        n, [[(hw, (i, 0)), (hw, (i, hw))] for i in range(2)], early_term, (eslot_r, eslot_l), (efirst_r, efirst_l),
        early_write, esend, erecv, place, sides, tp,
    )
    backs.begin()
    grow_back(n - 2)
    downs.last()
    grow_back(n - 1)

    def grad_rows(i, carry):
        here = pl.ds(pl.multiple_of(i * size, size), size)
        dhid = dhid_acc[here, :]
        dgt_ref[here, :] = (dhid * gate_acc[here, :]).astype(BF16)
        dup_ref[here, :] = (dhid * up_acc[here, :]).astype(BF16)
        return carry

    lax.fori_loop(0, rows // size, grad_rows, 0)

    def dw_part(which, c):
        mine = pl.ds(pl.multiple_of(which * half, half), half)
        back = pl.ds(c * span, span)
        return contract_cols(dgt_ref[mine, :], gate_all[back, :]) + contract_cols(dup_ref[mine, :], up_all[back, :])

    def layer_part(which_chip, which_core):
        back = pl.ds(pl.multiple_of((2 * which_chip + which_core) * span, span), span)
        return contract_cols(hid_ref[...], down_all[back, :])

    total = TpSum(dw_part, dw_ref, (a0, a1, a2, b3), bsend, brecv, core, sibling, across)
    layer = TpSplit(layer_part, (s0, s1, s2, s3), ssend, srecv, chip, core, sibling, across)
    total.first()
    backs.advance(1)
    earlies.begin()
    total.second()
    gates.sent()
    if attention:
        pairs = heads // 2

        def kv_copies(it):
            part, pair = lax.div(it, pairs), lax.rem(it, pairs)
            source = pl.ds(pl.multiple_of(part * rows, rows), rows)
            target = pl.ds(pl.multiple_of(pair * rows, rows), rows)
            lanes = pl.ds(pl.multiple_of(part * LANES, LANES), LANES)
            return [
                pltpu.make_async_copy(ref.at[pair, source, :], held.at[target, lanes], kv_sem.at[i, it])
                for i, (ref, held) in enumerate(((k_in, gate_all), (v_in, up_all)))
            ]

        def bring(it, carry):
            for copy in kv_copies(it):
                copy.start()
            return carry

        lax.fori_loop(0, n * pairs, bring, 0)
    layer.first()
    layer.second()
    backs.advance(1)
    earlies.advance(1)
    backs.advance(1)
    earlies.advance(1)
    total.third()
    total.fourth()

    def middle_rows(i, acc):
        here = pl.ds(pl.multiple_of(i * size, size), size)
        middle = mid_ref[here, :]
        inverse = lax.rsqrt(jnp.mean(middle * middle, axis=-1, keepdims=True) + EPS)
        normal = middle * inverse
        dw = dw_ref[here, :].astype(F32)
        back = dw * gain_ref[...]
        back = inverse * (back - normal * jnp.mean(back * normal, axis=-1, keepdims=True))
        dmid = grad_ref[here, :].astype(F32) + back
        mid_ref[here, :] = dmid
        low = dmid.astype(BF16)
        branch_ref[here, :] = low
        if attention:
            for j in range(n):
                dm_ref[j, here, :] = low[:, j * shard : (j + 1) * shard]
        return acc + jnp.sum((dw * normal).reshape(size // 8, 8, width), axis=0)

    gain_out[...] = lax.fori_loop(0, rows // size, middle_rows, jnp.zeros((8, width), F32))
    moves.start("dmid", mid_ref, dmid_out)
    if attention:
        moves.start("dm", dm_ref, dm_out)
    da = dot(branch_ref[...], outw_ref[...])
    open_gate = jax.nn.sigmoid(gl_ref[...])
    do_ref[...] = (da * open_gate).astype(BF16)
    dgl_ref[...] = (da * att_ref[...] * open_gate * (1.0 - open_gate)).astype(BF16)
    moves.start("do", do_ref, do_out)
    moves.start("dgl", dgl_ref, dgl_out)
    backs.advance(1)
    earlies.advance(1)
    layer_ref[...] += layer.third()

    if attention:
        moves.wait("q", "term", *[("aug", i) for i in range(n)])
        first, second = group_map[2 * me], group_map[2 * me + 1]
        in_order = first < second
        query_groups = (jnp.minimum(first, second), jnp.maximum(first, second))

        def put_in(ref):
            def put(h, value, extra):
                ref[:, 2 * h * LANES : (2 * h + 1) * LANES] = value
                ref[:, (2 * h + 1) * LANES : (2 * h + 2) * LANES] = extra

            return put

        spread_heads(q_ref, row_pieces(term_ref[...], True), put_in(dw_ref), heads, in_order)
        delta = head_sums(do_ref[...].astype(F32) * att_ref[...], heads)
        spread_heads(do_ref, row_pieces(-delta, False), put_in(branch_ref), heads, in_order)
        accs[...] = jnp.zeros_like(accs)
        query_at = lax.broadcasted_iota(jnp.int32, (half, half), 1)
        key_at = lax.broadcasted_iota(jnp.int32, (half, half), 0)
        diff_ref[...] = key_at - query_at
        for i, group in enumerate(query_groups):
            span_ref[i] = document_start(group * half + query_at, doc_lengths) - key_at
        dk_acc, dv_acc, dcol_acc = (dhid_acc.at[:, pl.ds(i * LANES, LANES)] for i in range(3))

        def stage_copies(it):
            part, pair = lax.div(it, pairs), lax.rem(it, pairs)
            lanes = pl.ds(pl.multiple_of(pair * LANES, LANES), LANES)
            slot = lax.rem(it, 2)
            return [
                pltpu.make_async_copy(stage.at[slot, i], out.at[part, :, lanes], stage_sem.at[slot, i])
                for i, out in enumerate((dk_out, dv_out))
            ]

        def attend(it, carry):
            part, pair = lax.div(it, pairs), lax.rem(it, pairs)
            for copy in kv_copies(it):
                copy.wait()
            one, two = group_map[2 * part], group_map[2 * part + 1]
            forward = one < two
            key_groups = (jnp.minimum(one, two), jnp.maximum(one, two))
            lanes = pl.ds(pl.multiple_of(part * LANES, LANES), LANES)

            def ordered(ref, base, where):
                top = pl.ds(pl.multiple_of(base * rows, rows), half)
                bottom = pl.ds(pl.multiple_of(base * rows + half, half), half)
                return in_pack_order(forward, ref[top, where], ref[bottom, where])

            key_blocks = ordered(gate_all, pair, lanes)
            value_blocks = ordered(up_all, pair, lanes)
            aug_lanes = pl.ds(pl.multiple_of(narrow + part * LANES, LANES), LANES)
            aug_blocks = ordered(x_ref, 0, aug_lanes)
            dk_acc[...] = jnp.zeros_like(dk_acc)
            dv_acc[...] = jnp.zeros_like(dv_acc)

            @pl.when(pair == 0)
            def _():
                dcol_acc[...] = jnp.zeros_like(dcol_acc)

            for qi, ki in ((0, 0), (1, 0), (1, 1)):
                query_group, key_group = query_groups[qi], key_groups[ki]
                skipped = jnp.where(key_group < query_group, skip[query_group, key_group], 0)
                mask = (diff_ref[...] <= (query_group - key_group) * half) & (
                    span_ref[qi] <= key_group * half - (skipped == 1).astype(jnp.int32) * (1 << 30)
                )
                q_rows, k_rows = pl.ds(qi * half, half), pl.ds(ki * half, half)
                keys = jnp.concatenate([key_blocks[ki], aug_blocks[ki]], axis=1)
                values = jnp.concatenate([value_blocks[ki], aug_blocks[ki]], axis=1)
                for e in range(2):
                    h = 2 * pair + e
                    spot = pl.ds(pl.multiple_of(h * 2 * LANES, 2 * LANES), 2 * LANES)
                    queries, grads_out = dw_ref[q_rows, spot], branch_ref[q_rows, spot]
                    probs = jnp.where(mask, jnp.exp(contract_cols(keys, queries)), 0.0)
                    grads = (probs * contract_cols(values, grads_out)).astype(BF16)
                    dv_acc[k_rows, :] += dot(probs.astype(BF16), grads_out[:, :LANES])
                    both = dot(grads, queries)
                    dk_acc[k_rows, :] += both[:, :LANES]
                    dcol_acc[k_rows, :] += both[:, LANES:]
                    quarter = pl.ds(pl.multiple_of(lax.rem(h, 4) * 2 * LANES, 2 * LANES), 2 * LANES)
                    accs[lax.div(h, 4), q_rows, quarter] += contract_rows(grads, keys)

            @pl.when(it >= 2)
            def _():
                for copy in stage_copies(it - 2):
                    copy.wait()

            slot = lax.rem(it, 2)
            for i, acc in enumerate((dk_acc, dv_acc)):
                stage[slot, i] = jnp.concatenate(
                    in_pack_order(forward, acc[pl.ds(0, half), :], acc[pl.ds(half, half), :]), axis=0
                ).astype(BF16)
            for copy in stage_copies(it):
                copy.start()

            @pl.when(pair == pairs - 1)
            def _():
                columns = jnp.concatenate(
                    in_pack_order(forward, dcol_acc[pl.ds(0, half), :], dcol_acc[pl.ds(half, half), :]), axis=0
                )
                dcol_ref[part] = -(columns.T[:8])

            return carry

        done = 0
        while earlies.next < n - 1:
            lax.fori_loop(done, done + 2 * pairs, attend, 0)
            done += 2 * pairs
            backs.advance(1)
            earlies.advance(1)
        lax.fori_loop(done, n * pairs, attend, 0)
        for it in (n * pairs - 2, n * pairs - 1):
            for copy in stage_copies(it):
                copy.wait()

        lane = lax.broadcasted_iota(jnp.int32, (rows, LANES), 1)
        low = low_lanes(rows)
        sums = jnp.zeros((rows, LANES), F32)
        for pair in range(pairs):
            parts = []
            for h in (2 * pair, 2 * pair + 1):
                spot = pl.ds((h % 4) * 2 * LANES, 2 * LANES)
                value = jnp.concatenate(
                    in_pack_order(in_order, accs[h // 4, :half, spot], accs[h // 4, half:, spot]), axis=0
                )
                parts.append(value)
                sums = jnp.where(lane == 24 + h, value[:, LANES:], sums)
            dhid_acc[:, (3 + pair) * LANES : (4 + pair) * LANES] = jnp.where(
                low, parts[0][:, :LANES], parts[1][:, :LANES]
            )
        moves.start("dq", dhid_acc.at[:, pl.ds(3 * LANES, pairs * LANES)], dq_out)
        drow_ref[...] = pltpu.roll(sums, LANES - 24, 1).T[:8]

        moves.wait("dq")
    backs.end()
    moves.start("down", down_ref, down_out)
    earlies.end()
    moves.start("gate", gate_ref, gate_out)
    moves.start("up", up_ref, up_out)
    downs.sent()
    moves.wait()


def feed_forward(
    n, collective_id, heads, attended, gate_logit, out_weight, x, gain, dy, w_gate, w_up, w_down, attention=None
):
    rows, width = x.shape
    shard, hidden = w_gate.shape
    heads_width = attended.shape[1]
    own = width // 4
    half = rows // 2
    dma = pltpu.SemaphoreType.DMA
    vmem = pl.BlockSpec(memory_space=VMEM)
    anywhere = pl.BlockSpec(memory_space=pl.ANY)
    wide, narrow, deep = (rows, width), (rows, heads_width), (rows, hidden)
    by_shard = (n, rows, shard)
    weight = (shard, hidden)
    shapes = [
        (narrow, BF16),
        ((rows, own), F32),
        (weight, F32),
        (weight, F32),
        (weight, F32),
        (wide, F32),
        (narrow, BF16),
        (narrow, BF16),
        ((8, width), F32),
    ]
    kept = [1, 8]
    extra_specs, extra_scratch = [], []
    if attention is not None:
        assert heads // 2 * rows == n * shard and n * LANES == hidden and heads_width + hidden <= width
        shapes += [
            (by_shard, BF16),
            (narrow, F32),
            ((8, rows), F32),
            ((n, rows, heads_width), BF16),
            ((n, rows, heads_width), BF16),
            ((n, 8, rows), F32),
        ]
        kept += [11, 14]
        extra_specs = [smem()] * 3 + [anywhere] * 5
        extra_scratch = [
            VMEM((rows, LANES), F32),
            VMEM(by_shard, BF16),
            VMEM((half, half), jnp.int32),
            VMEM((2, half, half), jnp.int32),
            VMEM((2, 2, rows, LANES), BF16),
            dma((2, n * heads // 2)),
            dma((2, 2)),
        ]
    return pl.pallas_call(
        functools.partial(feed_kernel, n, heads, attention is not None),
        out_shape=[jax.ShapeDtypeStruct(*shape) for shape in shapes],
        in_specs=extra_specs + [anywhere] * 4 + [vmem] + [anywhere] * 4,
        out_specs=[vmem if i in kept else anywhere for i in range(len(shapes))],
        scratch_shapes=[
            VMEM(narrow, F32),
            VMEM(narrow, F32),
            VMEM(out_weight.shape, BF16),
            VMEM(wide, BF16),
            VMEM(wide, BF16),
            VMEM(narrow, BF16),
            VMEM(by_shard, BF16),
            VMEM(deep, BF16),
            VMEM(deep, BF16),
            VMEM(narrow, BF16),
            VMEM(narrow, BF16),
            *[VMEM((n * shard, hidden), BF16)] * 3,
            VMEM((2,) + deep, F32),
            VMEM(deep, F32),
            VMEM(deep, BF16),
            VMEM(wide, BF16),
            VMEM(wide, F32),
            VMEM(wide, BF16),
            VMEM(by_shard, BF16),
            *tp_buffers(rows, width),
            VMEM((rows // 2, width), BF16),
            VMEM((2, rows, own), BF16),
            VMEM((2, rows, own), BF16),
            VMEM((rows, own), BF16),
            VMEM((rows, own), BF16),
            *ring_scratch(n, shard, [hidden // 2] * 2),
            *ring_scratch(n, shard, [hidden] * 2),
            *[dma((4, n - 1))] * 4,
            *[dma((3, TP_CHUNKS))] * 4,
            *[dma((3,))] * 2,
            *[dma((2, 1, n - 1))] * 2,
            *[dma((2, 2, n - 1))] * 2,
            dma((27,)),
            *extra_scratch,
        ],
        compiler_params=pltpu.CompilerParams(
            collective_id=collective_id, has_side_effects=True, vmem_limit_bytes=VMEM_LIMIT
        ),
    )(*(attention or ()), attended, gate_logit, out_weight, x, gain, dy, w_gate, w_up, w_down)


def ring_scratch(n, height, widths):
    return [VMEM((n - 1, height, w), BF16) for w in widths] + [VMEM((height, w), BF16) for w in widths]


def head_means(value, heads):
    width = value.shape[1]
    size = width // heads
    left = lax.div(lax.broadcasted_iota(jnp.int32, (width, width), 0), size)
    right = lax.div(lax.broadcasted_iota(jnp.int32, (width, width), 1), size)
    member = (left == right).astype(BF16)
    high = value.astype(BF16)
    return (dot(high, member) + dot((value - high.astype(F32)).astype(BF16), member)) * (1.0 / size)


STAGED = (0, 1, 4, 5, 16, 11, 14, 17, 18, 19, 6, 12, 13, 20)


def finish_kernel(n, heads, gate_plan, attn_plan, *refs):
    operands, refs = list(refs[:24]), refs[24:]
    (q_out, k_out, v_out, g_out, o_out, small_out, input_out), refs = refs[:7], refs[7:]
    staged, refs = refs[: len(STAGED)], refs[len(STAGED) :]
    (
        pslot_r, pslot_l, gslot_r, gslot_l, gfirst_r, gfirst_l, aslot_r, aslot_l, afirst_r, afirst_l,
        dk_sum, dv_sum, dqr_ref, dkr_ref, dvl_ref, du_ref, sum_ref, t0, t1, t2, t3,
        off_ref, tot_ref, off_land, tot_land, small_ref, small_land,
        psend, precv, gsend, grecv, asend, arecv, osend, orecv, qsend, qrecv, xsend, xrecv, tsend, trecv, local,
    ) = refs
    moves = Moves(local)
    dk_hbm, dv_hbm = operands[:2]
    for target, index in zip(staged, STAGED):
        moves.start(index, operands[index], target)
        operands[index] = target
    (
        dk_ref, dv_ref, col_ref, row_ref, dq_ref, qr_ref, kr_ref, qgain_ref, kgain_ref, fz_ref, later_ref,
        wq_ref, wk_ref, wv_ref, wg_ref, wf_ref, dgl_ref, u_ref, dm_ref, gated_ref,
        x_ref, gain_ref, dmid_ref, gain_two_ref,
    ) = operands
    me, tp, place, sides = ring_setup(n)
    chip, core, sibling, across = tp_setup()
    rows, width = dq_ref.shape
    cols = x_ref.shape[1]
    shard = u_ref.shape[2]
    half = rows // 2
    head_dim = width // heads
    small_ref[...] = jnp.zeros_like(small_ref)
    greet(ctx_peers(me, tp, n) + [sibling, across])

    def pair_term(owner, tag):
        which, c0 = tag
        return (dk_ref, dv_ref)[which][owner, :, c0 : c0 + LANES].astype(F32)

    def pair_write(tag, value):
        which, c0 = tag
        (dk_sum, dv_sum)[which][:, c0 : c0 + LANES] = value

    pairs = ScatterRing(
        n, [[(w, (i, c)) for c, w in pieces(width, LANES)] for i in range(2)], pair_term,
        (pslot_r, pslot_l), None, pair_write, psend, precv, place, sides, tp,
        source=lambda target, side, window: (dk_hbm, dv_hbm)[side].at[target, :, window],
    )
    pairs.begin()
    off_ref[...] = col_ref[...]
    off_ref[me] += row_ref[...]
    tot_ref[...] = jnp.zeros_like(tot_ref)
    for i in range(n):
        for g in range(2):
            tot_ref[:, 2 * i + g : 2 * i + g + 1] = jnp.sum(
                off_ref[i, :, g * half : (g + 1) * half], axis=1, keepdims=True
            )
    exchange_start(n, me, tp, lambda peer: off_ref.at[peer], off_land, osend, orecv)
    exchange_start(n, me, tp, lambda peer: tot_ref, tot_land, qsend, qrecv)
    moves.start("off", off_ref.at[me], off_land.at[me])
    moves.start("tot", tot_ref, tot_land.at[me])

    def raw_grad(grad, raw, gain):
        inverse = lax.rsqrt(head_means(raw * raw, heads) + EPS)
        normal = raw * inverse
        back = grad * gain
        back = inverse * (back - normal * head_means(back * normal, heads))
        return back.astype(BF16), jnp.sum(grad * normal, axis=0, keepdims=True)

    def gain_rows(row, first):
        count = 2 * head_dim // n
        for i in range(n // 2):
            for h in range(heads):
                lane = h * head_dim + i * count
                small_ref[first + i, 2 + h : 3 + h, 0:count] = row[:, lane : lane + count]

    moves.wait(0, 1, 4, 5)
    pairs.advance(1)
    dqr, row = raw_grad(dq_ref[...], qr_ref[...], qgain_ref[...] * 0.125)
    dqr_ref[...] = dqr
    gain_rows(row * 0.125, 0)
    pairs.advance(1)
    moves.wait(16, 11, 14)
    span = cols // TP_CHUNKS
    for c in range(TP_CHUNKS):
        back = pl.ds(c * span, span)
        du_ref[:, back] = contract_cols(dqr_ref[...], wq_ref[back, :]) + contract_cols(dgl_ref[...], wg_ref[back, :])
    pairs.advance(n)
    moves.wait(17, 18, 19)

    def gate_term(owner, tag):
        left, right, c0, cw = tag
        grads = (gated_ref, dqr_ref, dgl_ref)[right]
        return contract_rows((dm_ref, u_ref)[left][owner], grads[:, c0 : c0 + cw])

    def gate_write(tag, value):
        _, right, c0, cw = tag
        (o_out, q_out, g_out)[right][:, c0 : c0 + cw] = value

    gates = ScatterRing(
        n, gate_plan, gate_term, (gslot_r, gslot_l), (gfirst_r, gfirst_l), gate_write, gsend, grecv, place, sides, tp,
    )
    gates.begin()
    pairs.end()

    moves.wait(6)
    dkr, row = raw_grad(dk_sum[...], kr_ref[...], kgain_ref[...])
    dkr_ref[...] = dkr
    gain_rows(row, n // 2)
    dvl_ref[...] = dv_sum[...].astype(BF16)

    def attn_term(owner, tag):
        c0, cw = tag[1], tag[2]
        return contract_rows(u_ref[owner], (dkr_ref, dvl_ref)[tag[0]][:, c0 : c0 + cw])

    def attn_write(tag, value):
        c0, cw = tag[1], tag[2]
        (k_out, v_out)[tag[0]][:, c0 : c0 + cw] = value

    attns = ScatterRing(
        n, attn_plan, attn_term, (aslot_r, aslot_l), (afirst_r, afirst_l), attn_write, asend, arecv, place, sides, tp,
    )
    attns.begin()
    gates.advance(1)
    moves.wait("off", "tot")
    exchange_wait(n, me, tp, lambda peer: off_ref.at[peer], off_land, osend, orecv)
    exchange_wait(n, me, tp, lambda peer: tot_ref, tot_land, qsend, qrecv)
    off_sum = ordered_sum(n, off_land)
    tot_sum = ordered_sum(n, tot_land)
    onward = (
        lax.broadcasted_iota(jnp.int32, (half, half), 0) >= lax.broadcasted_iota(jnp.int32, (half, half), 1)
    ).astype(F32)
    parts = []
    for g in range(2):
        suffix = jnp.dot(
            off_sum[:, g * half : (g + 1) * half], onward, precision=HIGHEST, preferred_element_type=F32
        )
        parts.append(suffix + jnp.sum(tot_sum * later_ref[g : g + 1, :], axis=1, keepdims=True))
    dfz = (jnp.concatenate(parts, axis=1) * jax.nn.sigmoid(-fz_ref[...])).astype(BF16).astype(F32)
    head = lax.broadcasted_iota(jnp.int32, dfz.shape, 0)
    dfz = jnp.where(head < heads, dfz, 0.0)
    bias = jnp.sum(dfz, axis=1, keepdims=True)
    dfz_cols = turn(dfz).astype(BF16)
    dfz_low = dfz.astype(BF16)
    for i in range(n):
        small_ref[i, 8:16, :shard] = dot(dfz_low, u_ref[i])
        small_ref[i, 8:16, 224:225] = bias
        small_ref[i, 1:2, :shard] = jnp.sum(gain_two_ref[:, i * shard : (i + 1) * shard], axis=0, keepdims=True)

    moves.wait(12, 13)
    forget = jnp.concatenate([wf_ref[...], jnp.zeros((LANES - 8, cols), F32)], axis=0).astype(BF16)
    for c in range(TP_CHUNKS):
        back = pl.ds(c * span, span)
        du_ref[:, back] += (
            contract_cols(dkr_ref[...], wk_ref[back, :])
            + contract_cols(dvl_ref[...], wv_ref[back, :])
            + dot(dfz_cols, forget[:, c * span : (c + 1) * span])
        )

    def part(which, c):
        return du_ref[pl.ds(pl.multiple_of(which * half, half), half), c * span : (c + 1) * span]

    total = TpSum(part, sum_ref, (t0, t1, t2, t3), tsend, trecv, core, sibling, across)
    total.first()
    attns.advance(1)
    total.second()
    moves.start("dmid", dmid_ref, du_ref)
    gates.advance(1)
    attns.advance(1)
    gates.advance(1)
    total.third()
    attns.advance(1)
    total.fourth()
    moves.wait("dmid", 20)
    size = 64

    def input_rows(i, acc):
        here = pl.ds(pl.multiple_of(i * size, size), size)
        value = x_ref[here, :].astype(F32)
        inverse = lax.rsqrt(jnp.mean(value * value, axis=-1, keepdims=True) + EPS)
        normal = value * inverse
        grad = sum_ref[here, :].astype(F32)
        back = grad * gain_ref[...]
        back = inverse * (back - normal * jnp.mean(back * normal, axis=-1, keepdims=True))
        du_ref[here, :] += back
        return acc + jnp.sum((grad * normal).reshape(size // 8, 8, cols), axis=0)

    gains = lax.fori_loop(0, rows // size, input_rows, jnp.zeros((8, cols), F32))
    moves.start("input", du_ref, input_out)
    for i in range(n):
        small_ref[i, 0:1, :shard] = jnp.sum(gains[:, i * shard : (i + 1) * shard], axis=0, keepdims=True)
    exchange_start(n, me, tp, lambda peer: small_ref.at[peer], small_land, xsend, xrecv)
    moves.start("small", small_ref.at[me], small_land.at[me])
    while gates.next < n - 1:
        gates.advance(1)
        attns.advance(1)
    gates.end()
    attns.end()
    moves.wait("small")
    exchange_wait(n, me, tp, lambda peer: small_ref.at[peer], small_land, xsend, xrecv)
    small_out[...] = ordered_sum(n, small_land)
    pairs.sent()
    moves.wait()


def finish_backward(n, collective_id, heads, gate_plan, attn_plan, *operands):
    dq, u, x = operands[4], operands[17], operands[20]
    rows, width = dq.shape
    cols = x.shape[1]
    shard = u.shape[2]
    dma = pltpu.SemaphoreType.DMA
    vmem = pl.BlockSpec(memory_space=VMEM)
    anywhere = pl.BlockSpec(memory_space=pl.ANY)
    outside = STAGED + (22,)
    gate_widths = [sum(w for w, _ in side) for side in gate_plan]
    attn_widths = [sum(w for w, _ in side) for side in attn_plan]

    def ring_semaphores(plan):
        return [dma((2, max(len(side) for side in plan), n - 1))] * 2

    shapes = [(shard, width)] * 5 + [(16, 256), (rows, cols)]
    return pl.pallas_call(
        functools.partial(finish_kernel, n, heads, gate_plan, attn_plan),
        out_shape=[jax.ShapeDtypeStruct(shape, F32) for shape in shapes],
        in_specs=[anywhere if i in outside else vmem for i in range(len(operands))],
        out_specs=[vmem] * 6 + [anywhere],
        scratch_shapes=[
            *[VMEM(operands[i].shape, operands[i].dtype) for i in STAGED],
            *[VMEM((n - 1, rows, width), BF16)] * 2,
            *ring_scratch(n, shard, gate_widths),
            *ring_scratch(n, shard, attn_widths),
            VMEM((rows, width), F32),
            VMEM((rows, width), F32),
            *[VMEM((rows, width), BF16)] * 3,
            VMEM((rows, cols), F32),
            VMEM((rows, cols), BF16),
            *tp_buffers(rows, cols),
            VMEM((n, 8, rows), F32),
            VMEM((8, LANES), F32),
            VMEM((n, 8, rows), F32),
            VMEM((n, 8, LANES), F32),
            VMEM((n, 16, 256), F32),
            VMEM((n, 16, 256), F32),
            *[dma((2, len(pieces(width, LANES)), n - 1))] * 2,
            *ring_semaphores(gate_plan),
            *ring_semaphores(attn_plan),
            *[dma((n - 1,))] * 6,
            *[dma((3, TP_CHUNKS))] * 2,
            dma((len(STAGED) + 5,)),
        ],
        compiler_params=pltpu.CompilerParams(
            collective_id=collective_id, has_side_effects=True, vmem_limit_bytes=VMEM_LIMIT
        ),
    )(*operands)


LANES = 128


def block_state(group_map, doc_lengths, skip, query_group, key_group, rows, docs):
    first_q = query_group * rows
    last_q = first_q + rows - 1
    first_k = key_group * rows
    last_k = first_k + rows - 1
    zero = jnp.int32(0)
    doc_qf, doc_ql, doc_kf, doc_kl, end = zero, zero, zero, zero, zero
    for d in range(docs):
        end = end + doc_lengths[d]
        doc_qf += (first_q >= end).astype(jnp.int32)
        doc_ql += (last_q >= end).astype(jnp.int32)
        doc_kf += (first_k >= end).astype(jnp.int32)
        doc_kl += (last_k >= end).astype(jnp.int32)
    earlier = key_group < query_group
    same = key_group == query_group
    kept = skip[query_group, key_group] != 1
    active = jnp.logical_or(same, earlier & kept & (doc_kl == doc_qf))
    full = earlier & (doc_kf == doc_ql)
    return active, full


def block_mask(doc_lengths, query_group, key_group, rows, docs, query_dim):
    shape = (rows, rows)
    pos_q = query_group * rows + lax.broadcasted_iota(jnp.int32, shape, query_dim)
    pos_k = key_group * rows + lax.broadcasted_iota(jnp.int32, shape, 1 - query_dim)
    start = jnp.zeros(shape, jnp.int32)
    end = jnp.int32(0)
    for d in range(docs):
        end = end + doc_lengths[d]
        start = jnp.where(pos_q >= end, end, start)
    return (pos_k <= pos_q) & (pos_k >= start)


def document_start(position, doc_lengths):
    start, end = jnp.zeros_like(position), jnp.int32(0)
    for d in range(doc_lengths.shape[0]):
        end = end + doc_lengths[d]
        start = jnp.where(position >= end, end, start)
    return start


def in_pack_order(forward, one, two):
    return jnp.where(forward, one, two), jnp.where(forward, two, one)


def low_lanes(rows):
    return lax.broadcasted_iota(jnp.int32, (rows, LANES), 1) < LANES // 2


def three_pieces(value):
    high = value.astype(BF16).astype(F32)
    rest = value - high
    middle = rest.astype(BF16).astype(F32)
    return high, middle, rest - middle


def turn(value):
    rows = value.shape[1]
    return jnp.concatenate([value, jnp.zeros((LANES - 8, rows), F32)], axis=0).T


def row_pieces(term, with_ones):
    lane = lax.broadcasted_iota(jnp.int32, term.shape, 1)
    term = jnp.where(lane < 8, term, 0.0)
    high, middle, low = three_pieces(term)
    result = pltpu.roll(high, 24, 1) + pltpu.roll(middle, 32, 1) + pltpu.roll(low, 40, 1)
    if with_ones:
        result = jnp.where(lane < 24, 1.0, result)
    return result


def key_pieces(offsets):
    rows = offsets.shape[1]
    high, middle, low = three_pieces(offsets)
    stack = jnp.concatenate(
        [-high, -middle, -low, jnp.ones((24, rows), F32), jnp.zeros((LANES - 48, rows), F32)], axis=0
    )
    return stack.T.astype(BF16)


def spread_heads(wide_ref, common, put, heads, forward=None):
    rows = wide_ref.shape[0]
    low = low_lanes(rows)
    lane = lax.broadcasted_iota(jnp.int32, (rows, LANES), 1)

    def ordered(value):
        if forward is None:
            return value
        return jnp.concatenate(in_pack_order(forward, value[: rows // 2], value[rows // 2 :]), axis=0)

    common = ordered(common)
    for h in range(heads):
        pair = h // 2
        block = ordered(wide_ref[:, pair * LANES : (pair + 1) * LANES])
        keep = low if h % 2 == 0 else jnp.logical_not(low)
        put(
            h,
            jnp.where(keep, block, jnp.zeros_like(block)),
            jnp.where(lax.rem(lane, 8) == h, common, 0.0).astype(BF16),
        )


def put_rows(cat_ref):
    def put(h, value, extra):
        cat_ref[h, :, :LANES] = value
        cat_ref[h, :, LANES:] = extra

    return put


def smem():
    return pl.BlockSpec(memory_space=pltpu.SMEM)


def whole(shape):
    return pl.BlockSpec(shape, lambda i: (0,) * len(shape))


def head_sums(value, heads):
    width = value.shape[1]
    feature = lax.broadcasted_iota(jnp.int32, (width, LANES), 0)
    lane = lax.broadcasted_iota(jnp.int32, (width, LANES), 1)
    member = (lax.div(feature, width // heads) == lane).astype(BF16)
    high = value.astype(BF16)
    return dot(high, member) + dot((value - high.astype(F32)).astype(BF16), member)


def backward_kernel(
    heads, rows, docs, me, group_map, doc_lengths, skip, q_ref, d_ref, out_ref, term_ref, k_ref, v_ref, kaug_ref,
    dq_ref, drow_ref, dk_ref, dv_ref, dcol_ref, acc_ref, qcat_ref, dcat_ref, dk_acc, dv_acc, dcol_acc,
):
    step = pl.program_id(0)

    @pl.when(step == 0)
    def _():
        acc_ref[...] = jnp.zeros_like(acc_ref)
        spread_heads(q_ref, row_pieces(term_ref[...], True), put_rows(qcat_ref), heads)
        delta = head_sums(d_ref[...].astype(F32) * out_ref[...], heads)
        spread_heads(d_ref, row_pieces(-delta, False), put_rows(dcat_ref), heads)

    dk_acc[...] = jnp.zeros_like(dk_acc)
    dv_acc[...] = jnp.zeros_like(dv_acc)
    dcol_acc[...] = jnp.zeros_like(dcol_acc)

    def tile(qi, ki, mask):
        q_rows = pl.ds(qi * rows, rows)
        k_rows = pl.ds(ki * rows, rows)
        aug = kaug_ref[k_rows, :]
        for pair in range(heads // 2):
            lanes = pl.ds(pair * LANES, LANES)
            keys = jnp.concatenate([k_ref[pair, k_rows, :], aug], axis=1)
            values = jnp.concatenate([v_ref[pair, k_rows, :], aug], axis=1)
            for h in (2 * pair, 2 * pair + 1):
                probs = jnp.exp(contract_cols(keys, qcat_ref[h, q_rows, :]))
                if mask is not None:
                    probs = jnp.where(mask, probs, 0.0)
                grads = (probs * contract_cols(values, dcat_ref[h, q_rows, :])).astype(BF16)
                dv_acc[k_rows, lanes] += dot(probs.astype(BF16), dcat_ref[h, q_rows, :LANES])
                both = dot(grads, qcat_ref[h, q_rows, :])
                dk_acc[k_rows, lanes] += both[:, :LANES]
                dcol_acc[k_rows, :] += both[:, LANES:]
                acc_ref[h, q_rows, :] += contract_rows(grads, keys)

    for ki in range(2):
        key_group = group_map[2 * step + ki]
        for qi in range(2):
            query_group = group_map[2 * me[0] + qi]
            active, full = block_state(group_map, doc_lengths, skip, query_group, key_group, rows, docs)

            @pl.when(active & full)
            def _(qi=qi, ki=ki):
                tile(qi, ki, None)

            @pl.when(active & jnp.logical_not(full))
            def _(qi=qi, ki=ki, query_group=query_group, key_group=key_group):
                tile(qi, ki, block_mask(doc_lengths, query_group, key_group, rows, docs, 1))

    dk_ref[0] = dk_acc[...].astype(BF16)
    dv_ref[0] = dv_acc[...].astype(BF16)
    dcol_ref[0] = -(dcol_acc[...].T[:8])

    @pl.when(step == pl.num_programs(0) - 1)
    def _():
        total_rows = dq_ref.shape[0]
        low = low_lanes(total_rows)
        lane = lax.broadcasted_iota(jnp.int32, (total_rows, LANES), 1)
        sums = jnp.zeros((total_rows, LANES), F32)
        for pair in range(heads // 2):
            a, b = 2 * pair, 2 * pair + 1
            dq_ref[:, pair * LANES : (pair + 1) * LANES] = jnp.where(
                low, acc_ref[a, :, :LANES], acc_ref[b, :, :LANES]
            )
            sums = jnp.where(
                lane == 24 + a, acc_ref[a, :, LANES:], jnp.where(lane == 24 + b, acc_ref[b, :, LANES:], sums)
            )
        drow_ref[...] = pltpu.roll(sums, LANES - 24, 1).T[:8]


def backward_attention(me, group_map, doc_lengths, skip, queries, grads, attended, term, keys, values, key_aug, heads):
    total = keys.shape[1]
    own, width = queries.shape
    rows = own // 2
    n = total // own
    docs = doc_lengths.shape[0]
    return pl.pallas_call(
        functools.partial(backward_kernel, heads, rows, docs),
        grid=(n,),
        out_shape=[
            jax.ShapeDtypeStruct((own, width), F32),
            jax.ShapeDtypeStruct((8, own), F32),
            jax.ShapeDtypeStruct((n, own, width), BF16),
            jax.ShapeDtypeStruct((n, own, width), BF16),
            jax.ShapeDtypeStruct((n, 8, own), F32),
        ],
        in_specs=[smem(), smem(), smem(), smem()]
        + [
            whole((own, width)),
            whole((own, width)),
            whole((own, width)),
            whole((own, LANES)),
            pl.BlockSpec((heads // 2, own, LANES), lambda i: (0, i, 0)),
            pl.BlockSpec((heads // 2, own, LANES), lambda i: (0, i, 0)),
            pl.BlockSpec((own, LANES), lambda i: (i, 0)),
        ],
        out_specs=[
            whole((own, width)),
            whole((8, own)),
            pl.BlockSpec((1, own, width), lambda i: (i, 0, 0)),
            pl.BlockSpec((1, own, width), lambda i: (i, 0, 0)),
            pl.BlockSpec((1, 8, own), lambda i: (i, 0, 0)),
        ],
        scratch_shapes=[
            VMEM((heads, own, 2 * LANES), F32),
            VMEM((heads, own, 2 * LANES), BF16),
            VMEM((heads, own, 2 * LANES), BF16),
            VMEM((own, width), F32),
            VMEM((own, width), F32),
            VMEM((own, LANES), F32),
        ],
        compiler_params=pltpu.CompilerParams(vmem_limit_bytes=VMEM_LIMIT),
        cost_estimate=pl.CostEstimate(
            flops=own * total * width * 10, bytes_accessed=total * width * 8, transcendentals=own * total * heads
        ),
    )(me, group_map, doc_lengths, skip, queries, grads, attended, term, keys, values, key_aug)


def on_device(
    hidden_in,
    norm_one,
    w_query,
    w_key,
    w_value,
    w_gate_out,
    w_forget,
    forget_bias,
    head_gains,
    w_output,
    norm_two,
    w_gate,
    w_up,
    w_down,
    out_grad,
    doc_lengths,
    group_map,
    skip_list,
):
    device_ctx = lax.axis_index("ctx")
    device_tp = lax.axis_index("tp")
    n = lax.axis_size("ctx")
    row_count, model_width = hidden_in.shape
    group_rows = row_count // 2
    heads = forget_bias.shape[0]
    shard = norm_one.shape[0]
    gain_rows = head_gains.shape[0]
    head_dim = gain_rows * n // 2
    width = heads * head_dim
    hidden_width = w_gate.shape[1]

    slots = 2 * n
    earlier = jnp.pad(
        (group_map[:, None] < group_map[None, :]).astype(F32), ((0, LANES - slots), (0, LANES - slots))
    )

    def lanes_of(value, first_rows, last_rows):
        return jnp.pad(value, ((first_rows, last_rows), (0, 256 - value.shape[1])))

    small = jnp.concatenate(
        [
            lanes_of(jnp.stack([norm_one, norm_two]), 0, 0),
            lanes_of(head_gains.T, 0, 6 - heads),
            lanes_of(w_forget.T, 0, 8 - heads),
        ],
        axis=0,
    )
    (
        query_weight,
        key_weight,
        value_weight,
        gate_out_weight,
        output_weight,
        normed_shards,
        query_rows,
        query_raw,
        key_raw,
        gate_logit,
        forget_logit,
        keys_all,
        values_all,
        key_aug,
        attended_flat,
        row_term,
        gain_one,
        gain_two,
        query_gain,
        key_gain,
        forget_weight,
    ) = start_forward(
        n, 1, group_map, doc_lengths, skip_list, earlier, hidden_in, small, forget_bias, [w_query, w_key, w_value, w_gate_out], w_output
    )
    half = width // 256 * 128
    me_one = device_ctx.astype(jnp.int32).reshape(1)
    fused = n <= 8
    (
        gated,
        layer_out,
        down_share,
        gate_share,
        up_share,
        grad_middle,
        grad_attended,
        grad_gate_logit,
        gain_two_parts,
        *attention_grads,
    ) = feed_forward(
        n,
        3,
        heads,
        attended_flat,
        gate_logit,
        output_weight,
        hidden_in,
        gain_two,
        out_grad,
        w_gate,
        w_up,
        w_down,
        (group_map, doc_lengths, skip_list, query_rows, row_term, keys_all, values_all, key_aug) if fused else None,
    )
    if not fused:
        grad_branch = grad_middle.astype(BF16).reshape(row_count, n, shard).transpose(1, 0, 2)
        attention_grads = grad_branch, *backward_attention(
            me_one,
            group_map,
            doc_lengths,
            skip_list,
            query_rows,
            grad_attended,
            attended_flat,
            row_term,
            keys_all,
            values_all,
            key_aug,
            heads,
        )
    grad_branch, grad_query, row_sums, key_part, value_part, column_sums = attention_grads

    gate_plan = [
        [(width, (1, 1 + i, 0, width)), (w, (0, 0, c, w))] for i, (c, w) in enumerate([(0, half), (half, width - half)])
    ]
    attn_plan = [[(half, (i, 0, half)), (width - half, (i, half, width - half))] for i in (0, 1)]
    own_groups = lax.dynamic_slice_in_dim(group_map, device_ctx * 2, 2, 0)
    later = (group_map[None, :] > own_groups[:, None]).astype(F32)
    if fused:
        (
            query_share,
            key_share,
            value_share,
            gate_out_share,
            output_share,
            small_share,
            input_grad,
        ) = finish_backward(
            n,
            7,
            heads,
            gate_plan,
            attn_plan,
            key_part,
            value_part,
            column_sums,
            row_sums,
            grad_query,
            query_raw,
            key_raw,
            query_gain,
            key_gain,
            forget_logit,
            jnp.pad(later, ((0, 6), (0, LANES - slots))),
            query_weight,
            key_weight,
            value_weight,
            gate_out_weight,
            forget_weight,
            grad_gate_logit,
            normed_shards,
            grad_branch,
            gated,
            hidden_in,
            gain_one,
            grad_middle,
            gain_two_parts,
        )
    else:
        query_gain, key_gain = (gain.reshape(heads, head_dim) for gain in (query_gain, key_gain))
        query_raw, key_raw = (raw.reshape(row_count, heads, head_dim) for raw in (query_raw, key_raw))
        query_norm, key_norm = rms_scale(query_raw), rms_scale(key_raw)
        forget_logit = forget_logit[:heads].T
        forget_weight = forget_weight[:heads].astype(BF16)
        normed_one = normed_shards.transpose(1, 0, 2).reshape(row_count, model_width)
        place = jnp.arange(group_rows, dtype=jnp.int32)
        upper = (place[:, None] <= place[None, :]).astype(F32)
        grad_key, grad_value, off_sum, tot_sum = pair_scatter(n, 7, key_part, value_part, column_sums, row_sums)
        after = contract_cols_exact(tot_sum[:heads, :slots], later)
        suffix = lax.dot_general(
            off_sum[:heads].reshape(heads, 2, group_rows), upper, (((2,), (1,)), ((), ())), precision=HIGHEST
        )
        grad_log_forget = (suffix + after[:, :, None]).reshape(heads, row_count).T
        grad_key3 = grad_key.reshape(row_count, heads, head_dim)
        grad_query3 = grad_query.reshape(row_count, heads, head_dim)
        key_raw_grad = rms_back(grad_key3 * key_gain, key_raw).astype(BF16).reshape(row_count, width)
        query_raw_grad = (
            rms_back(grad_query3 * query_gain * 0.125, query_raw).astype(BF16).reshape(row_count, width)
        )
        value_low = grad_value.astype(BF16)
        query_gain_grad = jnp.sum(grad_query3 * query_norm * 0.125, axis=0)
        key_gain_grad = jnp.sum(grad_key3 * key_norm, axis=0)
        head_gain_grad = jnp.concatenate([query_gain_grad, key_gain_grad], axis=1)
        grad_forget_logit = (grad_log_forget * jax.nn.sigmoid(-forget_logit)).astype(BF16)
        bias_part = jnp.sum(grad_forget_logit.astype(F32), axis=0)
        normed_one_part = (
            contract_cols(query_raw_grad, query_weight)
            + contract_cols(key_raw_grad, key_weight)
            + contract_cols(value_low, value_weight)
            + contract_cols(grad_gate_logit, gate_out_weight)
            + dot(grad_forget_logit, forget_weight)
        )
        forget_grad = contract_rows(grad_forget_logit, normed_one)

        def wide(value):
            return jnp.pad(value, ((0, 0), (0, 0), (0, 256 - value.shape[2])))

        forget_rows = wide(forget_grad.reshape(heads, n, shard).transpose(1, 0, 2))
        forget_rows = forget_rows.at[:, :, 224].set(bias_part[None, :])
        small_grad = jnp.concatenate(
            [
                jnp.zeros((n, 1, 256), F32),
                wide(jnp.sum(gain_two_parts, axis=0).reshape(n, 1, shard)),
                wide(head_gain_grad.reshape(heads, n, gain_rows).transpose(1, 0, 2)),
                jnp.pad(forget_rows, ((0, 0), (0, 8 - heads), (0, 0))),
            ],
            axis=1,
        )
        lefts, rights = (1, 0), (4, 0, 3)
        plan = [
            [(w, (0, 1 + i, c0, cw)) for w, (i, c0, cw) in attn]
            + [(w, (lefts[left], rights[right], c0, cw)) for w, (left, right, c0, cw) in gate]
            for attn, gate in zip(attn_plan, gate_plan)
        ]
        (
            query_share,
            key_share,
            value_share,
            gate_out_share,
            output_share,
            small_share,
            input_grad,
        ) = weight_scatter(
            n,
            8,
            plan,
            [normed_shards, grad_branch],
            [query_raw_grad, key_raw_grad, value_low, grad_gate_logit, gated],
            small_grad,
            normed_one_part,
            hidden_in,
            gain_one,
            grad_middle,
        )
    return (
        layer_out,
        input_grad,
        small_share[0, :shard],
        query_share,
        key_share,
        value_share,
        gate_out_share,
        small_share[8 : 8 + heads, :shard].T,
        small_share[8 : 8 + heads, 224],
        small_share[2 : 2 + heads, :gain_rows].T,
        output_share,
        small_share[1, :shard],
        gate_share,
        up_share,
        down_share,
    )


def solution(mesh):
    split = P("ctx", "tp")
    in_specs = (
        P("ctx", None),
        P("ctx"),
        split,
        split,
        split,
        split,
        split,
        P("tp"),
        split,
        split,
        P("ctx"),
        split,
        split,
        split,
        P("ctx", None),
        P(),
        P(),
        P(),
    )
    out_specs = (
        split,
        P("ctx", None),
        P("ctx"),
        split,
        split,
        split,
        split,
        split,
        P("tp"),
        split,
        split,
        P("ctx"),
        split,
        split,
        split,
    )
    return jax.shard_map(on_device, mesh=mesh, in_specs=in_specs, out_specs=out_specs, check_vma=False)
```

time: 2000 us -> 516 us (0.26)
  waiting for transfers between devices: 1300 us -> 0 us
  Pallas kernels: 0 us -> 483 us
  matrix products: 252 us -> 0 us
  blocking collectives: 180 us -> 0 us
  other arithmetic: 121 us -> 3.44 us
  local copies, waits for them, and re-layouts: 108 us -> 19 us
    reduce_scatter x10 -> x0, waiting for transfers between devices: 638 us -> none  [the longest x1 112 us: on_device(): lax.psum_scatter(value_all, 'ctx', scatter_dimension=0, tiled=True)]
    pallas_call x0 -> x3, Pallas kernels: none -> 483 us  [the longest x1 211 us: feed_forward(): pl.pallas_call(functools.partial(feed_kernel, n, heads, attention is not...]
    all_gather x10 -> x0, waiting for transfers between devices: 277 us -> none  [the longest x1 59.5 us: on_device(): lax.all_gather(key_flat, 'ctx', axis=0, tiled=True)]
    dot_general x57 -> x0, matrix products: 252 us -> none  [the longest x4 43.4 us: absorb_compute(): jnp.einsum('qhk,khe->qhe', weights, value_piece.reshape(block_rows, heads...]
    unnamed x31 -> x0, waiting for transfers between devices: 217 us -> none
    psum x3 -> x0, waiting for transfers between devices: 170 us -> none  [the longest x1 64.5 us: on_device(): branch = lax.psum(contract_cols(gated, output_weight), 'tp')]
    all_gather x4 -> x0, blocking collectives: 119 us -> none  [the longest x1 31.7 us: on_device(): offsets_grads_all = lax.all_gather(grad_offsets, 'ctx', axis=0, tiled=True)]
    unnamed x2 -> x0, blocking collectives: 60.7 us -> none
  transfers between devices with their start and end apart: 27 -> 0, of which waited for: 24 -> 0; matrix products, arithmetic and copies ran while one was open for 14% -> 0% of each run, Pallas kernels for 0% -> 0%
where the time goes in v1:
time: 516 us; the launch traced here: 507 us
  Pallas kernels  483 us (94%)
  local copies, waits for them, and re-layouts  19 us (4%)
    pallas_call x1, Pallas kernels, feed_forward(): pl.pallas_call(functools.partial(feed_kernel, n, heads, attention is not...  211 us
    pallas_call x1, Pallas kernels, start_forward(): pl.pallas_call(functools.partial(start_kernel, n, heads), out_shape=[jax....  138 us
    pallas_call x1, Pallas kernels, finish_backward(): pl.pallas_call(functools.partial(finish_kernel, n, heads, gate_plan, attn...  133 us
    unnamed x30, local copies, waits for them, and re-layouts  11 us

profile of v1, /device:TPU:0, one launch (start us, length us, event | category | flops | bytes accessed | tf_op | source)
XLA Modules:
  0.0 506.9 jit_solution(2881063551711306902)
XLA Ops:
  0.6 0.8 broadcast_compare_fusion
  1.4 0.6 pad_convert_fusion.earlier_ref
  2.1 0.7 stack.10
  2.7 0.7 stack.9
  3.4 1.3 fusion.4.small_in
  4.7 0.7 pad.33
  5.4 0.7 broadcast_in_dim.2.bias_ref
  6.0 138.4 %shard_map.289 = (bf16[1536,384]{1,0:T(8,128)(2,1)}, bf16[1536,384]{1,0:T(8,128)(2,1)}, bf16[1536,384]{1,0:T(8,128)(2,1)}, bf16[1536,384]{1,0:T(8,128)(2,1)}, bf...) custom-call(s32[16]{0:T(128)} %refs_0_.1, ...), custom_call_target="tpu_custom_call" | custom-call | tf_op jit(solution)/shard_map/pallas_call | solution.py:458
  144.5 211.5 %shard_map.290 = (bf16[512,384]{1,0:T(8,128)(2,1)}, f32[512,384]{1,0:T(8,128)}, f32[192,1024]{1,0:T(8,128)}, f32[192,1024]{1,0:T(8,128)}, f32[192,1024]{1,0:T(8,...) custom-call(s32[16]{0:T(128)} %refs_0_.1, ...), custom_call_target="tpu_custom_call" | custom-call | tf_op jit(solution)/shard_map/pallas_call | solution.py:1360
  356.8 133.4 %shard_map.291 = (f32[192,384]{1,0:T(8,128)}, f32[192,384]{1,0:T(8,128)}, f32[192,384]{1,0:T(8,128)}, f32[192,384]{1,0:T(8,128)}, f32[192,384]{1,0:T(8,128)}, /*index=5*/f32[16,256]{1,0:T(8,128)}, f32[512,1536]{1,0:T(8,128)}) custom-call(bf16[8,512,384]{2,1,0:T(8,128)(2,1)} %get-tuple-element.67.refs_0_, bf16[8,512,384]{2,1,0:T(8,128)(2,1)} %get-tuple-element.68.refs_1_, ...), custom_call_target="tpu_custom_call" | custom-call | tf_op jit(solution)/shard_map/pallas_call | solution.py:1640
  490.2 1.3 slice_bitcast_fusion
  491.5 1.3 slice_bitcast_fusion.1
  492.8 1.3 fusion.8
  494.1 1.4 slice_reduce_fusion
  495.5 0.9 copy.43
  496.4 3.9 copy.44
  500.2 0.7 copy.45
  500.9 0.7 copy.46
  501.7 0.7 copy.47
  502.4 0.7 copy.48
  503.1 0.7 copy.49
  503.8 0.9 copy.50
  504.7 0.9 copy.51
  505.6 0.9 copy.52
  (24 shorter events, 0.8 us)
Async XLA Ops:
  144.5 211.5 %copy-start.9 = (s32[16]{0:T(128)S(1)}, s32[16]{0:T(128)}, u32[]{:S(2)}) copy-start(s32[16]{0:T(128)} %refs_0_.1) | copy-start | bytes 196
  356.8 138.7 %copy-start.3 = (f32[512,384]{1,0:T(8,128)S(1)}, f32[512,384]{1,0:T(8,128)}, u32[]{:S(2)}) copy-start(f32[512,384]{1,0:T(8,128)} %get-tuple-element.116) | copy-start | bytes 2359300
  496.4 3.9 copy-start.8
  496.4 4.6 copy-start.7
  496.4 5.3 %copy-start.6 = (f32[192,384]{1,0:T(8,128)S(1)}, f32[192,384]{1,0:T(8,128)}, u32[]{:S(2)}) copy-start(f32[192,384]{1,0:T(8,128)} %get-tuple-element.121) | copy-start | bytes 884740
  496.4 6.0 %copy-start.5 = (f32[192,384]{1,0:T(8,128)S(1)}, f32[192,384]{1,0:T(8,128)}, u32[]{:S(2)}) copy-start(f32[192,384]{1,0:T(8,128)} %get-tuple-element.122) | copy-start | bytes 884740
  500.2 2.9 copy-start.4
  500.2 3.6 copy-start.2
  500.9 3.8 copy-start.1
  502.4 3.2 copy-start

commit v2 on v1

--- a/solution.py
+++ b/solution.py
@@ -11,7 +11,7 @@
 HIGHEST = lax.Precision.HIGHEST
 MESH = pl.DeviceIdType.MESH
 VMEM = pltpu.VMEM
-VMEM_LIMIT = 60 * 1024 * 1024
+VMEM_LIMIT = 62 * 1024 * 1024
 F32 = jnp.float32
 BF16 = jnp.bfloat16
 
@@ -362,19 +362,20 @@
         blocks = []
         for ref in (k_all.at[pair], v_all.at[pair], aug_ref):
             blocks.append(in_pack_order(forward, ref[top, :], ref[bottom, :]))
-        for qi, ki in ((0, 0), (1, 0), (1, 1)):
-            query_group, key_group = query_groups[qi], key_groups[ki]
-            skipped = jnp.where(key_group < query_group, skip[query_group, key_group], 0)
-            mask = (diff_ref[...] <= (query_group - key_group) * half) & (
-                span_ref[qi] <= key_group * half - (skipped == 1).astype(jnp.int32) * (1 << 30)
-            )
-            here = pl.ds(qi * half, half)
-            keys = jnp.concatenate([blocks[0][ki], blocks[2][ki]], axis=1)
-            values = jnp.concatenate([blocks[1][ki], ones], axis=1)
-            for e in range(2):
-                h = 2 * pair + e
-                weights = jnp.where(mask, jnp.exp(contract_cols(cat_ref[h, here, :], keys)), 0.0)
-                acc_ref[h, here, :] += dot(weights.astype(BF16), values)
+        masks = block_masks(diff_ref, span_ref, skip, query_groups, key_groups, half)
+        keys = [jnp.concatenate([blocks[0][ki], blocks[2][ki]], axis=1) for ki in range(2)]
+        values = [jnp.concatenate([blocks[1][ki], ones], axis=1) for ki in range(2)]
+        both_values = jnp.concatenate(values, axis=0)
+        for e in range(2):
+            h = 2 * pair + e
+            queries = cat_ref[h]
+            early = contract_cols(queries, keys[0])
+            weights = [
+                jnp.where(mask, jnp.exp(score), 0.0).astype(BF16)
+                for mask, score in zip(masks, (early[:half], early[half:], contract_cols(queries[half:], keys[1])))
+            ]
+            acc_ref[h, :half, :] += dot(weights[0], values[0])
+            acc_ref[h, half:, :] += dot(jnp.concatenate(weights[1:], axis=1), both_values)
 
     def attend_all(count, back):
         def body(i, carry):
@@ -899,11 +900,11 @@
     if attention:
         (dm_out, dq_out, drow_ref, dk_out, dv_out, dcol_ref), refs = refs[:6], refs[6:]
     (
-        att_ref, gl_ref, outw_ref, x_ref, grad_ref, gated_ref, normed_ref, dgt_ref, dup_ref, do_ref, dgl_ref,
+        att_ref, gl_ref, outw_ref, x_ref, gated_ref, normed_ref, dgt_ref, dup_ref, do_ref, dgl_ref,
         gate_all, up_all, down_all, accs, dhid_acc, hid_ref, branch_ref, mid_ref, dw_ref, dy_ref,
         a0, a1, a2, a3, b3, s0, s1, s2, s3, dslot_r, dslot_l, dfirst_r, dfirst_l, eslot_r, eslot_l, efirst_r, efirst_l,
         gsend, grecv, hsend, hrecv, asend, arecv, bsend, brecv, ssend, srecv, dsend, drecv, esend, erecv, local,
-    ), refs = refs[:53], refs[53:]
+    ), refs = refs[:52], refs[52:]
     if attention:
         term_ref, dm_ref, diff_ref, span_ref, stage, kv_sem, stage_sem = refs
     gate_acc, up_acc = accs.at[0], accs.at[1]
@@ -911,7 +912,7 @@
     chip, core, sibling, across = tp_setup()
     moves = Moves(local)
     for name, source, target in (
-        ("att", att_in, att_ref), ("gl", gl_in, gl_ref), ("outw", outw_in, outw_ref), ("grad", grad_in, grad_ref),
+        ("att", att_in, att_ref), ("gl", gl_in, gl_ref), ("outw", outw_in, outw_ref), ("grad", grad_in, dw_ref),
         ("x", x_in, x_ref),
     ):
         moves.start(name, source, target)
@@ -970,7 +971,7 @@
     gates.forward(1)
     moves.wait("grad")
     for j in range(n):
-        dy_ref[j] = grad_ref[:, j * shard : (j + 1) * shard]
+        dy_ref[j] = dw_ref[:, j * shard : (j + 1) * shard]
     dhid_acc[...] = jnp.zeros_like(dhid_acc)
     gate_acc[...] = jnp.zeros_like(gate_acc)
     up_acc[...] = jnp.zeros_like(up_acc)
@@ -1005,16 +1006,7 @@
     lax.fori_loop(0, rows // size, norm_rows, 0)
     own = pl.ds(pl.multiple_of(tp * span, span), span)
     layer_ref[...] = mid_ref[:, own]
-    if attention:
-        narrow = q_in.shape[1]
-        q_ref = x_ref.at[:, pl.ds(0, narrow)]
-        moves.start("q", q_in, q_ref)
-        for i in range(n):
-            moves.start(
-                ("aug", i),
-                aug_in.at[pl.ds(i * rows, rows), :],
-                x_ref.at[:, pl.ds(narrow + i * LANES, LANES)],
-            )
+    moves.start("again", grad_in, x_ref)
     gates.forward(3)
 
     def grow_step(step, carry):
@@ -1145,7 +1137,7 @@
         dw = dw_ref[here, :].astype(F32)
         back = dw * gain_ref[...]
         back = inverse * (back - normal * jnp.mean(back * normal, axis=-1, keepdims=True))
-        dmid = grad_ref[here, :].astype(F32) + back
+        dmid = x_ref[here, :].astype(F32) + back
         mid_ref[here, :] = dmid
         low = dmid.astype(BF16)
         branch_ref[here, :] = low
@@ -1154,7 +1146,18 @@
                 dm_ref[j, here, :] = low[:, j * shard : (j + 1) * shard]
         return acc + jnp.sum((dw * normal).reshape(size // 8, 8, width), axis=0)
 
+    moves.wait("again")
     gain_out[...] = lax.fori_loop(0, rows // size, middle_rows, jnp.zeros((8, width), F32))
+    if attention:
+        narrow = q_in.shape[1]
+        q_ref = x_ref.at[:, pl.ds(0, narrow)]
+        moves.start("q", q_in, q_ref)
+        for i in range(n):
+            moves.start(
+                ("aug", i),
+                aug_in.at[pl.ds(i * rows, rows), :],
+                x_ref.at[:, pl.ds(narrow + i * LANES, LANES)],
+            )
     moves.start("dmid", mid_ref, dmid_out)
     if attention:
         moves.start("dm", dm_ref, dm_out)
@@ -1190,7 +1193,7 @@
         diff_ref[...] = key_at - query_at
         for i, group in enumerate(query_groups):
             span_ref[i] = document_start(group * half + query_at, doc_lengths) - key_at
-        dk_acc, dv_acc, dcol_acc = (dhid_acc.at[:, pl.ds(i * LANES, LANES)] for i in range(3))
+        dcol_acc = dhid_acc.at[:, pl.ds(0, LANES)]
 
         def stage_copies(it):
             part, pair = lax.div(it, pairs), lax.rem(it, pairs)
@@ -1219,34 +1222,44 @@
             value_blocks = ordered(up_all, pair, lanes)
             aug_lanes = pl.ds(pl.multiple_of(narrow + part * LANES, LANES), LANES)
             aug_blocks = ordered(x_ref, 0, aug_lanes)
-            dk_acc[...] = jnp.zeros_like(dk_acc)
-            dv_acc[...] = jnp.zeros_like(dv_acc)
-
-            @pl.when(pair == 0)
-            def _():
-                dcol_acc[...] = jnp.zeros_like(dcol_acc)
-
-            for qi, ki in ((0, 0), (1, 0), (1, 1)):
-                query_group, key_group = query_groups[qi], key_groups[ki]
-                skipped = jnp.where(key_group < query_group, skip[query_group, key_group], 0)
-                mask = (diff_ref[...] <= (query_group - key_group) * half) & (
-                    span_ref[qi] <= key_group * half - (skipped == 1).astype(jnp.int32) * (1 << 30)
-                )
-                q_rows, k_rows = pl.ds(qi * half, half), pl.ds(ki * half, half)
-                keys = jnp.concatenate([key_blocks[ki], aug_blocks[ki]], axis=1)
-                values = jnp.concatenate([value_blocks[ki], aug_blocks[ki]], axis=1)
-                for e in range(2):
-                    h = 2 * pair + e
-                    spot = pl.ds(pl.multiple_of(h * 2 * LANES, 2 * LANES), 2 * LANES)
-                    queries, grads_out = dw_ref[q_rows, spot], branch_ref[q_rows, spot]
-                    probs = jnp.where(mask, jnp.exp(contract_cols(keys, queries)), 0.0)
-                    grads = (probs * contract_cols(values, grads_out)).astype(BF16)
-                    dv_acc[k_rows, :] += dot(probs.astype(BF16), grads_out[:, :LANES])
-                    both = dot(grads, queries)
-                    dk_acc[k_rows, :] += both[:, :LANES]
-                    dcol_acc[k_rows, :] += both[:, LANES:]
-                    quarter = pl.ds(pl.multiple_of(lax.rem(h, 4) * 2 * LANES, 2 * LANES), 2 * LANES)
-                    accs[lax.div(h, 4), q_rows, quarter] += contract_rows(grads, keys)
+            masks = block_masks(diff_ref, span_ref, skip, query_groups, key_groups, half)
+            keys = [jnp.concatenate([key_blocks[ki], aug_blocks[ki]], axis=1) for ki in range(2)]
+            values = [jnp.concatenate([value_blocks[ki], aug_blocks[ki]], axis=1) for ki in range(2)]
+            both_keys = jnp.concatenate(keys, axis=0)
+            queries, douts, probs, grads = [], [], ([], []), ([], [])
+            for e in range(2):
+                h = 2 * pair + e
+                spot = pl.ds(pl.multiple_of(h * 2 * LANES, 2 * LANES), 2 * LANES)
+                query, dout = dw_ref[:, spot], branch_ref[:, spot]
+                early = contract_cols(keys[0], query)
+                scores = (early[:, :half], early[:, half:], contract_cols(keys[1], query[half:]))
+                early = contract_cols(values[0], dout)
+                backs_out = (early[:, :half], early[:, half:], contract_cols(values[1], dout[half:]))
+                prob = [jnp.where(mask, jnp.exp(score), 0.0) for mask, score in zip(masks, scores)]
+                grad = [(p * back).astype(BF16) for p, back in zip(prob, backs_out)]
+                prob = [p.astype(BF16) for p in prob]
+                queries.append(query)
+                douts.append(dout[:, :LANES])
+                probs[0].extend(prob[:2])
+                probs[1].append(prob[2])
+                grads[0].extend(grad[:2])
+                grads[1].append(grad[2])
+                quarter = pl.ds(pl.multiple_of(lax.rem(h, 4) * 2 * LANES, 2 * LANES), 2 * LANES)
+                accs[lax.div(h, 4), :half, quarter] += contract_rows(grad[0], keys[0])
+                accs[lax.div(h, 4), half:, quarter] += contract_rows(jnp.concatenate(grad[1:], axis=0), both_keys)
+            late_queries = jnp.concatenate([query[half:] for query in queries], axis=0)
+            late_douts = jnp.concatenate([dout[half:] for dout in douts], axis=0)
+            queries, douts = jnp.concatenate(queries, axis=0), jnp.concatenate(douts, axis=0)
+            sums = [
+                dot(jnp.concatenate(grads[0], axis=1), queries),
+                dot(jnp.concatenate(grads[1], axis=1), late_queries),
+            ]
+            value_sums = [
+                dot(jnp.concatenate(probs[0], axis=1), douts),
+                dot(jnp.concatenate(probs[1], axis=1), late_douts),
+            ]
+            columns = jnp.concatenate([part_sum[:, LANES:] for part_sum in sums], axis=0)
+            dcol_acc[...] = jnp.where(pair == 0, 0.0, dcol_acc[...]) + columns
 
             @pl.when(it >= 2)
             def _():
@@ -1254,10 +1267,8 @@
                     copy.wait()
 
             slot = lax.rem(it, 2)
-            for i, acc in enumerate((dk_acc, dv_acc)):
-                stage[slot, i] = jnp.concatenate(
-                    in_pack_order(forward, acc[pl.ds(0, half), :], acc[pl.ds(half, half), :]), axis=0
-                ).astype(BF16)
+            for i, part_sums in enumerate(([part_sum[:, :LANES] for part_sum in sums], value_sums)):
+                stage[slot, i] = jnp.concatenate(in_pack_order(forward, *part_sums), axis=0).astype(BF16)
             for copy in stage_copies(it):
                 copy.start()
 
@@ -1367,7 +1378,6 @@
             VMEM(narrow, F32),
             VMEM(out_weight.shape, BF16),
             VMEM(wide, BF16),
-            VMEM(wide, BF16),
             VMEM(narrow, BF16),
             VMEM(by_shard, BF16),
             VMEM(deep, BF16),
@@ -1395,7 +1405,7 @@
             *[dma((3,))] * 2,
             *[dma((2, 1, n - 1))] * 2,
             *[dma((2, 2, n - 1))] * 2,
-            dma((27,)),
+            dma((28,)),
             *extra_scratch,
         ],
         compiler_params=pltpu.CompilerParams(
@@ -1714,6 +1724,19 @@
         end = end + doc_lengths[d]
         start = jnp.where(position >= end, end, start)
     return start
+
+
+def block_masks(diff_ref, span_ref, skip, query_groups, key_groups, rows):
+    masks = []
+    for qi, ki in ((0, 0), (1, 0), (1, 1)):
+        query_group, key_group = query_groups[qi], key_groups[ki]
+        skipped = jnp.where(key_group < query_group, skip[query_group, key_group], 0)
+        reach = key_group * rows - (skipped == 1).astype(jnp.int32) * (1 << 30)
+        mask = span_ref[qi] <= reach
+        if qi == ki:
+            mask = mask & (diff_ref[...] <= (query_group - key_group) * rows)
+        masks.append(mask)
+    return masks
 
 
 def in_pack_order(forward, one, two):

time: 516 us -> 500 us (0.969)
  Pallas kernels: 483 us -> 468 us
    pallas_call x1, Pallas kernels: 211 us -> 196 us  [feed_forward(): pl.pallas_call(functools.partial(feed_kernel, n, heads, attention is not...]
where the time goes in v2:
time: 500 us; the launch traced here: 491 us
  Pallas kernels  468 us (94%)
  local copies, waits for them, and re-layouts  19 us (4%)
    pallas_call x1, Pallas kernels, feed_forward(): pl.pallas_call(functools.partial(feed_kernel, n, heads, attention is not...  196 us
    pallas_call x1, Pallas kernels, start_forward(): pl.pallas_call(functools.partial(start_kernel, n, heads), out_shape=[jax....  138 us
    pallas_call x1, Pallas kernels, finish_backward(): pl.pallas_call(functools.partial(finish_kernel, n, heads, gate_plan, attn...  134 us
    unnamed x30, local copies, waits for them, and re-layouts  11 us

profile of v2, /device:TPU:0, one launch (start us, length us, event | category | flops | bytes accessed | tf_op | source)
XLA Modules:
  0.0 491.5 jit_solution(15899521439630562902)
XLA Ops:
  0.6 0.8 broadcast_compare_fusion
  1.4 0.6 pad_convert_fusion.earlier_ref
  2.1 0.7 stack.10
  2.7 0.7 stack.9
  3.4 1.3 fusion.4.small_in
  4.7 0.7 pad.33
  5.4 0.7 broadcast_in_dim.2.bias_ref
  6.0 138.3 %shard_map.289 = (bf16[1536,384]{1,0:T(8,128)(2,1)}, bf16[1536,384]{1,0:T(8,128)(2,1)}, bf16[1536,384]{1,0:T(8,128)(2,1)}, bf16[1536,384]{1,0:T(8,128)(2,1)}, bf...) custom-call(s32[16]{0:T(128)} %refs_0_.1, ...), custom_call_target="tpu_custom_call" | custom-call | tf_op jit(solution)/shard_map/pallas_call | solution.py:459
  144.3 195.8 %shard_map.290 = (bf16[512,384]{1,0:T(8,128)(2,1)}, f32[512,384]{1,0:T(8,128)}, f32[192,1024]{1,0:T(8,128)}, f32[192,1024]{1,0:T(8,128)}, f32[192,1024]{1,0:T(8,...) custom-call(s32[16]{0:T(128)} %refs_0_.1, ...), custom_call_target="tpu_custom_call" | custom-call | tf_op jit(solution)/shard_map/pallas_call | solution.py:1371
  341.0 133.8 %shard_map.291 = (f32[192,384]{1,0:T(8,128)}, f32[192,384]{1,0:T(8,128)}, f32[192,384]{1,0:T(8,128)}, f32[192,384]{1,0:T(8,128)}, f32[192,384]{1,0:T(8,128)}, /*index=5*/f32[16,256]{1,0:T(8,128)}, f32[512,1536]{1,0:T(8,128)}) custom-call(bf16[8,512,384]{2,1,0:T(8,128)(2,1)} %get-tuple-element.67.refs_0_, bf16[8,512,384]{2,1,0:T(8,128)(2,1)} %get-tuple-element.68.refs_1_, ...), custom_call_target="tpu_custom_call" | custom-call | tf_op jit(solution)/shard_map/pallas_call | solution.py:1650
  474.8 1.3 slice_bitcast_fusion
  476.1 1.3 slice_bitcast_fusion.1
  477.3 1.3 fusion.8
  478.7 1.4 slice_reduce_fusion
  480.1 0.9 copy.43
  480.9 3.9 copy.44
  484.8 0.7 copy.45
  485.5 0.7 copy.46
  486.2 0.7 copy.47
  487.0 0.7 copy.48
  487.7 0.7 copy.49
  488.4 0.9 copy.50
  489.3 0.9 copy.51
  490.2 0.9 copy.52
  (24 shorter events, 0.8 us)
Async XLA Ops:
  144.3 195.9 %copy-start.9 = (s32[16]{0:T(128)S(1)}, s32[16]{0:T(128)}, u32[]{:S(2)}) copy-start(s32[16]{0:T(128)} %refs_0_.1) | copy-start | bytes 196
  341.0 139.1 %copy-start.3 = (f32[512,384]{1,0:T(8,128)S(1)}, f32[512,384]{1,0:T(8,128)}, u32[]{:S(2)}) copy-start(f32[512,384]{1,0:T(8,128)} %get-tuple-element.116) | copy-start | bytes 2359300
  480.9 3.9 copy-start.8
  480.9 4.6 copy-start.7
  480.9 5.3 %copy-start.6 = (f32[192,384]{1,0:T(8,128)S(1)}, f32[192,384]{1,0:T(8,128)}, u32[]{:S(2)}) copy-start(f32[192,384]{1,0:T(8,128)} %get-tuple-element.121) | copy-start | bytes 884740
  480.9 6.0 %copy-start.5 = (f32[192,384]{1,0:T(8,128)S(1)}, f32[192,384]{1,0:T(8,128)}, u32[]{:S(2)}) copy-start(f32[192,384]{1,0:T(8,128)} %get-tuple-element.122) | copy-start | bytes 884740
  484.8 2.9 copy-start.4
  484.8 3.6 copy-start.2
  485.5 3.8 copy-start.1
  487.0 3.2 copy-start

commit v3 on v2

--- a/solution.py
+++ b/solution.py
@@ -147,20 +147,29 @@
 
 
 def start_kernel(
-    n, heads, group_map, doc_lengths, skip, earlier_ref, x_ref, small_in, bias_ref, wq_in, wk_in, wv_in, wg_in, wo_in,
+    n, heads, group_map, doc_lengths, skip, bias_ref, x_ref, norm_one, norm_two, gains_in, forget_in,
+    wq_in, wk_in, wv_in, wg_in, wo_in,
     wq_out, wk_out, wv_out, wg_out, wo_ref, u_out, q_out, qr_out, kr_out, gl_out, fz_ref, k_out, v_out, aug_out,
     att_out, term_ref, gain_one, gain_two, qgain_ref, kgain_ref, wf_ref,
     x_vmem, wq_ref, wk_ref, wv_ref, wg_ref, u_ref, q_ref, k_all, v_all, aug_ref, att_ref, acc_ref, cat_ref,
-    diff_ref, span_ref, tot_ref, before_ref, inside_all,
+    diff_ref, span_ref, tot_ref, before_ref, inside_all, small_wide, small_in,
     small_all, acc_r, acc_l, inside_src,
     wsend, wrecv, osend, orecv, ksend, krecv, ssend, srecv, isend, irecv, spill, local,
 ):
     me, tp, place, sides = ring_setup(n)
     moves = Moves(local)
     moves.start("x", x_ref, x_vmem)
+    shard, width = wq_in.shape
+    small_wide[...] = jnp.zeros_like(small_wide)
+    small_wide[0:1, :shard] = norm_one[...].astype(F32).reshape(1, shard)
+    small_wide[1:2, :shard] = norm_two[...].astype(F32).reshape(1, shard)
+    for ref, first in ((gains_in, 2), (forget_in, 8)):
+        size = ref.shape[0]
+        same = lax.broadcasted_iota(jnp.int32, (size, size), 0) == lax.broadcasted_iota(jnp.int32, (size, size), 1)
+        small_wide[first : first + heads, :size] = contract_rows(ref[...], same.astype(BF16))
+    small_in[...] = small_wide[...].astype(BF16)
     greet(ctx_peers(me, tp, n))
     rows, cols = x_ref.shape
-    shard, width = wq_in.shape
     half = rows // 2
     head_dim = width // heads
 
@@ -259,10 +268,12 @@
     forget = jnp.zeros((16, rows), F32)
     for j in range(n):
         forget += contract_cols(small_all[j, :, :shard], u_ref[j])
-    fz = forget[8:16] + bias_ref[:, 0:1]
+    head = lax.broadcasted_iota(jnp.int32, (8, rows), 0)
+    fz = forget[8:16]
+    for h in range(heads):
+        fz = jnp.where(head == h, fz + bias_ref[h], fz)
     fz_ref[...] = fz
     logs = jnp.minimum(fz, 0.0) - jnp.log1p(jnp.exp(-jnp.abs(fz)))
-    head = lax.broadcasted_iota(jnp.int32, logs.shape, 0)
     logs = jnp.where(head < heads, logs, 0.0)
     upto = (
         lax.broadcasted_iota(jnp.int32, (half, half), 0) <= lax.broadcasted_iota(jnp.int32, (half, half), 1)
@@ -317,7 +328,10 @@
     for i in range(n):
         for g in range(2):
             tot_ref[:, 2 * i + g : 2 * i + g + 1] = inside_all[i, :, (g + 1) * half - 1 : (g + 1) * half]
-    before_ref[...] = jnp.dot(tot_ref[...], earlier_ref[...], precision=HIGHEST, preferred_element_type=F32)
+    earlier = groups_along(group_map, 0, 1 << 20) < groups_along(group_map, 1, 1 << 20)
+    before_ref[...] = jnp.dot(
+        tot_ref[...], earlier.astype(F32), precision=HIGHEST, preferred_element_type=F32
+    )
     lane8 = lax.broadcasted_iota(jnp.int32, (8, LANES), 1)
 
     def offsets_of(shard_index):
@@ -434,7 +448,15 @@
     pairs.sent()
 
 
-def start_forward(n, collective_id, group_map, doc_lengths, skip, earlier, x, small, bias, weights, out_weight):
+def groups_along(group_map, dim, fill, shape=(128, 128)):
+    slot = lax.broadcasted_iota(jnp.int32, shape, dim)
+    groups = jnp.full(shape, fill, jnp.int32)
+    for i in range(group_map.shape[0]):
+        groups = jnp.where(slot == i, group_map[i], groups)
+    return groups
+
+
+def start_forward(n, collective_id, group_map, doc_lengths, skip, bias, x, vectors, weights, out_weight):
     rows, cols = x.shape
     shard, width = out_weight.shape
     heads = bias.shape[0]
@@ -442,7 +464,6 @@
     dma = pltpu.SemaphoreType.DMA
     vmem = pl.BlockSpec(memory_space=VMEM)
     anywhere = pl.BlockSpec(memory_space=pl.ANY)
-    bias = jnp.broadcast_to(jnp.pad(bias, (0, 8 - heads))[:, None], (8, LANES))
     by_pair = (heads // 2, n * rows, LANES)
     weight, wide, narrow = (n * shard, width), (rows, cols), (rows, width)
     shapes = (
@@ -459,7 +480,7 @@
     return pl.pallas_call(
         functools.partial(start_kernel, n, heads),
         out_shape=[jax.ShapeDtypeStruct(*shape) for shape in shapes],
-        in_specs=[smem(), smem(), smem(), vmem, anywhere, vmem, vmem] + [anywhere] * 5,
+        in_specs=[smem(), smem(), smem(), smem(), anywhere] + [vmem] * 4 + [anywhere] * 5,
         out_specs=[anywhere if i < 10 or 11 <= i <= 14 else vmem for i in range(len(shapes))],
         scratch_shapes=[
             VMEM(wide, BF16),
@@ -476,6 +497,8 @@
             VMEM((8, LANES), F32),
             VMEM((8, LANES), F32),
             VMEM((n, 8, rows), F32),
+            VMEM((16, 256), F32),
+            VMEM((16, 256), BF16),
             VMEM((n, 16, 256), BF16),
             VMEM((rows, 2 * width), F32),
             VMEM((rows, 2 * width), F32),
@@ -490,7 +513,7 @@
         compiler_params=pltpu.CompilerParams(
             collective_id=collective_id, has_side_effects=True, vmem_limit_bytes=VMEM_LIMIT
         ),
-    )(group_map, doc_lengths, skip, earlier, x, small, bias, *weights, out_weight)
+    )(group_map, doc_lengths, skip, bias, x, *vectors, *weights, out_weight)
 
 
 class ScatterRing:
@@ -1067,10 +1090,13 @@
         n, [[(hw, 0)], [(hw, 1)]], down_term, (dslot_r, dslot_l), (dfirst_r, dfirst_l), down_write,
         dsend, drecv, place, sides, tp,
     )
-    earlies = ScatterRing(
-        n, [[(hw, (i, 0)), (hw, (i, hw))] for i in range(2)], early_term, (eslot_r, eslot_l), (efirst_r, efirst_l),
-        early_write, esend, erecv, place, sides, tp,
-    )
+    earlies = [
+        ScatterRing(
+            n, [[(hw, (i, part * hw))] for i in range(2)], early_term, (eslot_r.at[part], eslot_l.at[part]),
+            (efirst_r.at[part], efirst_l.at[part]), early_write, esend.at[part], erecv.at[part], place, sides, tp,
+        )
+        for part in range(2)
+    ]
     backs.begin()
     grow_back(n - 2)
     downs.last()
@@ -1098,7 +1124,8 @@
     layer = TpSplit(layer_part, (s0, s1, s2, s3), ssend, srecv, chip, core, sibling, across)
     total.first()
     backs.advance(1)
-    earlies.begin()
+    earlies[0].begin()
+    earlies[1].begin()
     total.second()
     gates.sent()
     if attention:
@@ -1122,10 +1149,10 @@
         lax.fori_loop(0, n * pairs, bring, 0)
     layer.first()
     layer.second()
-    backs.advance(1)
-    earlies.advance(1)
-    backs.advance(1)
-    earlies.advance(1)
+    for _ in range(2):
+        backs.advance(1)
+        earlies[0].advance(1)
+        earlies[1].advance(1)
     total.third()
     total.fourth()
 
@@ -1168,7 +1195,8 @@
     moves.start("do", do_ref, do_out)
     moves.start("dgl", dgl_ref, dgl_out)
     backs.advance(1)
-    earlies.advance(1)
+    earlies[0].advance(1)
+    earlies[1].advance(1)
     layer_ref[...] += layer.third()
 
     if attention:
@@ -1281,13 +1309,27 @@
 
             return carry
 
-        done = 0
-        while earlies.next < n - 1:
-            lax.fori_loop(done, done + 2 * pairs, attend, 0)
-            done += 2 * pairs
-            backs.advance(1)
-            earlies.advance(1)
-        lax.fori_loop(done, n * pairs, attend, 0)
+        turns = (*earlies, backs)
+        starts = [ring.next for ring in turns]
+        services = sum(n - 1 - start for start in starts)
+        assert starts[0] == starts[1] == starts[2] - 1
+        share = n * pairs // services
+
+        def serve(k, carry):
+            lax.fori_loop(k * share, (k + 1) * share, attend, 0)
+            for i, ring in enumerate(turns):
+
+                @pl.when(lax.rem(k, 3) == i)
+                def _(i=i, ring=ring):
+                    ring.forward(starts[i] + lax.div(k, 3))
+
+            return carry
+
+        lax.fori_loop(0, services, serve, 0)
+        for ring in turns:
+            ring.next = n - 1
+        if services * share < n * pairs:
+            lax.fori_loop(services * share, n * pairs, attend, 0)
         for it in (n * pairs - 2, n * pairs - 1):
             for copy in stage_copies(it):
                 copy.wait()
@@ -1313,7 +1355,8 @@
         moves.wait("dq")
     backs.end()
     moves.start("down", down_ref, down_out)
-    earlies.end()
+    earlies[0].end()
+    earlies[1].end()
     moves.start("gate", gate_ref, gate_out)
     moves.start("up", up_ref, up_out)
     downs.sent()
@@ -1399,12 +1442,13 @@
             VMEM((rows, own), BF16),
             VMEM((rows, own), BF16),
             *ring_scratch(n, shard, [hidden // 2] * 2),
-            *ring_scratch(n, shard, [hidden] * 2),
+            *[VMEM((2, n - 1, shard, hidden // 2), BF16)] * 2,
+            *[VMEM((2, shard, hidden // 2), BF16)] * 2,
             *[dma((4, n - 1))] * 4,
             *[dma((3, TP_CHUNKS))] * 4,
             *[dma((3,))] * 2,
             *[dma((2, 1, n - 1))] * 2,
-            *[dma((2, 2, n - 1))] * 2,
+            *[dma((2, 2, 1, n - 1))] * 2,
             dma((28,)),
             *extra_scratch,
         ],
@@ -1447,7 +1491,7 @@
         moves.start(index, operands[index], target)
         operands[index] = target
     (
-        dk_ref, dv_ref, col_ref, row_ref, dq_ref, qr_ref, kr_ref, qgain_ref, kgain_ref, fz_ref, later_ref,
+        dk_ref, dv_ref, col_ref, row_ref, dq_ref, qr_ref, kr_ref, qgain_ref, kgain_ref, fz_ref, group_map,
         wq_ref, wk_ref, wv_ref, wg_ref, wf_ref, dgl_ref, u_ref, dm_ref, gated_ref,
         x_ref, gain_ref, dmid_ref, gain_two_ref,
     ) = operands
@@ -1517,13 +1561,13 @@
     moves.wait(17, 18, 19)
 
     def gate_term(owner, tag):
-        left, right, c0, cw = tag
-        grads = (gated_ref, dqr_ref, dgl_ref)[right]
-        return contract_rows((dm_ref, u_ref)[left][owner], grads[:, c0 : c0 + cw])
+        right, c0, cw = tag
+        left = dm_ref if right == 2 else u_ref
+        return contract_rows(left[owner], (dqr_ref, dgl_ref, gated_ref)[right][:, c0 : c0 + cw])
 
     def gate_write(tag, value):
-        _, right, c0, cw = tag
-        (o_out, q_out, g_out)[right][:, c0 : c0 + cw] = value
+        right, c0, cw = tag
+        (q_out, g_out, o_out)[right][:, c0 : c0 + cw] = value
 
     gates = ScatterRing(
         n, gate_plan, gate_term, (gslot_r, gslot_l), (gfirst_r, gfirst_l), gate_write, gsend, grecv, place, sides, tp,
@@ -1563,7 +1607,8 @@
         suffix = jnp.dot(
             off_sum[:, g * half : (g + 1) * half], onward, precision=HIGHEST, preferred_element_type=F32
         )
-        parts.append(suffix + jnp.sum(tot_sum * later_ref[g : g + 1, :], axis=1, keepdims=True))
+        later = groups_along(group_map, 1, -1, (8, LANES)) > group_map[2 * me + g]
+        parts.append(suffix + jnp.sum(jnp.where(later, tot_sum, 0.0), axis=1, keepdims=True))
     dfz = (jnp.concatenate(parts, axis=1) * jax.nn.sigmoid(-fz_ref[...])).astype(BF16).astype(F32)
     head = lax.broadcasted_iota(jnp.int32, dfz.shape, 0)
     dfz = jnp.where(head < heads, dfz, 0.0)
@@ -1650,7 +1695,7 @@
     return pl.pallas_call(
         functools.partial(finish_kernel, n, heads, gate_plan, attn_plan),
         out_shape=[jax.ShapeDtypeStruct(shape, F32) for shape in shapes],
-        in_specs=[anywhere if i in outside else vmem for i in range(len(operands))],
+        in_specs=[anywhere if i in outside else smem() if i == 10 else vmem for i in range(len(operands))],
         out_specs=[vmem] * 6 + [anywhere],
         scratch_shapes=[
             *[VMEM(operands[i].shape, operands[i].dtype) for i in STAGED],
@@ -1944,6 +1989,48 @@
     )(me, group_map, doc_lengths, skip, queries, grads, attended, term, keys, values, key_aug)
 
 
+def deliver_kernel(heads, count, small_ref, *refs):
+    sources, refs = refs[:count], refs[count:]
+    targets, refs = refs[:count], refs[count:]
+    (first_ref, second_ref, forget_ref, bias_ref, gains_ref), refs = refs[:5], refs[5:]
+    held, local = refs[:count], refs[count]
+    moves = Moves(local)
+    for i in range(count):
+        moves.start(i, sources[i], held[i])
+    shard, gain_rows = first_ref.shape[0], gains_ref.shape[0]
+    first_ref[...] = small_ref[0:1, :shard].reshape(shard)
+    second_ref[...] = small_ref[1:2, :shard].reshape(shard)
+    turned = jnp.concatenate([small_ref[...], jnp.zeros((LANES - 16, 256), F32)], axis=0).T
+    forget_ref[...] = turned[:shard, 8 : 8 + heads]
+    gains_ref[...] = turned[:gain_rows, 2 : 2 + heads]
+    bias_ref[...] = turned[224:225, 8 : 8 + heads].reshape(heads)
+    for i in range(count):
+        moves.wait(i)
+        moves.start(i, held[i], targets[i])
+    moves.wait()
+
+
+def deliver(heads, shard, gain_rows, small, arrays):
+    vmem = pl.BlockSpec(memory_space=VMEM)
+    anywhere = pl.BlockSpec(memory_space=pl.ANY)
+    shapes = [array.shape for array in arrays]
+    shapes += [(shard,), (shard,), (shard, heads), (heads,), (gain_rows, heads)]
+    (layer, input_grad, query, key, value, gate_out, output, gate, up, down, one, two, forget, bias, gains) = (
+        pl.pallas_call(
+            functools.partial(deliver_kernel, heads, len(arrays)),
+            out_shape=[jax.ShapeDtypeStruct(shape, F32) for shape in shapes],
+            in_specs=[vmem] + [anywhere] * len(arrays),
+            out_specs=[anywhere] * len(arrays) + [vmem] * 5,
+            scratch_shapes=[VMEM(array.shape, F32) for array in arrays]
+            + [pltpu.SemaphoreType.DMA((2 * len(arrays),))],
+            compiler_params=pltpu.CompilerParams(vmem_limit_bytes=VMEM_LIMIT),
+        )(small, *arrays)
+    )
+    return (
+        layer, input_grad, one, query, key, value, gate_out, forget, bias, gains, output, two, gate, up, down,
+    )
+
+
 def on_device(
     hidden_in,
     norm_one,
@@ -1977,21 +2064,6 @@
     hidden_width = w_gate.shape[1]
 
     slots = 2 * n
-    earlier = jnp.pad(
-        (group_map[:, None] < group_map[None, :]).astype(F32), ((0, LANES - slots), (0, LANES - slots))
-    )
-
-    def lanes_of(value, first_rows, last_rows):
-        return jnp.pad(value, ((first_rows, last_rows), (0, 256 - value.shape[1])))
-
-    small = jnp.concatenate(
-        [
-            lanes_of(jnp.stack([norm_one, norm_two]), 0, 0),
-            lanes_of(head_gains.T, 0, 6 - heads),
-            lanes_of(w_forget.T, 0, 8 - heads),
-        ],
-        axis=0,
-    )
     (
         query_weight,
         key_weight,
@@ -2015,10 +2087,18 @@
         key_gain,
         forget_weight,
     ) = start_forward(
-        n, 1, group_map, doc_lengths, skip_list, earlier, hidden_in, small, forget_bias, [w_query, w_key, w_value, w_gate_out], w_output
+        n,
+        1,
+        group_map,
+        doc_lengths,
+        skip_list,
+        forget_bias,
+        hidden_in,
+        [norm_one, norm_two, head_gains, w_forget],
+        [w_query, w_key, w_value, w_gate_out],
+        w_output,
     )
     half = width // 256 * 128
-    me_one = device_ctx.astype(jnp.int32).reshape(1)
     fused = n <= 8
     (
         gated,
@@ -2046,44 +2126,16 @@
         w_down,
         (group_map, doc_lengths, skip_list, query_rows, row_term, keys_all, values_all, key_aug) if fused else None,
     )
-    if not fused:
-        grad_branch = grad_middle.astype(BF16).reshape(row_count, n, shard).transpose(1, 0, 2)
-        attention_grads = grad_branch, *backward_attention(
-            me_one,
-            group_map,
-            doc_lengths,
-            skip_list,
-            query_rows,
-            grad_attended,
-            attended_flat,
-            row_term,
-            keys_all,
-            values_all,
-            key_aug,
-            heads,
-        )
-    grad_branch, grad_query, row_sums, key_part, value_part, column_sums = attention_grads
-
-    gate_plan = [
-        [(width, (1, 1 + i, 0, width)), (w, (0, 0, c, w))] for i, (c, w) in enumerate([(0, half), (half, width - half)])
-    ]
-    attn_plan = [[(half, (i, 0, half)), (width - half, (i, half, width - half))] for i in (0, 1)]
-    own_groups = lax.dynamic_slice_in_dim(group_map, device_ctx * 2, 2, 0)
-    later = (group_map[None, :] > own_groups[:, None]).astype(F32)
+    halves = [(0, half), (half, width - half)]
+    attn_plan = [[(cw, (i, c0, cw)) for c0, cw in halves] for i in (0, 1)]
     if fused:
-        (
-            query_share,
-            key_share,
-            value_share,
-            gate_out_share,
-            output_share,
-            small_share,
-            input_grad,
-        ) = finish_backward(
+        grad_branch, grad_query, row_sums, key_part, value_part, column_sums = attention_grads
+        early_plan = [side + [(cw, (2, c0, cw))] for side, (c0, cw) in zip(attn_plan, halves)]
+        query_share, key_share, value_share, gate_out_share, output_share, small_share, input_grad = finish_backward(
             n,
             7,
             heads,
-            gate_plan,
+            early_plan,
             attn_plan,
             key_part,
             value_part,
@@ -2095,7 +2147,7 @@
             query_gain,
             key_gain,
             forget_logit,
-            jnp.pad(later, ((0, 6), (0, LANES - slots))),
+            group_map,
             query_weight,
             key_weight,
             value_weight,
@@ -2111,6 +2163,23 @@
             gain_two_parts,
         )
     else:
+        grad_branch = grad_middle.astype(BF16).reshape(row_count, n, shard).transpose(1, 0, 2)
+        grad_query, row_sums, key_part, value_part, column_sums = backward_attention(
+            device_ctx.astype(jnp.int32).reshape(1),
+            group_map,
+            doc_lengths,
+            skip_list,
+            query_rows,
+            grad_attended,
+            attended_flat,
+            row_term,
+            keys_all,
+            values_all,
+            key_aug,
+            heads,
+        )
+        own_groups = lax.dynamic_slice_in_dim(group_map, device_ctx * 2, 2, 0)
+        later = (group_map[None, :] > own_groups[:, None]).astype(F32)
         query_gain, key_gain = (gain.reshape(heads, head_dim) for gain in (query_gain, key_gain))
         query_raw, key_raw = (raw.reshape(row_count, heads, head_dim) for raw in (query_raw, key_raw))
         query_norm, key_norm = rms_scale(query_raw), rms_scale(key_raw)
@@ -2160,11 +2229,9 @@
             ],
             axis=1,
         )
-        lefts, rights = (1, 0), (4, 0, 3)
         plan = [
-            [(w, (0, 1 + i, c0, cw)) for w, (i, c0, cw) in attn]
-            + [(w, (lefts[left], rights[right], c0, cw)) for w, (left, right, c0, cw) in gate]
-            for attn, gate in zip(attn_plan, gate_plan)
+            [(cw, (0, right, c0, cw)) for right in rights for c0, cw in halves] + [(cw, (1, 4, c0, cw))]
+            for rights, (c0, cw) in zip(((0, 1), (2, 3)), halves)
         ]
         (
             query_share,
@@ -2186,22 +2253,23 @@
             gain_one,
             grad_middle,
         )
-    return (
-        layer_out,
-        input_grad,
-        small_share[0, :shard],
-        query_share,
-        key_share,
-        value_share,
-        gate_out_share,
-        small_share[8 : 8 + heads, :shard].T,
-        small_share[8 : 8 + heads, 224],
-        small_share[2 : 2 + heads, :gain_rows].T,
-        output_share,
-        small_share[1, :shard],
-        gate_share,
-        up_share,
-        down_share,
+    return deliver(
+        heads,
+        shard,
+        gain_rows,
+        small_share,
+        [
+            layer_out,
+            input_grad,
+            query_share,
+            key_share,
+            value_share,
+            gate_out_share,
+            output_share,
+            gate_share,
+            up_share,
+            down_share,
+        ],
     )
 
 

time: 500 us -> 491 us (0.982)
  local copies, waits for them, and re-layouts: 19 us -> 5.73 us
  Pallas kernels: 468 us -> 476 us
    pallas_call x0 -> x1, Pallas kernels: none -> 6.78 us  [deliver(): pl.pallas_call(functools.partial(deliver_kernel, heads, len(arrays)), out...]
    unnamed x30 -> x4, local copies, waits for them, and re-layouts: 11 us -> 5.73 us
where the time goes in v3:
time: 491 us; the launch traced here: 483 us
  Pallas kernels  476 us (97%)
  local copies, waits for them, and re-layouts  5.73 us (1%)
    pallas_call x1, Pallas kernels, feed_forward(): pl.pallas_call(functools.partial(feed_kernel, n, heads, attention is not...  196 us
    pallas_call x1, Pallas kernels, start_forward(): pl.pallas_call(functools.partial(start_kernel, n, heads), out_shape=[jax....  138 us
    pallas_call x1, Pallas kernels, finish_backward(): pl.pallas_call(functools.partial(finish_kernel, n, heads, gate_plan, attn...  134 us

profile of v3, /device:TPU:0, one launch (start us, length us, event | category | flops | bytes accessed | tf_op | source)
XLA Modules:
  0.0 482.5 jit_solution(16914143530358071428)
XLA Ops:
  0.6 1.4 copy.33.gains_in
  2.0 1.4 copy.34.forget_in
  3.4 138.5 %shard_map.289 = (bf16[1536,384]{1,0:T(8,128)(2,1)}, bf16[1536,384]{1,0:T(8,128)(2,1)}, bf16[1536,384]{1,0:T(8,128)(2,1)}, bf16[1536,384]{1,0:T(8,128)(2,1)}, bf...) custom-call(s32[16]{0:T(128)} %refs_10_.1, ...), custom_call_target="tpu_custom_call" | custom-call | tf_op jit(solution)/shard_map/pallas_call | solution.py:480
  141.9 196.4 %shard_map.290 = (bf16[512,384]{1,0:T(8,128)(2,1)}, f32[512,384]{1,0:T(8,128)}, f32[192,1024]{1,0:T(8,128)}, f32[192,1024]{1,0:T(8,128)}, f32[192,1024]{1,0:T(8,...) custom-call(s32[16]{0:T(128)} %refs_10_.1, ...), custom_call_target="tpu_custom_call" | custom-call | tf_op jit(solution)/shard_map/pallas_call | solution.py:1414
  338.4 134.0 %shard_map.291 = (f32[192,384]{1,0:T(8,128)}, f32[192,384]{1,0:T(8,128)}, f32[192,384]{1,0:T(8,128)}, f32[192,384]{1,0:T(8,128)}, f32[192,384]{1,0:T(8,128)}, /*index=5*/f32[16,256]{1,0:T(8,128)}, f32[512,1536]{1,0:T(8,128)}) custom-call(bf16[8,512,384]{2,1,0:T(8,128)(2,1)} %get-tuple-element.81.refs_0_, bf16[8,512,384]{2,1,0:T(8,128)(2,1)} %get-tuple-element.82.refs_1_, ...), custom_call_target="tpu_custom_call" | custom-call | tf_op jit(solution)/shard_map/pallas_call | solution.py:1695
  472.4 6.8 %shard_map.292 = (f32[512,384]{1,0:T(8,128)}, f32[512,1536]{1,0:T(8,128)}, f32[192,384]{1,0:T(8,128)}, f32[192,384]{1,0:T(8,128)}, f32[192,384]{1,0:T(8,128)}, /...) custom-call(f32[16,256]{1,0:T(8,128)} %get-tuple-element.103.small_r, ...), custom_call_target="tpu_custom_call" | custom-call | tf_op jit(solution)/shard_map/pallas_call | solution.py:2019
  479.1 1.4 copy.36
  480.5 1.6 copy.35

commit v4 on v3

--- a/solution.py
+++ b/solution.py
@@ -151,7 +151,7 @@
     wq_in, wk_in, wv_in, wg_in, wo_in,
     wq_out, wk_out, wv_out, wg_out, wo_ref, u_out, q_out, qr_out, kr_out, gl_out, fz_ref, k_out, v_out, aug_out,
     att_out, term_ref, gain_one, gain_two, qgain_ref, kgain_ref, wf_ref,
-    x_vmem, wq_ref, wk_ref, wv_ref, wg_ref, u_ref, q_ref, k_all, v_all, aug_ref, att_ref, acc_ref, cat_ref,
+    x_vmem, wq_ref, wk_ref, wv_ref, wg_ref, u_ref, turned_ref, q_ref, k_all, v_all, aug_ref, att_ref, acc_ref, cat_ref,
     diff_ref, span_ref, tot_ref, before_ref, inside_all, small_wide, small_in,
     small_all, acc_r, acc_l, inside_src,
     wsend, wrecv, osend, orecv, ksend, krecv, ssend, srecv, isend, irecv, spill, local,
@@ -164,9 +164,7 @@
     small_wide[0:1, :shard] = norm_one[...].astype(F32).reshape(1, shard)
     small_wide[1:2, :shard] = norm_two[...].astype(F32).reshape(1, shard)
     for ref, first in ((gains_in, 2), (forget_in, 8)):
-        size = ref.shape[0]
-        same = lax.broadcasted_iota(jnp.int32, (size, size), 0) == lax.broadcasted_iota(jnp.int32, (size, size), 1)
-        small_wide[first : first + heads, :size] = contract_rows(ref[...], same.astype(BF16))
+        small_wide[first : first + heads, : ref.shape[1]] = ref[...].astype(F32)
     small_in[...] = small_wide[...].astype(BF16)
     greet(ctx_peers(me, tp, n))
     rows, cols = x_ref.shape
@@ -239,18 +237,19 @@
             lane = h * head_dim + at * count
             target[:, lane : lane + count] = block_small[2 + h : 3 + h, :count]
 
-    size = 64
+    size = LANES
 
     def norm_rows(i, carry):
         here = pl.ds(pl.multiple_of(i * size, size), size)
         normed = (rms_scale(x_vmem[here, :].astype(F32)) * gain_one[...]).astype(BF16)
         for j in range(n):
             u_ref[j, here, :] = normed[:, j * shard : (j + 1) * shard]
+        turned_ref[:, here] = normed.astype(F32).T.astype(BF16)
         return carry
 
     moves.wait("x")
     lax.fori_loop(0, rows // size, norm_rows, 0)
-    moves.start("u", u_ref, u_out)
+    moves.start("u", turned_ref, u_out)
 
     def grow(back):
         for side, acc, sources in ((0, acc_r, (wq_ref, wk_ref)), (1, acc_l, (wv_ref, wg_ref))):
@@ -468,7 +467,7 @@
     weight, wide, narrow = (n * shard, width), (rows, cols), (rows, width)
     shapes = (
         [(weight, BF16)] * 5
-        + [((n, rows, shard), BF16), (narrow, BF16)]
+        + [((n * shard, rows), BF16), (narrow, BF16)]
         + [(narrow, F32)] * 3
         + [((8, rows), F32)]
         + [(by_pair, BF16)] * 2
@@ -486,6 +485,7 @@
             VMEM(wide, BF16),
             *[VMEM(weight, BF16)] * 4,
             VMEM((n, rows, shard), BF16),
+            VMEM((n * shard, rows), BF16),
             VMEM(narrow, BF16),
             *[VMEM(by_pair, BF16)] * 2,
             VMEM((n * rows, LANES), BF16),
@@ -929,7 +929,7 @@
         gsend, grecv, hsend, hrecv, asend, arecv, bsend, brecv, ssend, srecv, dsend, drecv, esend, erecv, local,
     ), refs = refs[:52], refs[52:]
     if attention:
-        term_ref, dm_ref, diff_ref, span_ref, stage, kv_sem, stage_sem = refs
+        term_ref, diff_ref, span_ref, stage, kv_sem, stage_sem = refs
     gate_acc, up_acc = accs.at[0], accs.at[1]
     me, tp, place, sides = ring_setup(n)
     chip, core, sibling, across = tp_setup()
@@ -993,8 +993,9 @@
     branch.second()
     gates.forward(1)
     moves.wait("grad")
-    for j in range(n):
-        dy_ref[j] = dw_ref[:, j * shard : (j + 1) * shard]
+    for c in range(TP_CHUNKS):
+        back = pl.ds(c * span, span)
+        dy_ref[back, :] = dw_ref[:, back].astype(F32).T.astype(BF16)
     dhid_acc[...] = jnp.zeros_like(dhid_acc)
     gate_acc[...] = jnp.zeros_like(gate_acc)
     up_acc[...] = jnp.zeros_like(up_acc)
@@ -1003,12 +1004,12 @@
         for side in (0, 1):
             owner = downs.owner(side, back)
             cols = pl.ds(side * hw, hw)
-            dhid_acc[:, cols] += dot(dy_ref[owner], down_all[rows_of(owner), cols])
+            dhid_acc[:, cols] += contract_rows(dy_ref[rows_of(owner), :], down_all[rows_of(owner), cols])
 
     def grow(back):
         for side, acc, source in ((0, gate_acc, gate_all), (1, up_acc, up_all)):
             owner = gates.owner(side, back)
-            acc[...] += dot(normed_ref[owner], source[rows_of(owner), :])
+            acc[...] += contract_rows(normed_ref[rows_of(owner), :], source[rows_of(owner), :])
 
     moves.wait(0, 1, 2)
     grow_back(0)
@@ -1018,15 +1019,13 @@
     moves.wait("x")
 
     def norm_rows(i, carry):
-        here = pl.ds(pl.multiple_of(i * size, size), size)
+        here = pl.ds(pl.multiple_of(i * LANES, LANES), LANES)
         middle = x_ref[here, :].astype(F32) + branch_ref[here, :].astype(F32)
         mid_ref[here, :] = middle
-        normed = (rms_scale(middle) * gain_ref[...]).astype(BF16)
-        for j in range(n):
-            normed_ref[j, here, :] = normed[:, j * shard : (j + 1) * shard]
+        normed_ref[:, here] = (rms_scale(middle) * gain_ref[...]).T.astype(BF16)
         return carry
 
-    lax.fori_loop(0, rows // size, norm_rows, 0)
+    lax.fori_loop(0, rows // LANES, norm_rows, 0)
     own = pl.ds(pl.multiple_of(tp * span, span), span)
     layer_ref[...] = mid_ref[:, own]
     moves.start("again", grad_in, x_ref)
@@ -1069,7 +1068,7 @@
     downs.forward(n - 2)
 
     def down_term(owner, tag):
-        return contract_rows(dy_ref[owner], hid_ref[:, tag * hw : (tag + 1) * hw])
+        return dot(dy_ref[rows_of(owner), :], hid_ref[:, tag * hw : (tag + 1) * hw])
 
     down_ref = accs.at[0, pl.ds(0, shard), :]
     gate_ref = accs.at[0, pl.ds(shard, shard), :]
@@ -1080,7 +1079,7 @@
 
     def early_term(owner, tag):
         which, c0 = tag
-        return contract_rows(normed_ref[owner], (dgt_ref, dup_ref)[which][:, c0 : c0 + hw])
+        return dot(normed_ref[rows_of(owner), :], (dgt_ref, dup_ref)[which][:, c0 : c0 + hw])
 
     def early_write(tag, value):
         which, c0 = tag
@@ -1166,11 +1165,7 @@
         back = inverse * (back - normal * jnp.mean(back * normal, axis=-1, keepdims=True))
         dmid = x_ref[here, :].astype(F32) + back
         mid_ref[here, :] = dmid
-        low = dmid.astype(BF16)
-        branch_ref[here, :] = low
-        if attention:
-            for j in range(n):
-                dm_ref[j, here, :] = low[:, j * shard : (j + 1) * shard]
+        branch_ref[here, :] = dmid.astype(BF16)
         return acc + jnp.sum((dw * normal).reshape(size // 8, 8, width), axis=0)
 
     moves.wait("again")
@@ -1187,7 +1182,7 @@
             )
     moves.start("dmid", mid_ref, dmid_out)
     if attention:
-        moves.start("dm", dm_ref, dm_out)
+        moves.start("dm", branch_ref, dm_out)
     da = dot(branch_ref[...], outw_ref[...])
     open_gate = jax.nn.sigmoid(gl_ref[...])
     do_ref[...] = (da * open_gate).astype(BF16)
@@ -1214,6 +1209,7 @@
 
         spread_heads(q_ref, row_pieces(term_ref[...], True), put_in(dw_ref), heads, in_order)
         delta = head_sums(do_ref[...].astype(F32) * att_ref[...], heads)
+        moves.wait("dm")
         spread_heads(do_ref, row_pieces(-delta, False), put_in(branch_ref), heads, in_order)
         accs[...] = jnp.zeros_like(accs)
         query_at = lax.broadcasted_iota(jnp.int32, (half, half), 1)
@@ -1375,7 +1371,7 @@
     vmem = pl.BlockSpec(memory_space=VMEM)
     anywhere = pl.BlockSpec(memory_space=pl.ANY)
     wide, narrow, deep = (rows, width), (rows, heads_width), (rows, hidden)
-    by_shard = (n, rows, shard)
+    turned = (n * shard, rows)
     weight = (shard, hidden)
     shapes = [
         (narrow, BF16),
@@ -1393,7 +1389,7 @@
     if attention is not None:
         assert heads // 2 * rows == n * shard and n * LANES == hidden and heads_width + hidden <= width
         shapes += [
-            (by_shard, BF16),
+            (wide, BF16),
             (narrow, F32),
             ((8, rows), F32),
             ((n, rows, heads_width), BF16),
@@ -1404,7 +1400,6 @@
         extra_specs = [smem()] * 3 + [anywhere] * 5
         extra_scratch = [
             VMEM((rows, LANES), F32),
-            VMEM(by_shard, BF16),
             VMEM((half, half), jnp.int32),
             VMEM((2, half, half), jnp.int32),
             VMEM((2, 2, rows, LANES), BF16),
@@ -1422,7 +1417,7 @@
             VMEM(out_weight.shape, BF16),
             VMEM(wide, BF16),
             VMEM(narrow, BF16),
-            VMEM(by_shard, BF16),
+            VMEM(turned, BF16),
             VMEM(deep, BF16),
             VMEM(deep, BF16),
             VMEM(narrow, BF16),
@@ -1434,7 +1429,7 @@
             VMEM(wide, BF16),
             VMEM(wide, F32),
             VMEM(wide, BF16),
-            VMEM(by_shard, BF16),
+            VMEM(turned, BF16),
             *tp_buffers(rows, width),
             VMEM((rows // 2, width), BF16),
             VMEM((2, rows, own), BF16),
@@ -1480,7 +1475,7 @@
     (q_out, k_out, v_out, g_out, o_out, small_out, input_out), refs = refs[:7], refs[7:]
     staged, refs = refs[: len(STAGED)], refs[len(STAGED) :]
     (
-        pslot_r, pslot_l, gslot_r, gslot_l, gfirst_r, gfirst_l, aslot_r, aslot_l, afirst_r, afirst_l,
+        dmt_ref, pslot_r, pslot_l, gslot_r, gslot_l, gfirst_r, gfirst_l, aslot_r, aslot_l, afirst_r, afirst_l,
         dk_sum, dv_sum, dqr_ref, dkr_ref, dvl_ref, du_ref, sum_ref, t0, t1, t2, t3,
         off_ref, tot_ref, off_land, tot_land, small_ref, small_land,
         psend, precv, gsend, grecv, asend, arecv, osend, orecv, qsend, qrecv, xsend, xrecv, tsend, trecv, local,
@@ -1499,9 +1494,13 @@
     chip, core, sibling, across = tp_setup()
     rows, width = dq_ref.shape
     cols = x_ref.shape[1]
-    shard = u_ref.shape[2]
+    shard = u_ref.shape[0] // n
     half = rows // 2
     head_dim = width // heads
+
+    def rows_of(owner):
+        return pl.ds(pl.multiple_of(owner * shard, 16), shard)
+
     small_ref[...] = jnp.zeros_like(small_ref)
     greet(ctx_peers(me, tp, n) + [sibling, across])
 
@@ -1557,13 +1556,17 @@
     for c in range(TP_CHUNKS):
         back = pl.ds(c * span, span)
         du_ref[:, back] = contract_cols(dqr_ref[...], wq_ref[back, :]) + contract_cols(dgl_ref[...], wg_ref[back, :])
+    moves.wait(18)
+    for c in range(TP_CHUNKS):
+        back = pl.ds(c * span, span)
+        dmt_ref[back, :] = dm_ref[:, back].astype(F32).T.astype(BF16)
     pairs.advance(n)
-    moves.wait(17, 18, 19)
+    moves.wait(17, 19)
 
     def gate_term(owner, tag):
         right, c0, cw = tag
-        left = dm_ref if right == 2 else u_ref
-        return contract_rows(left[owner], (dqr_ref, dgl_ref, gated_ref)[right][:, c0 : c0 + cw])
+        left = dmt_ref if right == 2 else u_ref
+        return dot(left[rows_of(owner), :], (dqr_ref, dgl_ref, gated_ref)[right][:, c0 : c0 + cw])
 
     def gate_write(tag, value):
         right, c0, cw = tag
@@ -1583,7 +1586,7 @@
 
     def attn_term(owner, tag):
         c0, cw = tag[1], tag[2]
-        return contract_rows(u_ref[owner], (dkr_ref, dvl_ref)[tag[0]][:, c0 : c0 + cw])
+        return dot(u_ref[rows_of(owner), :], (dkr_ref, dvl_ref)[tag[0]][:, c0 : c0 + cw])
 
     def attn_write(tag, value):
         c0, cw = tag[1], tag[2]
@@ -1616,7 +1619,7 @@
     dfz_cols = turn(dfz).astype(BF16)
     dfz_low = dfz.astype(BF16)
     for i in range(n):
-        small_ref[i, 8:16, :shard] = dot(dfz_low, u_ref[i])
+        small_ref[i, 8:16, :shard] = contract_cols(dfz_low, u_ref[i * shard : (i + 1) * shard, :])
         small_ref[i, 8:16, 224:225] = bias
         small_ref[i, 1:2, :shard] = jnp.sum(gain_two_ref[:, i * shard : (i + 1) * shard], axis=0, keepdims=True)
 
@@ -1680,7 +1683,7 @@
     dq, u, x = operands[4], operands[17], operands[20]
     rows, width = dq.shape
     cols = x.shape[1]
-    shard = u.shape[2]
+    shard = u.shape[0] // n
     dma = pltpu.SemaphoreType.DMA
     vmem = pl.BlockSpec(memory_space=VMEM)
     anywhere = pl.BlockSpec(memory_space=pl.ANY)
@@ -1699,6 +1702,7 @@
         out_specs=[vmem] * 6 + [anywhere],
         scratch_shapes=[
             *[VMEM(operands[i].shape, operands[i].dtype) for i in STAGED],
+            VMEM(u.shape, BF16),
             *[VMEM((n - 1, rows, width), BF16)] * 2,
             *ring_scratch(n, shard, gate_widths),
             *ring_scratch(n, shard, attn_widths),
@@ -1997,12 +2001,12 @@
     moves = Moves(local)
     for i in range(count):
         moves.start(i, sources[i], held[i])
-    shard, gain_rows = first_ref.shape[0], gains_ref.shape[0]
+    shard, gain_rows = first_ref.shape[0], gains_ref.shape[1]
     first_ref[...] = small_ref[0:1, :shard].reshape(shard)
     second_ref[...] = small_ref[1:2, :shard].reshape(shard)
     turned = jnp.concatenate([small_ref[...], jnp.zeros((LANES - 16, 256), F32)], axis=0).T
-    forget_ref[...] = turned[:shard, 8 : 8 + heads]
-    gains_ref[...] = turned[:gain_rows, 2 : 2 + heads]
+    forget_ref[...] = small_ref[8 : 8 + heads, :shard]
+    gains_ref[...] = small_ref[2 : 2 + heads, :gain_rows]
     bias_ref[...] = turned[224:225, 8 : 8 + heads].reshape(heads)
     for i in range(count):
         moves.wait(i)
@@ -2014,7 +2018,7 @@
     vmem = pl.BlockSpec(memory_space=VMEM)
     anywhere = pl.BlockSpec(memory_space=pl.ANY)
     shapes = [array.shape for array in arrays]
-    shapes += [(shard,), (shard,), (shard, heads), (heads,), (gain_rows, heads)]
+    shapes += [(shard,), (shard,), (heads, shard), (heads,), (heads, gain_rows)]
     (layer, input_grad, query, key, value, gate_out, output, gate, up, down, one, two, forget, bias, gains) = (
         pl.pallas_call(
             functools.partial(deliver_kernel, heads, len(arrays)),
@@ -2027,7 +2031,7 @@
         )(small, *arrays)
     )
     return (
-        layer, input_grad, one, query, key, value, gate_out, forget, bias, gains, output, two, gate, up, down,
+        layer, input_grad, one, query, key, value, gate_out, forget.T, bias, gains.T, output, two, gate, up, down,
     )
 
 
@@ -2094,7 +2098,7 @@
         skip_list,
         forget_bias,
         hidden_in,
-        [norm_one, norm_two, head_gains, w_forget],
+        [norm_one, norm_two, head_gains.T, w_forget.T],
         [w_query, w_key, w_value, w_gate_out],
         w_output,
     )
@@ -2164,6 +2168,7 @@
         )
     else:
         grad_branch = grad_middle.astype(BF16).reshape(row_count, n, shard).transpose(1, 0, 2)
+        normed_shards = normed_shards.reshape(n, shard, row_count).transpose(0, 2, 1)
         grad_query, row_sums, key_part, value_part, column_sums = backward_attention(
             device_ctx.astype(jnp.int32).reshape(1),
             group_map,

time: 491 us -> 485 us (0.988)
  local copies, waits for them, and re-layouts: 5.73 us -> 0 us
    unnamed x4 -> x0, local copies, waits for them, and re-layouts: 5.73 us -> none
where the time goes in v4:
time: 485 us; the launch traced here: 477 us
  Pallas kernels  475 us (98%)
    pallas_call x1, Pallas kernels, feed_forward(): pl.pallas_call(functools.partial(feed_kernel, n, heads, attention is not...  195 us
    pallas_call x1, Pallas kernels, start_forward(): pl.pallas_call(functools.partial(start_kernel, n, heads), out_shape=[jax....  138 us
    pallas_call x1, Pallas kernels, finish_backward(): pl.pallas_call(functools.partial(finish_kernel, n, heads, gate_plan, attn...  135 us

profile of v4, /device:TPU:0, one launch (start us, length us, event | category | flops | bytes accessed | tf_op | source)
XLA Modules:
  0.0 476.6 jit_solution(10061189832525002331)
XLA Ops:
  0.6 138.4 %shard_map.289 = (bf16[1536,384]{1,0:T(8,128)(2,1)}, bf16[1536,384]{1,0:T(8,128)(2,1)}, bf16[1536,384]{1,0:T(8,128)(2,1)}, bf16[1536,384]{1,0:T(8,128)(2,1)}, bf...) custom-call(s32[16]{0:T(128)} %refs_10_.1, ...), custom_call_target="tpu_custom_call" | custom-call | tf_op jit(solution)/shard_map/pallas_call | solution.py:479
  139.1 195.5 %shard_map.290 = (bf16[512,384]{1,0:T(8,128)(2,1)}, f32[512,384]{1,0:T(8,128)}, f32[192,1024]{1,0:T(8,128)}, f32[192,1024]{1,0:T(8,128)}, f32[192,1024]{1,0:T(8,...) custom-call(s32[16]{0:T(128)} %refs_10_.1, ...), custom_call_target="tpu_custom_call" | custom-call | tf_op jit(solution)/shard_map/pallas_call | solution.py:1409
  334.5 134.9 %shard_map.291 = (f32[192,384]{1,0:T(8,128)}, f32[192,384]{1,0:T(8,128)}, f32[192,384]{1,0:T(8,128)}, f32[192,384]{1,0:T(8,128)}, f32[192,384]{1,0:T(8,128)}, /*index=5*/f32[16,256]{1,0:T(8,128)}, f32[512,1536]{1,0:T(8,128)}) custom-call(bf16[8,512,384]{2,1,0:T(8,128)(2,1)} %get-tuple-element.81.refs_0_, bf16[8,512,384]{2,1,0:T(8,128)(2,1)} %get-tuple-element.82.refs_1_, ...), custom_call_target="tpu_custom_call" | custom-call | tf_op jit(solution)/shard_map/pallas_call | solution.py:1698
  469.4 6.7 %shard_map.292 = (f32[512,384]{1,0:T(8,128)}, f32[512,1536]{1,0:T(8,128)}, f32[192,384]{1,0:T(8,128)}, f32[192,384]{1,0:T(8,128)}, f32[192,384]{1,0:T(8,128)}, /...) custom-call(f32[16,256]{1,0:T(8,128)} %get-tuple-element.103.small_r, ...), custom_call_target="tpu_custom_call" | custom-call | tf_op jit(solution)/shard_map/pallas_call | solution.py:2023

commit v5 on v4

--- a/solution.py
+++ b/solution.py
@@ -344,9 +344,9 @@
         aug_ref[token_rows(i), :] = key_pieces(offsets_of(i))
         return carry
 
-    pairs.forward(1)
     lax.fori_loop(0, n, aug_rows, 0)
     moves.start("aug", aug_ref, aug_out)
+    pairs.forward(1)
 
     first, second = group_map[2 * me], group_map[2 * me + 1]
     in_order = first < second
@@ -398,13 +398,17 @@
         lax.fori_loop(0, count, body, 0)
 
     attend_all(3, 0)
-    attend_all(2, 1)
 
     def pair_step(step, count):
         outputs.forward(step)
         pairs.forward(step)
         attend_all(count, step)
 
+    outputs.forward(2)
+    pairs.forward(2)
+    attend_all(2, 1)
+    attend_all(2, 2)
+
     def early_step(step, carry):
         pair_step(step, 2)
         return carry
@@ -413,7 +417,7 @@
         pair_step(step, 4)
         return carry
 
-    lax.fori_loop(2, n // 2, early_step, 0)
+    lax.fori_loop(3, n // 2, early_step, 0)
     pair_step(n // 2, 3)
     lax.fori_loop(n // 2 + 1, n - 1, late_step, 0)
     outputs.last()
@@ -905,11 +909,13 @@
         self.half_b[...] = (mine + self.land_a[0].astype(F32)).astype(BF16)
         self.copy(2).start()
 
+    def mine(self):
+        return self.part(self.chip, self.core)
+
     def third(self):
-        mine = self.part(self.chip, self.core)
         self.copy(1).wait_recv()
         self.copy(2).wait_recv()
-        total = mine + self.land_a[1].astype(F32) + self.land_b[...].astype(F32)
+        total = self.land_a[1].astype(F32) + self.land_b[...].astype(F32)
         for stage in range(3):
             self.copy(stage).wait_send()
         return total
@@ -1029,6 +1035,9 @@
     own = pl.ds(pl.multiple_of(tp * span, span), span)
     layer_ref[...] = mid_ref[:, own]
     moves.start("again", grad_in, x_ref)
+    if attention:
+        moves.wait("gated")
+        moves.start("q", q_in, gated_ref)
     gates.forward(3)
 
     def grow_step(step, carry):
@@ -1148,10 +1157,33 @@
         lax.fori_loop(0, n * pairs, bring, 0)
     layer.first()
     layer.second()
-    for _ in range(2):
+    layer_ref[...] += layer.mine()
+
+    def serve_all():
         backs.advance(1)
         earlies[0].advance(1)
         earlies[1].advance(1)
+
+    serve_all()
+    if attention:
+        downs.sent()
+        moves.wait("q", "term")
+        first, second = group_map[2 * me], group_map[2 * me + 1]
+        in_order = first < second
+        query_groups = (jnp.minimum(first, second), jnp.maximum(first, second))
+
+        def put_query(h, value, extra):
+            here, lane = pl.ds(h // 4 * rows, rows), h % 4 * 2 * LANES
+            down_all[here, lane : lane + LANES] = value
+            down_all[here, lane + LANES : lane + 2 * LANES] = extra
+
+        spread_heads(gated_ref, row_pieces(term_ref[...], True), put_query, heads, in_order)
+        accs[...] = jnp.zeros_like(accs)
+        query_at = lax.broadcasted_iota(jnp.int32, (half, half), 1)
+        key_at = lax.broadcasted_iota(jnp.int32, (half, half), 0)
+        diff_ref[...] = key_at - query_at
+        for i, group in enumerate(query_groups):
+            span_ref[i] = document_start(group * half + query_at, doc_lengths) - key_at
     total.third()
     total.fourth()
 
@@ -1171,52 +1203,31 @@
     moves.wait("again")
     gain_out[...] = lax.fori_loop(0, rows // size, middle_rows, jnp.zeros((8, width), F32))
     if attention:
-        narrow = q_in.shape[1]
-        q_ref = x_ref.at[:, pl.ds(0, narrow)]
-        moves.start("q", q_in, q_ref)
         for i in range(n):
             moves.start(
-                ("aug", i),
-                aug_in.at[pl.ds(i * rows, rows), :],
-                x_ref.at[:, pl.ds(narrow + i * LANES, LANES)],
+                ("aug", i), aug_in.at[pl.ds(i * rows, rows), :], x_ref.at[:, pl.ds(i * LANES, LANES)]
             )
     moves.start("dmid", mid_ref, dmid_out)
     if attention:
         moves.start("dm", branch_ref, dm_out)
+    serve_all()
     da = dot(branch_ref[...], outw_ref[...])
     open_gate = jax.nn.sigmoid(gl_ref[...])
     do_ref[...] = (da * open_gate).astype(BF16)
     dgl_ref[...] = (da * att_ref[...] * open_gate * (1.0 - open_gate)).astype(BF16)
     moves.start("do", do_ref, do_out)
     moves.start("dgl", dgl_ref, dgl_out)
-    backs.advance(1)
-    earlies[0].advance(1)
-    earlies[1].advance(1)
+    serve_all()
     layer_ref[...] += layer.third()
 
     if attention:
-        moves.wait("q", "term", *[("aug", i) for i in range(n)])
-        first, second = group_map[2 * me], group_map[2 * me + 1]
-        in_order = first < second
-        query_groups = (jnp.minimum(first, second), jnp.maximum(first, second))
-
-        def put_in(ref):
-            def put(h, value, extra):
-                ref[:, 2 * h * LANES : (2 * h + 1) * LANES] = value
-                ref[:, (2 * h + 1) * LANES : (2 * h + 2) * LANES] = extra
-
-            return put
-
-        spread_heads(q_ref, row_pieces(term_ref[...], True), put_in(dw_ref), heads, in_order)
+        def put_grad(h, value, extra):
+            branch_ref[:, 2 * h * LANES : (2 * h + 1) * LANES] = value
+            branch_ref[:, (2 * h + 1) * LANES : (2 * h + 2) * LANES] = extra
+
         delta = head_sums(do_ref[...].astype(F32) * att_ref[...], heads)
-        moves.wait("dm")
-        spread_heads(do_ref, row_pieces(-delta, False), put_in(branch_ref), heads, in_order)
-        accs[...] = jnp.zeros_like(accs)
-        query_at = lax.broadcasted_iota(jnp.int32, (half, half), 1)
-        key_at = lax.broadcasted_iota(jnp.int32, (half, half), 0)
-        diff_ref[...] = key_at - query_at
-        for i, group in enumerate(query_groups):
-            span_ref[i] = document_start(group * half + query_at, doc_lengths) - key_at
+        moves.wait("dm", *[("aug", i) for i in range(n)])
+        spread_heads(do_ref, row_pieces(-delta, False), put_grad, heads, in_order)
         dcol_acc = dhid_acc.at[:, pl.ds(0, LANES)]
 
         def stage_copies(it):
@@ -1244,8 +1255,7 @@
 
             key_blocks = ordered(gate_all, pair, lanes)
             value_blocks = ordered(up_all, pair, lanes)
-            aug_lanes = pl.ds(pl.multiple_of(narrow + part * LANES, LANES), LANES)
-            aug_blocks = ordered(x_ref, 0, aug_lanes)
+            aug_blocks = ordered(x_ref, 0, lanes)
             masks = block_masks(diff_ref, span_ref, skip, query_groups, key_groups, half)
             keys = [jnp.concatenate([key_blocks[ki], aug_blocks[ki]], axis=1) for ki in range(2)]
             values = [jnp.concatenate([value_blocks[ki], aug_blocks[ki]], axis=1) for ki in range(2)]
@@ -1254,7 +1264,9 @@
             for e in range(2):
                 h = 2 * pair + e
                 spot = pl.ds(pl.multiple_of(h * 2 * LANES, 2 * LANES), 2 * LANES)
-                query, dout = dw_ref[:, spot], branch_ref[:, spot]
+                quarter = pl.ds(pl.multiple_of(lax.rem(h, 4) * 2 * LANES, 2 * LANES), 2 * LANES)
+                query_rows = pl.ds(pl.multiple_of(lax.div(h, 4) * rows, rows), rows)
+                query, dout = down_all[query_rows, quarter], branch_ref[:, spot]
                 early = contract_cols(keys[0], query)
                 scores = (early[:, :half], early[:, half:], contract_cols(keys[1], query[half:]))
                 early = contract_cols(values[0], dout)
@@ -1268,7 +1280,6 @@
                 probs[1].append(prob[2])
                 grads[0].extend(grad[:2])
                 grads[1].append(grad[2])
-                quarter = pl.ds(pl.multiple_of(lax.rem(h, 4) * 2 * LANES, 2 * LANES), 2 * LANES)
                 accs[lax.div(h, 4), :half, quarter] += contract_rows(grad[0], keys[0])
                 accs[lax.div(h, 4), half:, quarter] += contract_rows(jnp.concatenate(grad[1:], axis=0), both_keys)
             late_queries = jnp.concatenate([query[half:] for query in queries], axis=0)
@@ -1355,7 +1366,8 @@
     earlies[1].end()
     moves.start("gate", gate_ref, gate_out)
     moves.start("up", up_ref, up_out)
-    downs.sent()
+    if not attention:
+        downs.sent()
     moves.wait()
 
 
@@ -1387,7 +1399,7 @@
     kept = [1, 8]
     extra_specs, extra_scratch = [], []
     if attention is not None:
-        assert heads // 2 * rows == n * shard and n * LANES == hidden and heads_width + hidden <= width
+        assert heads // 2 * rows == n * shard and n * LANES == hidden and 2 * rows <= n * shard
         shapes += [
             (wide, BF16),
             (narrow, F32),
@@ -1641,10 +1653,11 @@
     attns.advance(1)
     total.second()
     moves.start("dmid", dmid_ref, du_ref)
+    for _ in range(3):
+        gates.advance(1)
+        attns.advance(1)
+    total.third()
     gates.advance(1)
-    attns.advance(1)
-    gates.advance(1)
-    total.third()
     attns.advance(1)
     total.fourth()
     moves.wait("dmid", 20)

time: 485 us -> 486 us (level)
    pallas_call x1, Pallas kernels: 195 us -> 201 us  [feed_forward(): pl.pallas_call(functools.partial(feed_kernel, n, heads, attention is not...]
where the time goes in v5:
time: 486 us; the launch traced here: 477 us
  Pallas kernels  476 us (98%)
    pallas_call x1, Pallas kernels, feed_forward(): pl.pallas_call(functools.partial(feed_kernel, n, heads, attention is not...  201 us
    pallas_call x1, Pallas kernels, start_forward(): pl.pallas_call(functools.partial(start_kernel, n, heads), out_shape=[jax....  138 us
    pallas_call x1, Pallas kernels, finish_backward(): pl.pallas_call(functools.partial(finish_kernel, n, heads, gate_plan, attn...  130 us

profile of v5, /device:TPU:0, one launch (start us, length us, event | category | flops | bytes accessed | tf_op | source)
XLA Modules:
  0.0 477.4 jit_solution(5740974505698609507)
XLA Ops:
  0.6 137.9 %shard_map.289 = (bf16[1536,384]{1,0:T(8,128)(2,1)}, bf16[1536,384]{1,0:T(8,128)(2,1)}, bf16[1536,384]{1,0:T(8,128)(2,1)}, bf16[1536,384]{1,0:T(8,128)(2,1)}, bf...) custom-call(s32[16]{0:T(128)} %refs_10_.1, ...), custom_call_target="tpu_custom_call" | custom-call | tf_op jit(solution)/shard_map/pallas_call | solution.py:483
  138.5 201.2 %shard_map.290 = (bf16[512,384]{1,0:T(8,128)(2,1)}, f32[512,384]{1,0:T(8,128)}, f32[192,1024]{1,0:T(8,128)}, f32[192,1024]{1,0:T(8,128)}, f32[192,1024]{1,0:T(8,...) custom-call(s32[16]{0:T(128)} %refs_10_.1, ...), custom_call_target="tpu_custom_call" | custom-call | tf_op jit(solution)/shard_map/pallas_call | solution.py:1421
  339.8 130.5 %shard_map.291 = (f32[192,384]{1,0:T(8,128)}, f32[192,384]{1,0:T(8,128)}, f32[192,384]{1,0:T(8,128)}, f32[192,384]{1,0:T(8,128)}, f32[192,384]{1,0:T(8,128)}, /*index=5*/f32[16,256]{1,0:T(8,128)}, f32[512,1536]{1,0:T(8,128)}) custom-call(bf16[8,512,384]{2,1,0:T(8,128)(2,1)} %get-tuple-element.81.refs_0_, bf16[8,512,384]{2,1,0:T(8,128)(2,1)} %get-tuple-element.82.refs_1_, ...), custom_call_target="tpu_custom_call" | custom-call | tf_op jit(solution)/shard_map/pallas_call | solution.py:1711
  470.2 6.7 %shard_map.292 = (f32[512,384]{1,0:T(8,128)}, f32[512,1536]{1,0:T(8,128)}, f32[192,384]{1,0:T(8,128)}, f32[192,384]{1,0:T(8,128)}, f32[192,384]{1,0:T(8,128)}, /...) custom-call(f32[16,256]{1,0:T(8,128)} %get-tuple-element.103.small_r, ...), custom_call_target="tpu_custom_call" | custom-call | tf_op jit(solution)/shard_map/pallas_call | solution.py:2036

commit v6 on v5

--- a/solution.py
+++ b/solution.py
@@ -237,19 +237,17 @@
             lane = h * head_dim + at * count
             target[:, lane : lane + count] = block_small[2 + h : 3 + h, :count]
 
-    size = LANES
+    size = 64
 
     def norm_rows(i, carry):
         here = pl.ds(pl.multiple_of(i * size, size), size)
         normed = (rms_scale(x_vmem[here, :].astype(F32)) * gain_one[...]).astype(BF16)
         for j in range(n):
             u_ref[j, here, :] = normed[:, j * shard : (j + 1) * shard]
-        turned_ref[:, here] = normed.astype(F32).T.astype(BF16)
         return carry
 
     moves.wait("x")
     lax.fori_loop(0, rows // size, norm_rows, 0)
-    moves.start("u", turned_ref, u_out)
 
     def grow(back):
         for side, acc, sources in ((0, acc_r, (wq_ref, wk_ref)), (1, acc_l, (wv_ref, wg_ref))):
@@ -264,6 +262,8 @@
     projections.forward(2)
     grow(1)
     grow(2)
+    projections.forward(3)
+    grow(3)
     forget = jnp.zeros((16, rows), F32)
     for j in range(n):
         forget += contract_cols(small_all[j, :, :shard], u_ref[j])
@@ -289,7 +289,7 @@
         grow(step)
         return carry
 
-    lax.fori_loop(3, n - 2, step_on, 0)
+    lax.fori_loop(4, n - 2, step_on, 0)
     outputs.begin()
     projections.forward(n - 2)
     grow(n - 2)
@@ -408,6 +408,13 @@
     pairs.forward(2)
     attend_all(2, 1)
     attend_all(2, 2)
+
+    def turn_shard(i, carry):
+        turned_ref[shard_rows(i), :] = u_ref[i].astype(F32).T.astype(BF16)
+        return carry
+
+    lax.fori_loop(0, n, turn_shard, 0)
+    moves.start("u", turned_ref, u_out)
 
     def early_step(step, carry):
         pair_step(step, 2)
@@ -1184,6 +1191,7 @@
         diff_ref[...] = key_at - query_at
         for i, group in enumerate(query_groups):
             span_ref[i] = document_start(group * half + query_at, doc_lengths) - key_at
+    serve_all()
     total.third()
     total.fourth()
 
@@ -1210,7 +1218,6 @@
     moves.start("dmid", mid_ref, dmid_out)
     if attention:
         moves.start("dm", branch_ref, dm_out)
-    serve_all()
     da = dot(branch_ref[...], outw_ref[...])
     open_gate = jax.nn.sigmoid(gl_ref[...])
     do_ref[...] = (da * open_gate).astype(BF16)
@@ -1320,7 +1327,7 @@
         starts = [ring.next for ring in turns]
         services = sum(n - 1 - start for start in starts)
         assert starts[0] == starts[1] == starts[2] - 1
-        share = n * pairs // services
+        share = 2 * n * pairs // (3 * services)
 
         def serve(k, carry):
             lax.fori_loop(k * share, (k + 1) * share, attend, 0)

time: 486 us -> 483 us (level)
    pallas_call x1, Pallas kernels: 201 us -> 196 us  [feed_forward(): pl.pallas_call(functools.partial(feed_kernel, n, heads, attention is not...]
where the time goes in v6:
time: 483 us; the launch traced here: 474 us
  Pallas kernels  473 us (98%)
    pallas_call x1, Pallas kernels, feed_forward(): pl.pallas_call(functools.partial(feed_kernel, n, heads, attention is not...  196 us
    pallas_call x1, Pallas kernels, start_forward(): pl.pallas_call(functools.partial(start_kernel, n, heads), out_shape=[jax....  138 us
    pallas_call x1, Pallas kernels, finish_backward(): pl.pallas_call(functools.partial(finish_kernel, n, heads, gate_plan, attn...  132 us

profile of v6, /device:TPU:0, one launch (start us, length us, event | category | flops | bytes accessed | tf_op | source)
XLA Modules:
  0.0 473.9 jit_solution(13664769433686725322)
XLA Ops:
  0.6 137.9 %shard_map.289 = (bf16[1536,384]{1,0:T(8,128)(2,1)}, bf16[1536,384]{1,0:T(8,128)(2,1)}, bf16[1536,384]{1,0:T(8,128)(2,1)}, bf16[1536,384]{1,0:T(8,128)(2,1)}, bf...) custom-call(s32[16]{0:T(128)} %refs_10_.1, ...), custom_call_target="tpu_custom_call" | custom-call | tf_op jit(solution)/shard_map/pallas_call | solution.py:490
  138.5 196.1 %shard_map.290 = (bf16[512,384]{1,0:T(8,128)(2,1)}, f32[512,384]{1,0:T(8,128)}, f32[192,1024]{1,0:T(8,128)}, f32[192,1024]{1,0:T(8,128)}, f32[192,1024]{1,0:T(8,...) custom-call(s32[16]{0:T(128)} %refs_10_.1, ...), custom_call_target="tpu_custom_call" | custom-call | tf_op jit(solution)/shard_map/pallas_call | solution.py:1428
  334.6 132.1 %shard_map.291 = (f32[192,384]{1,0:T(8,128)}, f32[192,384]{1,0:T(8,128)}, f32[192,384]{1,0:T(8,128)}, f32[192,384]{1,0:T(8,128)}, f32[192,384]{1,0:T(8,128)}, /*index=5*/f32[16,256]{1,0:T(8,128)}, f32[512,1536]{1,0:T(8,128)}) custom-call(bf16[8,512,384]{2,1,0:T(8,128)(2,1)} %get-tuple-element.81.refs_0_, bf16[8,512,384]{2,1,0:T(8,128)(2,1)} %get-tuple-element.82.refs_1_, ...), custom_call_target="tpu_custom_call" | custom-call | tf_op jit(solution)/shard_map/pallas_call | solution.py:1718
  466.7 6.7 %shard_map.292 = (f32[512,384]{1,0:T(8,128)}, f32[512,1536]{1,0:T(8,128)}, f32[192,384]{1,0:T(8,128)}, f32[192,384]{1,0:T(8,128)}, f32[192,384]{1,0:T(8,128)}, /...) custom-call(f32[16,256]{1,0:T(8,128)} %get-tuple-element.103.small_r, ...), custom_call_target="tpu_custom_call" | custom-call | tf_op jit(solution)/shard_map/pallas_call | solution.py:2043

commit v7 on v6

--- a/solution.py
+++ b/solution.py
@@ -390,12 +390,12 @@
             acc_ref[h, :half, :] += dot(weights[0], values[0])
             acc_ref[h, half:, :] += dot(jnp.concatenate(weights[1:], axis=1), both_values)
 
-    def attend_all(count, back):
+    def attend_all(count, back, first=0):
         def body(i, carry):
             attend(i, back)
             return carry
 
-        lax.fori_loop(0, count, body, 0)
+        lax.fori_loop(first, count, body, 0)
 
     attend_all(3, 0)
 
@@ -427,9 +427,13 @@
     lax.fori_loop(3, n // 2, early_step, 0)
     pair_step(n // 2, 3)
     lax.fori_loop(n // 2 + 1, n - 1, late_step, 0)
+    for index in range(4):
+        pairs.arrive(index, n - 2)
+    attend_all(2, n - 1)
     outputs.last()
-    pairs.last()
-    attend_all(4, n - 1)
+    for index in (4, 5):
+        pairs.arrive(index, n - 2)
+    attend_all(4, n - 1, 2)
 
     lane = lax.broadcasted_iota(jnp.int32, (rows, LANES), 1)
     low = low_lanes(rows)

time: 483 us -> 481 us (level)
  no operation moved by 1% of the time
where the time goes in v7:
time: 481 us; the launch traced here: 473 us
  Pallas kernels  471 us (98%)
    pallas_call x1, Pallas kernels, feed_forward(): pl.pallas_call(functools.partial(feed_kernel, n, heads, attention is not...  196 us
    pallas_call x1, Pallas kernels, start_forward(): pl.pallas_call(functools.partial(start_kernel, n, heads), out_shape=[jax....  136 us
    pallas_call x1, Pallas kernels, finish_backward(): pl.pallas_call(functools.partial(finish_kernel, n, heads, gate_plan, attn...  132 us

profile of v7, /device:TPU:0, one launch (start us, length us, event | category | flops | bytes accessed | tf_op | source)
XLA Modules:
  0.0 472.5 jit_solution(12288550890854898319)
XLA Ops:
  0.6 136.5 %shard_map.289 = (bf16[1536,384]{1,0:T(8,128)(2,1)}, bf16[1536,384]{1,0:T(8,128)(2,1)}, bf16[1536,384]{1,0:T(8,128)(2,1)}, bf16[1536,384]{1,0:T(8,128)(2,1)}, bf...) custom-call(s32[16]{0:T(128)} %refs_10_.1, ...), custom_call_target="tpu_custom_call" | custom-call | tf_op jit(solution)/shard_map/pallas_call | solution.py:494
  137.1 196.1 %shard_map.290 = (bf16[512,384]{1,0:T(8,128)(2,1)}, f32[512,384]{1,0:T(8,128)}, f32[192,1024]{1,0:T(8,128)}, f32[192,1024]{1,0:T(8,128)}, f32[192,1024]{1,0:T(8,...) custom-call(s32[16]{0:T(128)} %refs_10_.1, ...), custom_call_target="tpu_custom_call" | custom-call | tf_op jit(solution)/shard_map/pallas_call | solution.py:1432
  333.2 132.1 %shard_map.291 = (f32[192,384]{1,0:T(8,128)}, f32[192,384]{1,0:T(8,128)}, f32[192,384]{1,0:T(8,128)}, f32[192,384]{1,0:T(8,128)}, f32[192,384]{1,0:T(8,128)}, /*index=5*/f32[16,256]{1,0:T(8,128)}, f32[512,1536]{1,0:T(8,128)}) custom-call(bf16[8,512,384]{2,1,0:T(8,128)(2,1)} %get-tuple-element.81.refs_0_, bf16[8,512,384]{2,1,0:T(8,128)(2,1)} %get-tuple-element.82.refs_1_, ...), custom_call_target="tpu_custom_call" | custom-call | tf_op jit(solution)/shard_map/pallas_call | solution.py:1722
  465.3 6.7 %shard_map.292 = (f32[512,384]{1,0:T(8,128)}, f32[512,1536]{1,0:T(8,128)}, f32[192,384]{1,0:T(8,128)}, f32[192,384]{1,0:T(8,128)}, f32[192,384]{1,0:T(8,128)}, /...) custom-call(f32[16,256]{1,0:T(8,128)} %get-tuple-element.103.small_r, ...), custom_call_target="tpu_custom_call" | custom-call | tf_op jit(solution)/shard_map/pallas_call | solution.py:2047
